TPU v7x, 128 devices: a whole 4x4x4 slice. The times are simulated.
128 devices in a mesh: row: 8 (over z, y_hi), col: 16 (over x, y_lo, core).
Axes of the slice: x: 4, y: 4 (y_hi: 2, y_lo: 2; y = y_hi * 2 + y_lo), z: 4, core: 2. Of those that a mesh axis runs over, the one named last changes fastest.
Arguments:
- amplitudes: bfloat16 [7168, 2048], P('row', 'col'), may hold values from -24 to 24
- integrals: bfloat16 [2048, 61440], P('row', 'col'), may hold values from -0.125 to 0.125
- occ_energy: float32 [7168], P('row'), may hold values from -4 to -1
- slab_energy: float32 [64], P('col'), may hold values from 0.5 to 3
- virt_energy: float32 [960], replicated, may hold values from 0.5 to 3
Outputs:
- amplitude_step: bfloat16 [7168, 61440], P(('row', 'col'))
All inputs are finite; a program needn't handle non-finite values.
Results may differ from a plain program's by a relative error of at most 0.001.
Values may be sent and summed in bfloat16 or wider, within the bound.
No kernel may reach another device: no remote copies, remote signals or barrier semaphores. Data moves between devices by JAX's collectives and lax.ppermute only.
A program may use at most 128 MiB of HBM per device.

v0:
```python
import jax
import jax.numpy as jnp
from jax import lax
from jax.sharding import PartitionSpec as P


def local(amplitudes, integrals, occ_energy, slab_energy, virt_energy):
    panels = lax.all_gather(amplitudes, "col", axis=1, tiled=True)
    columns = lax.all_gather(integrals, "row", axis=0, tiled=True)
    virtual_pair = (slab_energy[:, None] + virt_energy[None, :]).reshape(-1)
    groups = lax.axis_size("col")
    portion = panels.shape[0] // groups
    residual = jnp.dot(panels, columns, preferred_element_type=jnp.float32)
    denominator = occ_energy[:, None] - virtual_pair[None, :]
    update = (residual / denominator).astype(jnp.bfloat16).reshape(groups, portion, -1)
    arrived = lax.all_to_all(update, "col", split_axis=0, concat_axis=2, tiled=True)
    return arrived.reshape(portion, -1)


def solution(mesh):
    return jax.shard_map(
        local,
        mesh=mesh,
        in_specs=(P("row", "col"), P("row", "col"), P("row"), P("col"), P()),
        out_specs=P(("row", "col"), None),
        check_vma=False,
    )
```

profile of v0, /device:TPU:1, one launch (start us, length us, event | category | flops | bytes accessed | tf_op | source)
XLA Modules:
  0.0 343.1 jit_solution(15877810200572226445)
XLA Ops:
  6.5 0.0 all-gather.3.cloned.1.call-start
  6.5 0.7 all-gather.3.cloned.1.call-update
  7.3 0.0 all-gather.5.cloned.1.call-start
  7.3 0.7 all-gather.5.cloned.1.call-update
  8.0 0.8 broadcast_add_fusion
  8.8 0.1 add.23
  8.9 46.8 %all-gather.3.cloned.1.call-done = bf16[896,2048]{1,0:T(8,128)(2,1)} async-done(((bf16[896,128]{1,0:T(8,128)(2,1)}), bf16[896,2048]{1,0:T(8,128)(2,1)}) %all-gather.3.cloned.1.call-update) | async-done | bytes 3670032 | tf_op jit(solution)/shard_map/all_gather | solution.py:8
  55.6 175.0 %all-gather.5.cloned.1.call-done = bf16[2048,3840]{1,0:T(8,128)(2,1)} async-done(((bf16[256,3840]{1,0:T(8,128)(2,1)}), bf16[2048,3840]{1,0:T(8,128)(2,1)}) %all-gather.5.cloned.1.call-update) | async-done | bytes 15728656 | tf_op jit(solution)/shard_map/all_gather | solution.py:9
  230.6 18.4 %divide_convert_fusion = bf16[896,3840]{1,0:T(8,128)(2,1)S(1)} fusion(bf16[896,2048]{1,0:T(8,128)(2,1)} %all-gather.3.cloned.1.call-done, bf16[2048,3840]{1,0:T(8,128)(2,1)} %all-gather.5.cloned.1.call-done, f32[3840]{0:T(1024)S(1)} %add.23, f32[896]{0:T(1024)} %param.7), kind=kOutput, calls=%fused_computation | convolution fusion | flops 14103183360 | bytes 26298880 | tf_op jit(solution)/shard_map/dot_general | solution.py:13
  249.0 83.9 %all_to_all.15 = bf16[16,56,3840]{2,1,0:T(8,128)(2,1)S(1)} all-to-all(bf16[16,56,3840]{2,1,0:T(8,128)(2,1)S(1)} %bitcast.12), channel_id=1, replica_groups=mesh['row'=8,'col'=16] {'col'}, dimensions={0} | all-to-all | bytes 13762560 | tf_op jit(solution)/shard_map/all_to_all | solution.py:16
  332.9 3.4 copy.7
Async XLA Ops:
  6.5 49.1 %all-gather.3.cloned.1.call-start = ((), (), s32[]{:S(2)}) async-start(), calls=%async_computation.1 | async-start | bytes 3899392 | tf_op jit(solution)/shard_map/all_gather | solution.py:8
  7.3 223.4 %all-gather.5.cloned.1.call-start = ((), (), s32[]{:S(2)}) async-start(), calls=%async_computation.2 | async-start | bytes 17694720 | tf_op jit(solution)/shard_map/all_gather | solution.py:9
Sparse Core Ops, SparseCore 0:
  9.0 46.6 all-gather.2
  57.9 172.6 all-gather.4
where the time goes:
time: 343 us
  waiting for transfers between devices  223 us (65%)
  blocking collectives  83.9 us (24%)
  matrix products  18.4 us (5%)
  between operations  13.4 us (4%)
  local copies, waits for them, and re-layouts  3.45 us (1%)
    all_gather x1, waiting for transfers between devices, local(): columns = lax.all_gather(integrals, 'row', axis=0, tiled=True)  175 us
    all_to_all x1, blocking collectives, local(): lax.all_to_all(update, 'col', split_axis=0, concat_axis=2, tiled=True)  83.9 us
    all_gather x1, waiting for transfers between devices, local(): panels = lax.all_gather(amplitudes, 'col', axis=1, tiled=True)  46.8 us
    dot_general x1, matrix products, local(): residual = jnp.dot(panels, columns, preferred_element_type=jnp.float32)  18.4 us
  transfers between devices with their start and end apart: 2, of which 2 were waited for; matrix products, arithmetic and copies ran while one was open for 0% of the time, Pallas kernels for 0%

commit v1 on v0

v1 whole, which is shorter than its diff:
```python
import functools

import jax
import jax.numpy as jnp
from jax import lax
from jax.experimental import pallas as pl
from jax.experimental.pallas import tpu as pltpu
from jax.sharding import Mesh, PartitionSpec as P

AXES = ("z", "yh", "x", "yl", "c")
SIZES = (4, 2, 4, 2, 2)
Y = ("yh", "yl")
PLANE = ("yh", "x", "yl", "c")
CHUNKS = 3


def shift(value, axis, step, size):
    return lax.ppermute(value, axis, [((i + step) % size, i) for i in range(size)])


def ring(value, axis):
    return jnp.stack([value] + [shift(value, axis, e, 4) for e in (1, 2, 3)])


def product_kernel(p0, q0, p1, q1, own, other, occ_own, occ_other, pair, out):
    yh, x = lax.axis_index("yh"), lax.axis_index("x")
    yl, c = lax.axis_index("yl"), lax.axis_index("c")
    y = yh * 2 + yl
    block, half = pl.program_id(0), pl.program_id(1)
    depth = 128

    def tile(p, q, first_x):
        left, right = [], []
        for d in range(4):
            ex = lax.rem(d - x + 4, 4)
            for f in range(2):
                source = own if f == 0 else other
                low = yh if f == 0 else 1 - yh
                ey = lax.rem(block * 2 + low - y + 4, 4)
                at = (ex, ey) if first_x else (ey, ex)
                left += [p[at], q[at]]
                start = pl.multiple_of(c * depth, depth)
                rest = pl.multiple_of((1 - c) * depth, depth)
                right += [source[d, pl.ds(start, depth), :], source[d, pl.ds(rest, depth), :]]
        a = jnp.concatenate(left, axis=1)
        b = jnp.concatenate(right, axis=0)
        residual = jnp.dot(a, b, preferred_element_type=jnp.float32)
        energy = jnp.where(block == yh, occ_own[half], occ_other[half])
        out[...] = (residual / (energy - pair[...])).astype(out.dtype)

    @pl.when(half == 0)
    def _():
        tile(p0, q0, True)

    @pl.when(half == 1)
    def _():
        tile(p1, q1, False)


def product(panels, own, other, occ_own, occ_other, pair):
    rows = panels[0].shape[2]
    width = own.shape[2]
    whole = pl.BlockSpec(memory_space=pltpu.VMEM)
    return pl.pallas_call(
        product_kernel,
        grid=(2, 2),
        out_shape=jax.ShapeDtypeStruct((4 * rows, width), jnp.bfloat16),
        in_specs=[whole] * 9,
        out_specs=pl.BlockSpec((rows, width), lambda i, h: (i * 2 + h, 0)),
        compiler_params=pltpu.CompilerParams(vmem_limit_bytes=56 << 20),
        cost_estimate=pl.CostEstimate(
            flops=2 * 4 * rows * 2048 * width, bytes_accessed=14 << 20, transcendentals=0
        ),
        name="product",
    )(*panels, own, other, occ_own, occ_other, pair)


def local(amplitudes, integrals, occ_energy, slab_energy, virt_energy):
    yh = lax.axis_index("yh")
    rows = amplitudes.shape[0]
    half = rows // 2
    columns = integrals.shape[1] // 2
    width = columns // CHUNKS

    with jax.named_scope("amplitudes"):
        first = ring(amplitudes[:half], Y)
        second = ring(amplitudes[half:], "x")
        p0 = ring(first, "x")
        p1 = ring(second, Y)
        q0 = shift(p0, "c", 1, 2)
        q1 = shift(p1, "c", 1, 2)
        panels = (p0, q0, p1, q1)
    occ_own = occ_energy.reshape(2, half, 1)
    occ_other = shift(occ_energy, "yh", 1, 2).reshape(2, half, 1)
    pair = (slab_energy[:, None] + virt_energy[None, :]).reshape(2, columns)
    pair = lax.dynamic_index_in_dim(pair, yh, 0, False)

    arrived = []
    for k in range(CHUNKS):
        mine = lax.dynamic_slice(integrals, (0, yh * columns + k * width), (256, width))
        theirs = lax.dynamic_slice(integrals, (0, (1 - yh) * columns + k * width), (256, width))
        own = lax.all_gather(mine, "z", axis=0)
        other = lax.all_gather(shift(theirs, "yh", 1, 2), "z", axis=0)
        part = product(panels, own, other, occ_own, occ_other, pair[None, k * width : (k + 1) * width])
        sent = lax.all_to_all(part.reshape(32, rows // 16, width), PLANE, 0, 0, tiled=True)
        arrived.append(sent.reshape(2, 16, rows // 16, width))
    whole = jnp.stack(arrived)
    return whole.transpose(3, 2, 1, 0, 4).reshape(rows // 16, -1)


def solution(mesh):
    fine = Mesh(mesh.devices.reshape(SIZES), AXES)
    return jax.shard_map(
        local,
        mesh=fine,
        in_specs=(P(("z", "yh"), ("x", "yl", "c")), P(("z", "yh"), ("x", "yl", "c")), P(("z", "yh")), P(("x", "yl", "c")), P()),
        out_specs=P(AXES, None),
        check_vma=False,
    )
```

time: 343 us -> 261 us (0.76)
  waiting for transfers between devices: 223 us -> 75.7 us
  starting transfers between devices: 0.04 us -> 58.4 us
  blocking collectives: 83.9 us -> 38.4 us
  Pallas kernels: 0 us -> 34.6 us
  local copies, waits for them, and re-layouts: 3.45 us -> 34.5 us
  matrix products: 18.4 us -> 0 us
  other arithmetic: 0.76 us -> 4.75 us
    all_gather x2 -> x6, waiting for transfers between devices: 222 us -> 19.7 us  [the longest x3 19.6 us: local(): other = lax.all_gather(shift(theirs, 'yh', 1, 2), 'z', axis=0)]
    ppermute x0 -> x18, waiting for transfers between devices: none -> 53.7 us  [shift(): lax.ppermute(value, axis, [((i + step) % size, i) for i in range(size)])]
    all_to_all x1, blocking collectives: 83.9 us -> 38.4 us  [local(): lax.all_to_all(part.reshape(32, rows // 16, width), PLANE, 0, 0, tiled=True)]
    ppermute x0 -> x18, starting transfers between devices: none -> 45.5 us  [shift(): lax.ppermute(value, axis, [((i + step) % size, i) for i in range(size)])]
    pallas_call x0 -> x3, Pallas kernels: none -> 34.6 us  [product(): pl.pallas_call(product_kernel, grid=(2, 2), out_shape=jax.ShapeDtypeStruc...]
    dot_general x1 -> x0, matrix products: 18.4 us -> none  [local(): residual = jnp.dot(panels, columns, preferred_element_type=jnp.float32)]
    transpose x0 -> x1, local copies, waits for them, and re-layouts: none -> 15.5 us  [local(): return whole.transpose(3, 2, 1, 0, 4).reshape(rows // 16, -1)]
    reshape x0 -> x3, local copies, waits for them, and re-layouts: none -> 13.2 us  [the longest x1 11.1 us: local(): return whole.transpose(3, 2, 1, 0, 4).reshape(rows // 16, -1)]
  transfers between devices with their start and end apart: 2 -> 26, of which waited for: 2 -> 9; matrix products, arithmetic and copies ran while one was open for 0% -> 2% of each run, Pallas kernels for 0% -> 13%
where the time goes in v1:
time: 261 us; the launch traced here: 260 us
  waiting for transfers between devices  75.7 us (29%)
  starting transfers between devices  58.4 us (22%)
  blocking collectives  38.4 us (15%)
  Pallas kernels  34.6 us (13%)
  local copies, waits for them, and re-layouts  34.5 us (13%)
  between operations  13.6 us (5%)
  other arithmetic  4.75 us (2%)
    ppermute x18, waiting for transfers between devices, shift(): lax.ppermute(value, axis, [((i + step) % size, i) for i in range(size)])  53.7 us
    ppermute x18, starting transfers between devices, shift(): lax.ppermute(value, axis, [((i + step) % size, i) for i in range(size)])  45.5 us
    all_to_all x1, blocking collectives, local(): lax.all_to_all(part.reshape(32, rows // 16, width), PLANE, 0, 0, tiled=True)  38.4 us
    pallas_call x3, Pallas kernels, product(): pl.pallas_call(product_kernel, grid=(2, 2), out_shape=jax.ShapeDtypeStruc...  34.6 us
    all_gather x3, waiting for transfers between devices, local(): other = lax.all_gather(shift(theirs, 'yh', 1, 2), 'z', axis=0)  19.6 us
    transpose x1, local copies, waits for them, and re-layouts, local(): return whole.transpose(3, 2, 1, 0, 4).reshape(rows // 16, -1)  15.5 us
    all_to_all x2, starting transfers between devices, local(): lax.all_to_all(part.reshape(32, rows // 16, width), PLANE, 0, 0, tiled=True)  12.7 us
    reshape x1, local copies, waits for them, and re-layouts, local(): return whole.transpose(3, 2, 1, 0, 4).reshape(rows // 16, -1)  11.1 us
  transfers between devices with their start and end apart: 26, of which 9 were waited for; matrix products, arithmetic and copies ran while one was open for 2% of the time, Pallas kernels for 13%

profile of v1, /device:TPU:1, one launch (start us, length us, event | category | flops | bytes accessed | tf_op | source)
XLA Modules:
  0.0 259.9 jit_solution(10827374735861539190)
XLA Ops:
  6.5 2.5 constant_dynamic-slice_fusion.4
  9.1 3.8 %collective-permute-start.14 = (bf16[256,640]{1,0:T(8,128)(2,1)S(1)}, bf16[256,640]{1,0:T(8,128)(2,1)S(1)}, u32[]{:S(2)}, u32[]{:S(2)}) collective-permute-start(bf16[256,640]{1,0:T(8,128)(2,1)S(1)} %get-tuple-element.5), channel_id=1, source_target_pairs={{16,0},{0,16},{17,1},{1,17},{18,2},{2,18},{19,3},{3,19},{20,4},{4,... | collective-permute-start | bytes 983048 | tf_op jit(solution)/shard_map/ppermute | solution.py:18
  13.0 7.2 %collective-permute-done.14 = bf16[256,640]{1,0:T(8,128)(2,1)S(1)} collective-permute-done((bf16[256,640]{1,0:T(8,128)(2,1)S(1)}, bf16[256,640]{1,0:T(8,128)(2,1)S(1)}, u32[]{:S(2)}, u32[]{:S(2)}) %collective-permute-start.14) | collective-permute-done | bytes 327712 | tf_op jit(solution)/shard_map/ppermute | solution.py:18
  21.7 3.0 %collective-permute-start.1 = (bf16[448,128]{1,0:T(8,128)(2,1)S(1)}, bf16[448,128]{1,0:T(8,128)(2,1)S(1)}, u32[]{:S(2)}, u32[]{:S(2)}) collective-permute-start(bf16[448,128]{1,0:T(8,128)(2,1)S(1)} %get-tuple-element.18), channel_id=1, source_target_pairs={{16,0},{18,2},{0,16},{2,18},{17,1},{19,3},{1,17},{3,19},{20,4},{22... | collective-permute-start | bytes 344072 | tf_op jit(solution)/shard_map/amplitudes/ppermute | solution.py:18
  27.0 2.4 collective-permute-done
  29.3 2.6 collective-permute-done.2
  32.0 2.8 %collective-permute-start.4 = (bf16[4,448,128]{2,1,0:T(8,128)(2,1)S(1)}, bf16[4,448,128]{2,1,0:T(8,128)(2,1)S(1)}, u32[]{:S(2)}, u32[]{:S(2)}) collective-permute-start(bf16[4,448,128]{2,1,0:T(8,128)(2,1)S(1)} %get-tuple-element.14), channel_id=1, source_target_pairs={{8,0},{12,4},{0,8},{4,12},{9,1},{13,5},{1,9},{5,13},{10,2},{14,6},... | collective-permute-start | bytes 1376264 | tf_op jit(solution)/shard_map/amplitudes/ppermute | solution.py:18
  35.0 2.5 collective-permute-start.7
  38.3 2.7 %collective-permute-start.3 = (bf16[4,448,128]{2,1,0:T(8,128)(2,1)S(1)}, bf16[4,448,128]{2,1,0:T(8,128)(2,1)S(1)}, u32[]{:S(2)}, u32[]{:S(2)}) collective-permute-start(bf16[4,448,128]{2,1,0:T(8,128)(2,1)S(1)} %get-tuple-element.14), channel_id=1, source_target_pairs={{4,0},{8,4},{12,8},{0,12},{5,1},{9,5},{13,9},{1,13},{6,2},{10,6},{... | collective-permute-start | bytes 1376264 | tf_op jit(solution)/shard_map/amplitudes/ppermute | solution.py:18
  41.1 1.2 collective-permute-done.8
  42.2 1.2 collective-permute-start.5
  43.6 4.1 %collective-permute-start.11 = (bf16[4,448,128]{2,1,0:T(8,128)(2,1)S(1)}, bf16[4,448,128]{2,1,0:T(8,128)(2,1)S(1)}, u32[]{:S(2)}, u32[]{:S(2)}) collective-permute-start(bf16[4,448,128]{2,1,0:T(8,128)(2,1)S(1)} %get-tuple-element.12), channel_id=1, source_target_pairs={{16,0},{18,2},{0,16},{2,18},{17,1},{19,3},{1,17},{3,19},{20,4},{22... | collective-permute-start | bytes 1376264 | tf_op jit(solution)/shard_map/amplitudes/ppermute | solution.py:18
  47.6 3.4 %collective-permute-start.10 = (bf16[4,448,128]{2,1,0:T(8,128)(2,1)S(1)}, bf16[4,448,128]{2,1,0:T(8,128)(2,1)S(1)}, u32[]{:S(2)}, u32[]{:S(2)}) collective-permute-start(bf16[4,448,128]{2,1,0:T(8,128)(2,1)S(1)} %get-tuple-element.12), channel_id=1, source_target_pairs={{2,0},{16,2},{18,16},{0,18},{3,1},{17,3},{19,17},{1,19},{6,4},{20,... | collective-permute-start | bytes 1376264 | tf_op jit(solution)/shard_map/amplitudes/ppermute | solution.py:18
  51.1 4.8 %collective-permute-done.3 = bf16[4,448,128]{2,1,0:T(8,128)(2,1)S(1)} collective-permute-done((bf16[4,448,128]{2,1,0:T(8,128)(2,1)S(1)}, bf16[4,448,128]{2,1,0:T(8,128)(2,1)S(1)}, u32[]{:S(2)}, u32[]{:S(2)}) %collective-permute-start.3) | collective-permute-done | bytes 458784 | tf_op jit(solution)/shard_map/amplitudes/ppermute | solution.py:18
  55.9 1.2 collective-permute-done.5
  57.3 8.0 %collective-permute-start.6 = (bf16[4,4,448,128]{3,2,1,0:T(8,128)(2,1)S(1)}, bf16[4,4,448,128]{3,2,1,0:T(8,128)(2,1)}, u32[]{:S(2)}, u32[]{:S(2)}) collective-permute-start(bf16[4,4,448,128]{3,2,1,0:T(8,128)(2,1)S(1)} %pad_maximum_fusion.p0), channel_id=1, source_target_pairs={{1,0},{0,1},{3,2},{2,3},{5,4},{4,5},{7,6},{6,7},{9,8},{8,9},{11,10... | collective-permute-start | bytes 5505032 | tf_op jit(solution)/shard_map/amplitudes/ppermute | solution.py:18
  65.3 1.5 pad_maximum_fusion.1.p1
  66.8 6.5 %collective-permute-start.13 = (bf16[4,4,448,128]{3,2,1,0:T(8,128)(2,1)}, bf16[4,4,448,128]{3,2,1,0:T(8,128)(2,1)}, u32[]{:S(2)}, u32[]{:S(2)}) collective-permute-start(bf16[4,4,448,128]{3,2,1,0:T(8,128)(2,1)} %pad_maximum_fusion.1.p1), channel_id=1, source_target_pairs={{1,0},{0,1},{3,2},{2,3},{5,4},{4,5},{7,6},{6,7},{9,8},{8,9},{11,10... | collective-permute-start | bytes 5505032 | tf_op jit(solution)/shard_map/amplitudes/ppermute | solution.py:18
  73.3 1.9 collective-permute-start.15
  78.4 11.5 %product.3 = bf16[1792,640]{1,0:T(8,128)(2,1)} custom-call(bf16[4,4,448,128]{3,2,1,0:T(8,128)(2,1)} %copy-done, bf16[4,4,448,128]{3,2,1,0:T(8,128)(2,1)} %collective-permute-done.6.q0, bf16[4,4,448,128]{3,2,1,0:T(8,128)(2,1)} %pad_maximum_fusion.1.p1, bf16[4,4,448,128]{3,2,1,0:T(8,128)(2,1)} %collective-permute-done.13.q1, bf16[4,256,640]{2,1,0:T(8,128)(2,1)} %bitcast.52, ...), custom_call_target="tpu_custom_call" | custom-call | flops 4697620480 | bytes 14680064 | tf_op jit(solution)/shard_map/product/pallas_call | solution.py:64
  89.9 7.2 %all-to-all-start = ((bf16[32,56,640]{2,1,0:T(8,128)(2,1)}), bf16[32,56,640]{2,1,0:T(8,128)(2,1)S(1)}, u32[]{:S(2)}, u32[]{:S(2)}) async-start(bf16[32,56,640]{2,1,0:T(8,128)(2,1)} %bitcast.36), calls=%async_computation | async-start | bytes 4587520 | tf_op jit(solution)/shard_map/all_to_all | solution.py:105
  97.2 3.2 %collective-permute-start.17 = (bf16[256,640]{1,0:T(8,128)(2,1)S(1)}, bf16[256,640]{1,0:T(8,128)(2,1)S(1)}, u32[]{:S(2)}, u32[]{:S(2)}) collective-permute-start(bf16[256,640]{1,0:T(8,128)(2,1)S(1)} %get-tuple-element.9), channel_id=1, source_target_pairs={{16,0},{0,16},{17,1},{1,17},{18,2},{2,18},{19,3},{3,19},{20,4},{4,... | collective-permute-start | bytes 983048 | tf_op jit(solution)/shard_map/ppermute | solution.py:18
  100.3 34.3 %collective-permute-done.17 = bf16[256,640]{1,0:T(8,128)(2,1)S(1)} collective-permute-done((bf16[256,640]{1,0:T(8,128)(2,1)S(1)}, bf16[256,640]{1,0:T(8,128)(2,1)S(1)}, u32[]{:S(2)}, u32[]{:S(2)}) %collective-permute-start.17) | collective-permute-done | bytes 327712 | tf_op jit(solution)/shard_map/ppermute | solution.py:18
  135.5 11.6 %product.4 = bf16[1792,640]{1,0:T(8,128)(2,1)} custom-call(bf16[4,4,448,128]{3,2,1,0:T(8,128)(2,1)} %copy-done, bf16[4,4,448,128]{3,2,1,0:T(8,128)(2,1)} %collective-permute-done.6.q0, bf16[4,4,448,128]{3,2,1,0:T(8,128)(2,1)} %pad_maximum_fusion.1.p1, bf16[4,4,448,128]{3,2,1,0:T(8,128)(2,1)} %collective-permute-done.13.q1, bf16[4,256,640]{2,1,0:T(8,128)(2,1)} %bitcast.51, ...), custom_call_target="tpu_custom_call" | custom-call | flops 4697620480 | bytes 14680064 | tf_op jit(solution)/shard_map/product/pallas_call | solution.py:64
  147.1 5.5 %all-to-all-start.1 = ((bf16[32,56,640]{2,1,0:T(8,128)(2,1)}), bf16[32,56,640]{2,1,0:T(8,128)(2,1)}, u32[]{:S(2)}, u32[]{:S(2)}) async-start(bf16[32,56,640]{2,1,0:T(8,128)(2,1)} %bitcast.37), calls=%async_computation.1 | async-start | bytes 4587520 | tf_op jit(solution)/shard_map/all_to_all | solution.py:105
  152.6 19.6 %all-gather.23.cloned.1.call-done = bf16[1024,640]{1,0:T(8,128)(2,1)} async-done(((bf16[256,640]{1,0:T(8,128)(2,1)}), bf16[1024,640]{1,0:T(8,128)(2,1)}) %all-gather.23.cloned.1.call-update) | async-done | bytes 1310736 | tf_op jit(solution)/shard_map/all_gather | solution.py:103
  172.3 11.4 %product.5 = bf16[1792,640]{1,0:T(8,128)(2,1)} custom-call(bf16[4,4,448,128]{3,2,1,0:T(8,128)(2,1)} %copy-done, bf16[4,4,448,128]{3,2,1,0:T(8,128)(2,1)} %collective-permute-done.6.q0, bf16[4,4,448,128]{3,2,1,0:T(8,128)(2,1)} %pad_maximum_fusion.1.p1, bf16[4,4,448,128]{3,2,1,0:T(8,128)(2,1)} %collective-permute-done.13.q1, bf16[4,256,640]{2,1,0:T(8,128)(2,1)} %bitcast.55, ...), custom_call_target="tpu_custom_call" | custom-call | flops 4697620480 | bytes 14680064 | tf_op jit(solution)/shard_map/product/pallas_call | solution.py:64
  183.7 1.5 all-to-all-done.1
  185.2 38.4 %all_to_all.15 = bf16[32,56,640]{2,1,0:T(8,128)(2,1)S(1)} all-to-all(bf16[32,56,640]{2,1,0:T(8,128)(2,1)} %bitcast.38), channel_id=1, replica_groups=mesh['z'=4,'yh'=2,'x'=4,'yl'=2,'c'=2] {'yh','x','yl','c'}, dimensions={0} | all-to-all | bytes 4587520 | tf_op jit(solution)/shard_map/all_to_all | solution.py:105
  223.6 2.9 %maximum_bitcast_fusion = bf16[56,16,2,3,640]{4,0,1,2,3:T(8,128)(2,1)S(1)} fusion(bf16[1,2,16,56,640]{4,3,2,1,0:T(8,128)(2,1)S(1)} %bitcast.35, bf16[1,2,16,56,640]{4,3,2,1,0:T(8,128)(2,1)} %bitcast.23, bf16[1,2,16,56,640]{4,3,2,1,0:T(8,128)(2,1)S(1)} %bitcast.34), kind=kLoop, calls=%fused_computation | loop fusion | flops 6881280 | bytes 13762560 | tf_op jit(solution)/shard_map/transpose | solution.py:108
  226.5 15.5 %copy.21 = bf16[56,16,2,3,640]{4,3,2,1,0:T(4,128)(2,1)} copy(bf16[56,16,2,3,640]{4,0,1,2,3:T(8,128)(2,1)S(1)} %maximum_bitcast_fusion) | data formatting | bytes 13762560 | tf_op jit(solution)/shard_map/transpose | solution.py:108
  242.0 11.1 %reshape.36 = bf16[56,61440]{1,0:T(8,128)(2,1)} reshape(bf16[56,16,2,3,640]{4,3,2,1,0:T(4,128)(2,1)} %copy.21) | data formatting | bytes 13762560 | tf_op jit(solution)/shard_map/reshape | solution.py:108
  (64 shorter events, 9.3 us)
Async XLA Ops:
  6.5 71.8 %all-gather.13.cloned.1.call-start = ((), (), s32[]{:S(2)}) async-start(), calls=%async_computation.3 | async-start | bytes 1638400 | tf_op jit(solution)/shard_map/all_gather | solution.py:102
  6.5 15.1 %copy-start.4 = (bf16[896,128]{1,0:T(8,128)(2,1)S(1)}, bf16[896,128]{1,0:T(8,128)(2,1)}, u32[]{:S(2)}) copy-start(bf16[896,128]{1,0:T(8,128)(2,1)} %param.5) | copy-start | bytes 688132
  9.1 69.3 %all-gather.15.cloned.1.call-start = ((), (), s32[]{:S(2)}) async-start(), calls=%async_computation.4 | async-start | bytes 1638400 | tf_op jit(solution)/shard_map/all_gather | solution.py:103
  9.1 11.0 %collective-permute-start.14 = (bf16[256,640]{1,0:T(8,128)(2,1)S(1)}, bf16[256,640]{1,0:T(8,128)(2,1)S(1)}, u32[]{:S(2)}, u32[]{:S(2)}) collective-permute-start(bf16[256,640]{1,0:T(8,128)(2,1)S(1)} %get-tuple-element.5), channel_id=1, source_target_pairs={{16,0},{0,16},{17,1},{1,17},{18,2},{2,18},{19,3},{3,19},{20,4},{4,... | collective-permute-start | bytes 983048 | tf_op jit(solution)/shard_map/ppermute | solution.py:18
  20.9 114.5 %all-gather.17.cloned.1.call-start = ((), (), s32[]{:S(2)}) async-start(), calls=%async_computation.5 | async-start | bytes 1638400 | tf_op jit(solution)/shard_map/all_gather | solution.py:102
  21.6 113.8 %all-gather.19.cloned.1.call-start = ((), (), s32[]{:S(2)}) async-start(), calls=%async_computation.6 | async-start | bytes 1638400 | tf_op jit(solution)/shard_map/all_gather | solution.py:103
  21.7 5.2 %collective-permute-start.1 = (bf16[448,128]{1,0:T(8,128)(2,1)S(1)}, bf16[448,128]{1,0:T(8,128)(2,1)S(1)}, u32[]{:S(2)}, u32[]{:S(2)}) collective-permute-start(bf16[448,128]{1,0:T(8,128)(2,1)S(1)} %get-tuple-element.18), channel_id=1, source_target_pairs={{16,0},{18,2},{0,16},{2,18},{17,1},{19,3},{1,17},{3,19},{20,4},{22... | collective-permute-start | bytes 344072 | tf_op jit(solution)/shard_map/amplitudes/ppermute | solution.py:18
  24.7 4.6 %collective-permute-start = (bf16[448,128]{1,0:T(8,128)(2,1)S(1)}, bf16[448,128]{1,0:T(8,128)(2,1)S(1)}, u32[]{:S(2)}, u32[]{:S(2)}) collective-permute-start(bf16[448,128]{1,0:T(8,128)(2,1)S(1)} %get-tuple-element.18), channel_id=1, source_target_pairs={{2,0},{16,2},{18,16},{0,18},{3,1},{17,3},{19,17},{1,19},{6,4},{20,... | collective-permute-start | bytes 344072 | tf_op jit(solution)/shard_map/amplitudes/ppermute | solution.py:18
  25.5 6.4 %collective-permute-start.2 = (bf16[448,128]{1,0:T(8,128)(2,1)S(1)}, bf16[448,128]{1,0:T(8,128)(2,1)S(1)}, u32[]{:S(2)}, u32[]{:S(2)}) collective-permute-start(bf16[448,128]{1,0:T(8,128)(2,1)S(1)} %get-tuple-element.18), channel_id=1, source_target_pairs={{18,0},{0,2},{2,16},{16,18},{19,1},{1,3},{3,17},{17,19},{22,4},{4,... | collective-permute-start | bytes 344072 | tf_op jit(solution)/shard_map/amplitudes/ppermute | solution.py:18
  26.2 11.3 %collective-permute-start.16 = (bf16[256,640]{1,0:T(8,128)(2,1)S(1)}, bf16[256,640]{1,0:T(8,128)(2,1)S(1)}, u32[]{:S(2)}, u32[]{:S(2)}) collective-permute-start(bf16[256,640]{1,0:T(8,128)(2,1)S(1)} %get-tuple-element.6), channel_id=1, source_target_pairs={{16,0},{0,16},{17,1},{1,17},{18,2},{2,18},{19,3},{3,19},{20,4},{4,... | collective-permute-start | bytes 983048 | tf_op jit(solution)/shard_map/ppermute | solution.py:18
  32.0 19.1 %collective-permute-start.4 = (bf16[4,448,128]{2,1,0:T(8,128)(2,1)S(1)}, bf16[4,448,128]{2,1,0:T(8,128)(2,1)S(1)}, u32[]{:S(2)}, u32[]{:S(2)}) collective-permute-start(bf16[4,448,128]{2,1,0:T(8,128)(2,1)S(1)} %get-tuple-element.14), channel_id=1, source_target_pairs={{8,0},{12,4},{0,8},{4,12},{9,1},{13,5},{1,9},{5,13},{10,2},{14,6},... | collective-permute-start | bytes 1376264 | tf_op jit(solution)/shard_map/amplitudes/ppermute | solution.py:18
  34.8 7.4 %collective-permute-start.8 = (bf16[448,128]{1,0:T(8,128)(2,1)S(1)}, bf16[448,128]{1,0:T(8,128)(2,1)S(1)}, u32[]{:S(2)}, u32[]{:S(2)}) collective-permute-start(bf16[448,128]{1,0:T(8,128)(2,1)S(1)} %get-tuple-element.17), channel_id=1, source_target_pairs={{8,0},{12,4},{0,8},{4,12},{9,1},{13,5},{1,9},{5,13},{10,2},{14,6},... | collective-permute-start | bytes 344072 | tf_op jit(solution)/shard_map/amplitudes/ppermute | solution.py:18
  35.0 8.5 %collective-permute-start.7 = (bf16[448,128]{1,0:T(8,128)(2,1)S(1)}, bf16[448,128]{1,0:T(8,128)(2,1)S(1)}, u32[]{:S(2)}, u32[]{:S(2)}) collective-permute-start(bf16[448,128]{1,0:T(8,128)(2,1)S(1)} %get-tuple-element.17), channel_id=1, source_target_pairs={{4,0},{8,4},{12,8},{0,12},{5,1},{9,5},{13,9},{1,13},{6,2},{10,6},{... | collective-permute-start | bytes 344072 | tf_op jit(solution)/shard_map/amplitudes/ppermute | solution.py:18
  37.5 6.0 %collective-permute-start.9 = (bf16[448,128]{1,0:T(8,128)(2,1)S(1)}, bf16[448,128]{1,0:T(8,128)(2,1)S(1)}, u32[]{:S(2)}, u32[]{:S(2)}) collective-permute-start(bf16[448,128]{1,0:T(8,128)(2,1)S(1)} %get-tuple-element.17), channel_id=1, source_target_pairs={{12,0},{0,4},{4,8},{8,12},{13,1},{1,5},{5,9},{9,13},{14,2},{2,6},{... | collective-permute-start | bytes 344072 | tf_op jit(solution)/shard_map/amplitudes/ppermute | solution.py:18
  37.5 0.7 copy-start.2
  38.3 114.4 %all-gather.21.cloned.1.call-start = ((), (), s32[]{:S(2)}) async-start(), calls=%async_computation.7 | async-start | bytes 1638400 | tf_op jit(solution)/shard_map/all_gather | solution.py:102
  38.3 17.6 %collective-permute-start.3 = (bf16[4,448,128]{2,1,0:T(8,128)(2,1)S(1)}, bf16[4,448,128]{2,1,0:T(8,128)(2,1)S(1)}, u32[]{:S(2)}, u32[]{:S(2)}) collective-permute-start(bf16[4,448,128]{2,1,0:T(8,128)(2,1)S(1)} %get-tuple-element.14), channel_id=1, source_target_pairs={{4,0},{8,4},{12,8},{0,12},{5,1},{9,5},{13,9},{1,13},{6,2},{10,6},{... | collective-permute-start | bytes 1376264 | tf_op jit(solution)/shard_map/amplitudes/ppermute | solution.py:18
  42.2 14.9 %collective-permute-start.5 = (bf16[4,448,128]{2,1,0:T(8,128)(2,1)S(1)}, bf16[4,448,128]{2,1,0:T(8,128)(2,1)S(1)}, u32[]{:S(2)}, u32[]{:S(2)}) collective-permute-start(bf16[4,448,128]{2,1,0:T(8,128)(2,1)S(1)} %get-tuple-element.14), channel_id=1, source_target_pairs={{12,0},{0,4},{4,8},{8,12},{13,1},{1,5},{5,9},{9,13},{14,2},{2,6},{... | collective-permute-start | bytes 1376264 | tf_op jit(solution)/shard_map/amplitudes/ppermute | solution.py:18
  43.6 21.7 %collective-permute-start.11 = (bf16[4,448,128]{2,1,0:T(8,128)(2,1)S(1)}, bf16[4,448,128]{2,1,0:T(8,128)(2,1)S(1)}, u32[]{:S(2)}, u32[]{:S(2)}) collective-permute-start(bf16[4,448,128]{2,1,0:T(8,128)(2,1)S(1)} %get-tuple-element.12), channel_id=1, source_target_pairs={{16,0},{18,2},{0,16},{2,18},{17,1},{19,3},{1,17},{3,19},{20,4},{22... | collective-permute-start | bytes 1376264 | tf_op jit(solution)/shard_map/amplitudes/ppermute | solution.py:18
  47.6 17.7 %collective-permute-start.10 = (bf16[4,448,128]{2,1,0:T(8,128)(2,1)S(1)}, bf16[4,448,128]{2,1,0:T(8,128)(2,1)S(1)}, u32[]{:S(2)}, u32[]{:S(2)}) collective-permute-start(bf16[4,448,128]{2,1,0:T(8,128)(2,1)S(1)} %get-tuple-element.12), channel_id=1, source_target_pairs={{2,0},{16,2},{18,16},{0,18},{3,1},{17,3},{19,17},{1,19},{6,4},{20,... | collective-permute-start | bytes 1376264 | tf_op jit(solution)/shard_map/amplitudes/ppermute | solution.py:18
  51.1 14.2 %collective-permute-start.12 = (bf16[4,448,128]{2,1,0:T(8,128)(2,1)S(1)}, bf16[4,448,128]{2,1,0:T(8,128)(2,1)S(1)}, u32[]{:S(2)}, u32[]{:S(2)}) collective-permute-start(bf16[4,448,128]{2,1,0:T(8,128)(2,1)S(1)} %get-tuple-element.12), channel_id=1, source_target_pairs={{18,0},{0,2},{2,16},{16,18},{19,1},{1,3},{3,17},{17,19},{22,4},{4,... | collective-permute-start | bytes 1376264 | tf_op jit(solution)/shard_map/amplitudes/ppermute | solution.py:18
  57.3 9.5 %copy-start = (bf16[4,4,448,128]{3,2,1,0:T(8,128)(2,1)}, bf16[4,4,448,128]{3,2,1,0:T(8,128)(2,1)S(1)}, u32[]{:S(2)}) copy-start(bf16[4,4,448,128]{3,2,1,0:T(8,128)(2,1)S(1)} %pad_maximum_fusion.p0) | copy-start | bytes 5505028
  57.3 21.1 %collective-permute-start.6 = (bf16[4,4,448,128]{3,2,1,0:T(8,128)(2,1)S(1)}, bf16[4,4,448,128]{3,2,1,0:T(8,128)(2,1)}, u32[]{:S(2)}, u32[]{:S(2)}) collective-permute-start(bf16[4,4,448,128]{3,2,1,0:T(8,128)(2,1)S(1)} %pad_maximum_fusion.p0), channel_id=1, source_target_pairs={{1,0},{0,1},{3,2},{2,3},{5,4},{4,5},{7,6},{6,7},{9,8},{8,9},{11,10... | collective-permute-start | bytes 5505032 | tf_op jit(solution)/shard_map/amplitudes/ppermute | solution.py:18
  65.3 8.0 %copy-start.5 = (f32[896]{0:T(1024)S(1)}, f32[896]{0:T(1024)}, u32[]{:S(2)}) copy-start(f32[896]{0:T(1024)} %param.7) | copy-start | bytes 10756
  65.3 9.9 %copy-start.7 = (f32[4]{0:T(128)S(1)}, f32[4]{0:T(128)}, u32[]{:S(2)}) copy-start(f32[4]{0:T(128)} %param.8) | copy-start | bytes 52
  65.3 10.0 %copy-start.6 = (f32[960]{0:T(1024)S(1)}, f32[960]{0:T(1024)}, u32[]{:S(2)}) copy-start(f32[960]{0:T(1024)} %param.9) | copy-start | bytes 11524
  66.8 11.6 %collective-permute-start.13 = (bf16[4,4,448,128]{3,2,1,0:T(8,128)(2,1)}, bf16[4,4,448,128]{3,2,1,0:T(8,128)(2,1)}, u32[]{:S(2)}, u32[]{:S(2)}) collective-permute-start(bf16[4,4,448,128]{3,2,1,0:T(8,128)(2,1)} %pad_maximum_fusion.1.p1), channel_id=1, source_target_pairs={{1,0},{0,1},{3,2},{2,3},{5,4},{4,5},{7,6},{6,7},{9,8},{8,9},{11,10... | collective-permute-start | bytes 5505032 | tf_op jit(solution)/shard_map/amplitudes/ppermute | solution.py:18
  73.3 4.0 %collective-permute-start.15 = (f32[896]{0:T(1024)S(1)}, f32[896]{0:T(1024)S(1)}, u32[]{:S(2)}, u32[]{:S(2)}) collective-permute-start(f32[896]{0:T(1024)S(1)} %copy-done.5), channel_id=1, source_target_pairs={{16,0},{0,16},{17,1},{1,17},{18,2},{2,18},{19,3},{3,19},{20,4},{4,... | collective-permute-start | bytes 10760 | tf_op jit(solution)/shard_map/ppermute | solution.py:18
  89.9 57.2 %all-to-all-start = ((bf16[32,56,640]{2,1,0:T(8,128)(2,1)}), bf16[32,56,640]{2,1,0:T(8,128)(2,1)S(1)}, u32[]{:S(2)}, u32[]{:S(2)}) async-start(bf16[32,56,640]{2,1,0:T(8,128)(2,1)} %bitcast.36), calls=%async_computation | async-start | bytes 4587520 | tf_op jit(solution)/shard_map/all_to_all | solution.py:105
  97.1 75.1 %all-gather.23.cloned.1.call-start = ((), (), s32[]{:S(2)}) async-start(), calls=%async_computation.8 | async-start | bytes 1638400 | tf_op jit(solution)/shard_map/all_gather | solution.py:103
  97.2 37.5 %collective-permute-start.17 = (bf16[256,640]{1,0:T(8,128)(2,1)S(1)}, bf16[256,640]{1,0:T(8,128)(2,1)S(1)}, u32[]{:S(2)}, u32[]{:S(2)}) collective-permute-start(bf16[256,640]{1,0:T(8,128)(2,1)S(1)} %get-tuple-element.9), channel_id=1, source_target_pairs={{16,0},{0,16},{17,1},{1,17},{18,2},{2,18},{19,3},{3,19},{20,4},{4,... | collective-permute-start | bytes 983048 | tf_op jit(solution)/shard_map/ppermute | solution.py:18
  147.1 38.1 %all-to-all-start.1 = ((bf16[32,56,640]{2,1,0:T(8,128)(2,1)}), bf16[32,56,640]{2,1,0:T(8,128)(2,1)}, u32[]{:S(2)}, u32[]{:S(2)}) async-start(bf16[32,56,640]{2,1,0:T(8,128)(2,1)} %bitcast.37), calls=%async_computation.1 | async-start | bytes 4587520 | tf_op jit(solution)/shard_map/all_to_all | solution.py:105
  (2 other events, 1.4 us)
Sparse Core Ops, SparseCore 0:
  9.2 27.1 all-gather.12
  38.1 25.5 all-gather.14
  65.3 25.5 all-gather.16
  92.4 25.5 all-gather.18
  119.5 25.5 all-gather.20
  146.6 25.6 all-gather.22

commit v2 on v0

v2 whole, which is shorter than its diff:
```python
import jax
import jax.numpy as jnp
from jax import lax
from jax.experimental import pallas as pl
from jax.experimental.pallas import tpu as pltpu
from jax.sharding import Mesh, PartitionSpec as P

AXES = ("z", "yh", "x", "yl", "c")
SIZES = (4, 2, 4, 2, 2)
Y = ("yh", "yl")
PLANE = ("yh", "x", "yl", "c")
WIDTHS = (768, 1152)
DEPTH = 128
ANY = pl.BlockSpec(memory_space=pl.ANY)
VMEM = pl.BlockSpec(memory_space=pltpu.VMEM)


def shift(value, axis, step, size):
    return lax.ppermute(value, axis, [((i + step) % size, i) for i in range(size)])


def ring(value, axis):
    return jnp.stack([value] + [shift(value, axis, e, 4) for e in (1, 2, 3)])


def product_kernel(p0, q0, p1, q1, *refs):
    integrals, (energy, pair, out, panel, block, result, loads, fetches, stores) = refs[:8], refs[8:]
    z, yh, x, yl = (lax.axis_index(a) for a in ("z", "yh", "x", "yl"))
    y = yh * 2 + yl
    rows = p0.shape[2]

    def fetch(d, f):
        slot = pl.multiple_of(lax.rem(z + d, 4) * 512 + f * 256, 256)
        return pltpu.make_async_copy(integrals[d * 2 + f], block.at[pl.ds(slot, 256)], fetches.at[d * 2 + f])

    def load(tile, ex, f, other):
        b, h = tile // 2, tile % 2
        low = yh if f == 0 else 1 - yh
        ey = lax.rem(b * 2 + low - y + 4, 4)
        source = ((p0, q0), (p1, q1))[h][other]
        source = source.at[ex, ey] if h == 0 else source.at[ey, ex]
        slot = pl.multiple_of(lax.rem(x + ex, 4) * 512 + f * 256 + other * DEPTH, DEPTH)
        index = ex * 4 + f * 2 + other
        return pltpu.make_async_copy(source, panel.at[pl.ds(tile * rows, rows), pl.ds(slot, DEPTH)], loads.at[tile, index])

    def store(tile):
        return pltpu.make_async_copy(result.at[tile % 2], out.at[pl.ds(tile * rows, rows)], stores.at[tile % 2])

    pieces = [(ex, f, other) for ex in range(4) for f in range(2) for other in range(2)]
    for d in range(4):
        for f in range(2):
            fetch(d, f).start()
    for tile in range(4):
        for piece in pieces:
            load(tile, *piece).start()
    for d in range(4):
        for f in range(2):
            fetch(d, f).wait()
    for tile in range(4):
        for piece in pieces:
            load(tile, *piece).wait()
        if tile >= 2:
            store(tile - 2).wait()
        residual = jnp.dot(panel[tile * rows : (tile + 1) * rows], block[...], preferred_element_type=jnp.float32)
        denominator = energy[tile * rows : (tile + 1) * rows] - pair[...]
        inverse = pl.reciprocal(denominator, approx=True)
        inverse = inverse * (2.0 - denominator * inverse)
        result[tile % 2] = (residual * inverse).astype(out.dtype)
        store(tile).start()
    store(2).wait()
    store(3).wait()


def product(panels, integrals, energy, pair):
    rows = panels[0].shape[2]
    width = pair.shape[1]
    return pl.pallas_call(
        product_kernel,
        out_shape=jax.ShapeDtypeStruct((4 * rows, width), jnp.bfloat16),
        in_specs=[ANY] * 12 + [VMEM] * 2,
        out_specs=ANY,
        scratch_shapes=[
            pltpu.VMEM((4 * rows, 2048), jnp.bfloat16),
            pltpu.VMEM((2048, width), jnp.bfloat16),
            pltpu.VMEM((2, rows, width), jnp.bfloat16),
            pltpu.SemaphoreType.DMA((4, 16)),
            pltpu.SemaphoreType.DMA((8,)),
            pltpu.SemaphoreType.DMA((2,)),
        ],
        compiler_params=pltpu.CompilerParams(vmem_limit_bytes=40 << 20),
        cost_estimate=pl.CostEstimate(
            flops=2 * 4 * rows * 2048 * width, bytes_accessed=14 << 20, transcendentals=0
        ),
        name="product",
    )(*panels, *integrals, energy, pair)


def place_kernel(offset, columns, piece, *refs):
    out, sems = refs[-2:]
    width = piece.shape[3]

    def copy(h, s):
        at = s * 2 * columns + h * columns + offset
        return pltpu.make_async_copy(piece.at[h, s], out.at[:, pl.ds(at, width)], sems.at[h, s])

    for s in range(16):
        for h in range(2):
            copy(h, s).start()
    for s in range(16):
        for h in range(2):
            copy(h, s).wait()


def place(piece, offset, columns, whole):
    rows = piece.shape[2]
    operands = [piece] if whole is None else [piece, whole]
    return pl.pallas_call(
        lambda *refs: place_kernel(offset, columns, *refs),
        out_shape=jax.ShapeDtypeStruct((rows, 32 * columns), jnp.bfloat16),
        in_specs=[ANY] * len(operands),
        out_specs=ANY,
        scratch_shapes=[pltpu.SemaphoreType.DMA((2, 16))],
        input_output_aliases={} if whole is None else {1: 0},
        cost_estimate=pl.CostEstimate(flops=0, bytes_accessed=4 * piece.size, transcendentals=0),
        name="place",
    )(*operands)


def local(amplitudes, integrals, occ_energy, slab_energy, virt_energy):
    yh, c = lax.axis_index("yh"), lax.axis_index("c")
    rows = amplitudes.shape[0]
    half = rows // 2
    columns = integrals.shape[1] // 2

    with jax.named_scope("amplitudes"):
        first = ring(amplitudes[:half], Y)
        second = ring(amplitudes[half:], "x")
        p0 = ring(first, "x")
        p1 = ring(second, Y)
        q0 = shift(p0, "c", 1, 2)
        q1 = shift(p1, "c", 1, 2)
        panels = (p0, q0, p1, q1)
    energies = jnp.stack([occ_energy, shift(occ_energy, "yh", 1, 2)])
    energy = jnp.concatenate([energies[yh], energies[1 - yh]]).reshape(2 * rows, 1)
    pair = (slab_energy[:, None] + virt_energy[None, :]).reshape(2, columns)
    pair = lax.dynamic_index_in_dim(pair, yh, 0, True)

    def part(h, offset, width):
        at = h * columns + offset
        return jnp.concatenate(
            [lax.dynamic_slice(integrals, (o * DEPTH, at), (DEPTH, width)) for o in (c, 1 - c)]
        )

    whole, offset = None, 0
    for width in WIDTHS:
        own = part(yh, offset, width)
        other = shift(part(1 - yh, offset, width), "yh", 1, 2)
        pieces = [own, other]
        for d in (1, 2, 3):
            pieces += [shift(own, "z", d, 4), shift(other, "z", d, 4)]
        update = product(panels, pieces, energy, pair[:, offset : offset + width])
        sent = lax.all_to_all(update.reshape(32, rows // 16, width), PLANE, 0, 0, tiled=True)
        whole = place(sent.reshape(2, 16, rows // 16, width), offset, columns, whole)
        offset += width
    return whole


def solution(mesh):
    fine = Mesh(mesh.devices.reshape(SIZES), AXES)
    split = P(("z", "yh"), ("x", "yl", "c"))
    return jax.shard_map(
        local,
        mesh=fine,
        in_specs=(split, split, P(("z", "yh")), P(("x", "yl", "c")), P()),
        out_specs=P(AXES, None),
        check_vma=False,
    )
```

time: 343 us -> 438 us (1.28)
  Pallas kernels: 0 us -> 239 us
  waiting for transfers between devices: 223 us -> 127 us
  blocking collectives: 83.9 us -> 0 us
  starting transfers between devices: 0.04 us -> 60.3 us
  matrix products: 18.4 us -> 0 us
  between operations: 13.4 us -> 0.39 us
    pallas_call x0 -> x4, Pallas kernels: none -> 239 us  [the longest x2 211 us: place(): pl.pallas_call(lambda *refs: place_kernel(offset, columns, *refs), out_sh...]
    all_gather x2 -> x0, waiting for transfers between devices: 222 us -> none  [the longest x1 175 us: local(): columns = lax.all_gather(integrals, 'row', axis=0, tiled=True)]
    ppermute x0 -> x29, waiting for transfers between devices: none -> 127 us  [shift(): lax.ppermute(value, axis, [((i + step) % size, i) for i in range(size)])]
    all_to_all x1 -> x0, blocking collectives: 83.9 us -> none  [local(): lax.all_to_all(update, 'col', split_axis=0, concat_axis=2, tiled=True)]
    ppermute x0 -> x29, starting transfers between devices: none -> 49.8 us  [shift(): lax.ppermute(value, axis, [((i + step) % size, i) for i in range(size)])]
    dot_general x1 -> x0, matrix products: 18.4 us -> none  [local(): residual = jnp.dot(panels, columns, preferred_element_type=jnp.float32)]
    all_to_all x0 -> x2, starting transfers between devices: none -> 10.5 us  [local(): lax.all_to_all(update.reshape(32, rows // 16, width), PLANE, 0, 0, tiled=...]
  transfers between devices with their start and end apart: 2 -> 31, of which waited for: 2 -> 17; matrix products, arithmetic and copies ran while one was open for 0% -> 1% of each run, Pallas kernels for 0% -> 23%
where the time goes in v2:
time: 438 us; the launch traced here: 437 us
  Pallas kernels  239 us (55%)
  waiting for transfers between devices  127 us (29%)
  starting transfers between devices  60.3 us (14%)
  local copies, waits for them, and re-layouts  7.76 us (2%)
    pallas_call x2, Pallas kernels, place(): pl.pallas_call(lambda *refs: place_kernel(offset, columns, *refs), out_sh...  211 us
    ppermute x29, waiting for transfers between devices, shift(): lax.ppermute(value, axis, [((i + step) % size, i) for i in range(size)])  127 us
    ppermute x29, starting transfers between devices, shift(): lax.ppermute(value, axis, [((i + step) % size, i) for i in range(size)])  49.8 us
    pallas_call x2, Pallas kernels, product(): pl.pallas_call(product_kernel, out_shape=jax.ShapeDtypeStruct((4 * rows,...  28.2 us
    all_to_all x2, starting transfers between devices, local(): lax.all_to_all(update.reshape(32, rows // 16, width), PLANE, 0, 0, tiled=...  10.5 us
  transfers between devices with their start and end apart: 31, of which 17 were waited for; matrix products, arithmetic and copies ran while one was open for 1% of the time, Pallas kernels for 23%

profile of v2, /device:TPU:1, one launch (start us, length us, event | category | flops | bytes accessed | tf_op | source)
XLA Modules:
  0.0 437.1 jit_solution(11576594071123385471)
XLA Ops:
  1.0 2.2 collective-permute-start.2
  3.2 2.6 collective-permute-start.1
  7.4 3.5 collective-permute-done.1
  17.2 7.9 %collective-permute-done.9 = bf16[448,128]{1,0:T(8,128)(2,1)S(1)} collective-permute-done((bf16[448,128]{1,0:T(8,128)(2,1)S(1)}, bf16[448,128]{1,0:T(8,128)(2,1)S(1)}, u32[]{:S(2)}, u32[]{:S(2)}) %collective-permute-start.9) | collective-permute-done | bytes 114720 | tf_op jit(solution)/shard_map/amplitudes/ppermute | solution.py:19
  26.4 1.9 collective-permute-done.8
  28.8 2.7 collective-permute-start.11
  31.9 6.5 %collective-permute-done.4 = bf16[4,448,128]{2,1,0:T(8,128)(2,1)S(1)} collective-permute-done((bf16[4,448,128]{2,1,0:T(8,128)(2,1)S(1)}, bf16[4,448,128]{2,1,0:T(8,128)(2,1)S(1)}, u32[]{:S(2)}, u32[]{:S(2)}) %collective-permute-start.4) | collective-permute-done | bytes 458784 | tf_op jit(solution)/shard_map/amplitudes/ppermute | solution.py:19
  39.0 3.0 collective-permute-start.6
  42.0 4.8 %collective-permute-done.11 = bf16[4,448,128]{2,1,0:T(8,128)(2,1)S(1)} collective-permute-done((bf16[4,448,128]{2,1,0:T(8,128)(2,1)S(1)}, bf16[4,448,128]{2,1,0:T(8,128)(2,1)S(1)}, u32[]{:S(2)}, u32[]{:S(2)}) %collective-permute-start.11) | collective-permute-done | bytes 458784 | tf_op jit(solution)/shard_map/amplitudes/ppermute | solution.py:19
  46.8 3.1 collective-permute-done.10
  51.4 3.1 collective-permute-start.13
  58.9 3.8 collective-permute-start.23
  62.7 5.5 %collective-permute-done.21 = f32[896]{0:T(1024)S(1)} collective-permute-done((f32[896]{0:T(1024)S(1)}, f32[896]{0:T(1024)S(1)}, u32[]{:S(2)}, u32[]{:S(2)}) %collective-permute-start.21) | collective-permute-done | bytes 3616 | tf_op jit(solution)/shard_map/ppermute | solution.py:19
  68.2 3.6 collective-permute-start.25
  73.6 1.9 collective-permute-start.24
  75.6 4.9 %collective-permute-done.25.refs_4_ = bf16[256,768]{1,0:T(8,128)(2,1)S(1)} collective-permute-done((bf16[256,768]{1,0:T(8,128)(2,1)S(1)}, bf16[256,768]{1,0:T(8,128)(2,1)S(1)}, u32[]{:S(2)}, u32[]{:S(2)}) %collective-permute-start.25) | collective-permute-done | bytes 393248 | tf_op jit(solution)/shard_map/ppermute | solution.py:19
  81.2 2.7 collective-permute-start.26
  83.9 6.8 %collective-permute-done.27.refs_6_ = bf16[256,768]{1,0:T(8,128)(2,1)} collective-permute-done((bf16[256,768]{1,0:T(8,128)(2,1)S(1)}, bf16[256,768]{1,0:T(8,128)(2,1)}, u32[]{:S(2)}, u32[]{:S(2)}) %collective-permute-start.27) | collective-permute-done | bytes 393248 | tf_op jit(solution)/shard_map/ppermute | solution.py:19
  91.2 6.3 %collective-permute-done.26.refs_5_ = bf16[256,768]{1,0:T(8,128)(2,1)} collective-permute-done((bf16[256,768]{1,0:T(8,128)(2,1)S(1)}, bf16[256,768]{1,0:T(8,128)(2,1)}, u32[]{:S(2)}, u32[]{:S(2)}) %collective-permute-start.26) | collective-permute-done | bytes 393248 | tf_op jit(solution)/shard_map/ppermute | solution.py:19
  97.5 9.3 %collective-permute-done.28.refs_7_ = bf16[256,768]{1,0:T(8,128)(2,1)} collective-permute-done((bf16[256,768]{1,0:T(8,128)(2,1)S(1)}, bf16[256,768]{1,0:T(8,128)(2,1)}, u32[]{:S(2)}, u32[]{:S(2)}) %collective-permute-start.28) | collective-permute-done | bytes 393248 | tf_op jit(solution)/shard_map/ppermute | solution.py:19
  108.8 12.2 %product.3 = bf16[1792,768]{1,0:T(8,128)(2,1)} custom-call(bf16[4,4,448,128]{3,2,1,0:T(8,128)(2,1)S(1)} %pad_maximum_fusion.p0, bf16[4,4,448,128]{3,2,1,0:T(8,128)(2,1)} %collective-permute-done.6.q0, bf16[4,4,448,128]{3,2,1,0:T(8,128)(2,1)} %pad_maximum_fusion.1.p1, bf16[4,4,448,128]{3,2,1,0:T(8,128)(2,1)} %collective-permute-done.13.q1, ...), custom_call_target="tpu_custom_call" | custom-call | flops 5637144576 | bytes 14680064 | tf_op jit(solution)/shard_map/product/pallas_call | solution.py:77
  120.9 4.9 %all-to-all-start.1 = ((bf16[32,56,768]{2,1,0:T(8,128)(2,1)}), bf16[32,56,768]{2,1,0:T(8,128)(2,1)}, u32[]{:S(2)}, u32[]{:S(2)}) async-start(bf16[32,56,768]{2,1,0:T(8,128)(2,1)} %bitcast.18), calls=%async_computation.1 | async-start | bytes 5505024 | tf_op jit(solution)/shard_map/all_to_all | solution.py:162
  127.3 3.1 collective-permute-start.14
  130.8 3.0 collective-permute-start.17
  134.3 40.1 %collective-permute-done.14.refs_1_ = bf16[256,1152]{1,0:T(8,128)(2,1)S(1)} collective-permute-done((bf16[256,1152]{1,0:T(8,128)(2,1)S(1)}, bf16[256,1152]{1,0:T(8,128)(2,1)S(1)}, u32[]{:S(2)}, u32[]{:S(2)}) %collective-permute-start.14) | collective-permute-done | bytes 589856 | tf_op jit(solution)/shard_map/ppermute | solution.py:19
  174.7 3.0 collective-permute-start.18
  178.2 10.2 %collective-permute-done.16.refs_3_ = bf16[256,1152]{1,0:T(8,128)(2,1)S(1)} collective-permute-done((bf16[256,1152]{1,0:T(8,128)(2,1)S(1)}, bf16[256,1152]{1,0:T(8,128)(2,1)S(1)}, u32[]{:S(2)}, u32[]{:S(2)}) %collective-permute-start.16) | collective-permute-done | bytes 589856 | tf_op jit(solution)/shard_map/ppermute | solution.py:19
  189.9 14.2 %collective-permute-done.20.refs_7_ = bf16[256,1152]{1,0:T(8,128)(2,1)S(1)} collective-permute-done((bf16[256,1152]{1,0:T(8,128)(2,1)S(1)}, bf16[256,1152]{1,0:T(8,128)(2,1)S(1)}, u32[]{:S(2)}, u32[]{:S(2)}) %collective-permute-start.20) | collective-permute-done | bytes 589856 | tf_op jit(solution)/shard_map/ppermute | solution.py:19
  204.1 16.0 %product.2 = bf16[1792,1152]{1,0:T(8,128)(2,1)} custom-call(bf16[4,4,448,128]{3,2,1,0:T(8,128)(2,1)S(1)} %pad_maximum_fusion.p0, bf16[4,4,448,128]{3,2,1,0:T(8,128)(2,1)} %collective-permute-done.6.q0, bf16[4,4,448,128]{3,2,1,0:T(8,128)(2,1)} %pad_maximum_fusion.1.p1, bf16[4,4,448,128]{3,2,1,0:T(8,128)(2,1)} %collective-permute-done.13.q1, ...), custom_call_target="tpu_custom_call" | custom-call | flops 8455716864 | bytes 14680064 | tf_op jit(solution)/shard_map/product/pallas_call | solution.py:77
  220.1 5.6 %all-to-all-start = ((bf16[32,56,1152]{2,1,0:T(8,128)(2,1)}), bf16[32,56,1152]{2,1,0:T(8,128)(2,1)}, u32[]{:S(2)}, u32[]{:S(2)}) async-start(bf16[32,56,1152]{2,1,0:T(8,128)(2,1)} %bitcast.24), calls=%async_computation | async-start | bytes 8257536 | tf_op jit(solution)/shard_map/all_to_all | solution.py:162
  225.7 84.8 %place.2.refs_1_ = bf16[56,61440]{1,0:T(8,128)(2,1)} custom-call(bf16[2,16,56,768]{3,2,1,0:T(8,128)(2,1)} %bitcast.19.refs_0_), custom_call_target="tpu_custom_call" | custom-call | bytes 5505024 | tf_op jit(solution)/shard_map/place/pallas_call | solution.py:117
  310.5 126.5 %place.3 = bf16[56,61440]{1,0:T(8,128)(2,1)} custom-call(bf16[2,16,56,1152]{3,2,1,0:T(8,128)(2,1)} %bitcast.17.refs_0_, bf16[56,61440]{1,0:T(8,128)(2,1)} %place.2.refs_1_), custom_call_target="tpu_custom_call", output_to_operand_aliasing={{}: (1, {})} | custom-call | bytes 8257536 | tf_op jit(solution)/shard_map/place/pallas_call | solution.py:117
  (72 shorter events, 27.2 us)
Async XLA Ops:
  1.0 6.4 %collective-permute-start.2 = (bf16[448,128]{1,0:T(8,128)(2,1)S(1)}, bf16[448,128]{1,0:T(8,128)(2,1)S(1)}, u32[]{:S(2)}, u32[]{:S(2)}) collective-permute-start(bf16[448,128]{1,0:T(8,128)(2,1)S(1)} %get-tuple-element.22), channel_id=1, source_target_pairs={{18,0},{0,2},{2,16},{16,18},{19,1},{1,3},{3,17},{17,19},{22,4},{4,... | collective-permute-start | bytes 344072 | tf_op jit(solution)/shard_map/amplitudes/ppermute | solution.py:19
  3.2 7.6 %collective-permute-start.1 = (bf16[448,128]{1,0:T(8,128)(2,1)S(1)}, bf16[448,128]{1,0:T(8,128)(2,1)S(1)}, u32[]{:S(2)}, u32[]{:S(2)}) collective-permute-start(bf16[448,128]{1,0:T(8,128)(2,1)S(1)} %get-tuple-element.22), channel_id=1, source_target_pairs={{16,0},{18,2},{0,16},{2,18},{17,1},{19,3},{1,17},{3,19},{20,4},{22... | collective-permute-start | bytes 344072 | tf_op jit(solution)/shard_map/amplitudes/ppermute | solution.py:19
  5.8 5.0 %collective-permute-start = (bf16[448,128]{1,0:T(8,128)(2,1)S(1)}, bf16[448,128]{1,0:T(8,128)(2,1)S(1)}, u32[]{:S(2)}, u32[]{:S(2)}) collective-permute-start(bf16[448,128]{1,0:T(8,128)(2,1)S(1)} %get-tuple-element.22), channel_id=1, source_target_pairs={{2,0},{16,2},{18,16},{0,18},{3,1},{17,3},{19,17},{1,19},{6,4},{20,... | collective-permute-start | bytes 344072 | tf_op jit(solution)/shard_map/amplitudes/ppermute | solution.py:19
  10.9 20.6 %collective-permute-start.5 = (bf16[4,448,128]{2,1,0:T(8,128)(2,1)S(1)}, bf16[4,448,128]{2,1,0:T(8,128)(2,1)S(1)}, u32[]{:S(2)}, u32[]{:S(2)}) collective-permute-start(bf16[4,448,128]{2,1,0:T(8,128)(2,1)S(1)} %get-tuple-element.18), channel_id=1, source_target_pairs={{12,0},{0,4},{4,8},{8,12},{13,1},{1,5},{5,9},{9,13},{14,2},{2,6},{... | collective-permute-start | bytes 1376264 | tf_op jit(solution)/shard_map/amplitudes/ppermute | solution.py:19
  12.2 12.9 %collective-permute-start.9 = (bf16[448,128]{1,0:T(8,128)(2,1)S(1)}, bf16[448,128]{1,0:T(8,128)(2,1)S(1)}, u32[]{:S(2)}, u32[]{:S(2)}) collective-permute-start(bf16[448,128]{1,0:T(8,128)(2,1)S(1)} %get-tuple-element.21), channel_id=1, source_target_pairs={{12,0},{0,4},{4,8},{8,12},{13,1},{1,5},{5,9},{9,13},{14,2},{2,6},{... | collective-permute-start | bytes 344072 | tf_op jit(solution)/shard_map/amplitudes/ppermute | solution.py:19
  13.4 14.9 %collective-permute-start.8 = (bf16[448,128]{1,0:T(8,128)(2,1)S(1)}, bf16[448,128]{1,0:T(8,128)(2,1)S(1)}, u32[]{:S(2)}, u32[]{:S(2)}) collective-permute-start(bf16[448,128]{1,0:T(8,128)(2,1)S(1)} %get-tuple-element.21), channel_id=1, source_target_pairs={{8,0},{12,4},{0,8},{4,12},{9,1},{13,5},{1,9},{5,13},{10,2},{14,6},... | collective-permute-start | bytes 344072 | tf_op jit(solution)/shard_map/amplitudes/ppermute | solution.py:19
  14.9 13.4 %collective-permute-start.7 = (bf16[448,128]{1,0:T(8,128)(2,1)S(1)}, bf16[448,128]{1,0:T(8,128)(2,1)S(1)}, u32[]{:S(2)}, u32[]{:S(2)}) collective-permute-start(bf16[448,128]{1,0:T(8,128)(2,1)S(1)} %get-tuple-element.21), channel_id=1, source_target_pairs={{4,0},{8,4},{12,8},{0,12},{5,1},{9,5},{13,9},{1,13},{6,2},{10,6},{... | collective-permute-start | bytes 344072 | tf_op jit(solution)/shard_map/amplitudes/ppermute | solution.py:19
  16.7 21.7 %collective-permute-start.4 = (bf16[4,448,128]{2,1,0:T(8,128)(2,1)S(1)}, bf16[4,448,128]{2,1,0:T(8,128)(2,1)S(1)}, u32[]{:S(2)}, u32[]{:S(2)}) collective-permute-start(bf16[4,448,128]{2,1,0:T(8,128)(2,1)S(1)} %get-tuple-element.18), channel_id=1, source_target_pairs={{8,0},{12,4},{0,8},{4,12},{9,1},{13,5},{1,9},{5,13},{10,2},{14,6},... | collective-permute-start | bytes 1376264 | tf_op jit(solution)/shard_map/amplitudes/ppermute | solution.py:19
  25.1 13.6 %collective-permute-start.3 = (bf16[4,448,128]{2,1,0:T(8,128)(2,1)S(1)}, bf16[4,448,128]{2,1,0:T(8,128)(2,1)S(1)}, u32[]{:S(2)}, u32[]{:S(2)}) collective-permute-start(bf16[4,448,128]{2,1,0:T(8,128)(2,1)S(1)} %get-tuple-element.18), channel_id=1, source_target_pairs={{4,0},{8,4},{12,8},{0,12},{5,1},{9,5},{13,9},{1,13},{6,2},{10,6},{... | collective-permute-start | bytes 1376264 | tf_op jit(solution)/shard_map/amplitudes/ppermute | solution.py:19
  28.4 13.7 %collective-permute-start.12 = (bf16[4,448,128]{2,1,0:T(8,128)(2,1)S(1)}, bf16[4,448,128]{2,1,0:T(8,128)(2,1)S(1)}, u32[]{:S(2)}, u32[]{:S(2)}) collective-permute-start(bf16[4,448,128]{2,1,0:T(8,128)(2,1)S(1)} %get-tuple-element.16), channel_id=1, source_target_pairs={{18,0},{0,2},{2,16},{16,18},{19,1},{1,3},{3,17},{17,19},{22,4},{4,... | collective-permute-start | bytes 1376264 | tf_op jit(solution)/shard_map/amplitudes/ppermute | solution.py:19
  28.8 18.0 %collective-permute-start.11 = (bf16[4,448,128]{2,1,0:T(8,128)(2,1)S(1)}, bf16[4,448,128]{2,1,0:T(8,128)(2,1)S(1)}, u32[]{:S(2)}, u32[]{:S(2)}) collective-permute-start(bf16[4,448,128]{2,1,0:T(8,128)(2,1)S(1)} %get-tuple-element.16), channel_id=1, source_target_pairs={{16,0},{18,2},{0,16},{2,18},{17,1},{19,3},{1,17},{3,19},{20,4},{22... | collective-permute-start | bytes 1376264 | tf_op jit(solution)/shard_map/amplitudes/ppermute | solution.py:19
  31.6 18.4 %collective-permute-start.10 = (bf16[4,448,128]{2,1,0:T(8,128)(2,1)S(1)}, bf16[4,448,128]{2,1,0:T(8,128)(2,1)S(1)}, u32[]{:S(2)}, u32[]{:S(2)}) collective-permute-start(bf16[4,448,128]{2,1,0:T(8,128)(2,1)S(1)} %get-tuple-element.16), channel_id=1, source_target_pairs={{2,0},{16,2},{18,16},{0,18},{3,1},{17,3},{19,17},{1,19},{6,4},{20,... | collective-permute-start | bytes 1376264 | tf_op jit(solution)/shard_map/amplitudes/ppermute | solution.py:19
  39.0 67.8 %collective-permute-start.6 = (bf16[4,4,448,128]{3,2,1,0:T(8,128)(2,1)S(1)}, bf16[4,4,448,128]{3,2,1,0:T(8,128)(2,1)}, u32[]{:S(2)}, u32[]{:S(2)}) collective-permute-start(bf16[4,4,448,128]{3,2,1,0:T(8,128)(2,1)S(1)} %pad_maximum_fusion.p0), channel_id=1, source_target_pairs={{1,0},{0,1},{3,2},{2,3},{5,4},{4,5},{7,6},{6,7},{9,8},{8,9},{11,10... | collective-permute-start | bytes 5505032 | tf_op jit(solution)/shard_map/amplitudes/ppermute | solution.py:19
  51.4 21.3 %copy-start.4 = (f32[960]{0:T(1024)S(1)}, f32[960]{0:T(1024)}, u32[]{:S(2)}) copy-start(f32[960]{0:T(1024)} %param.9) | copy-start | bytes 11524
  51.4 55.4 %collective-permute-start.13 = (bf16[4,4,448,128]{3,2,1,0:T(8,128)(2,1)}, bf16[4,4,448,128]{3,2,1,0:T(8,128)(2,1)}, u32[]{:S(2)}, u32[]{:S(2)}) collective-permute-start(bf16[4,4,448,128]{3,2,1,0:T(8,128)(2,1)} %pad_maximum_fusion.1.p1), channel_id=1, source_target_pairs={{1,0},{0,1},{3,2},{2,3},{5,4},{4,5},{7,6},{6,7},{9,8},{8,9},{11,10... | collective-permute-start | bytes 5505032 | tf_op jit(solution)/shard_map/amplitudes/ppermute | solution.py:19
  55.8 16.0 %collective-permute-start.22 = (bf16[256,768]{1,0:T(8,128)(2,1)S(1)}, bf16[256,768]{1,0:T(8,128)(2,1)S(1)}, u32[]{:S(2)}, u32[]{:S(2)}) collective-permute-start(bf16[256,768]{1,0:T(8,128)(2,1)S(1)} %pad_maximum_fusion.7), channel_id=1, source_target_pairs={{16,0},{0,16},{17,1},{1,17},{18,2},{2,18},{19,3},{3,19},{20,4},{4,... | collective-permute-start | bytes 1179656 | tf_op jit(solution)/shard_map/ppermute | solution.py:19
  57.3 10.9 %collective-permute-start.21 = (f32[896]{0:T(1024)S(1)}, f32[896]{0:T(1024)S(1)}, u32[]{:S(2)}, u32[]{:S(2)}) collective-permute-start(f32[896]{0:T(1024)S(1)} %copy-done.5), channel_id=1, source_target_pairs={{16,0},{0,16},{17,1},{1,17},{18,2},{2,18},{19,3},{3,19},{20,4},{4,... | collective-permute-start | bytes 10760 | tf_op jit(solution)/shard_map/ppermute | solution.py:19
  58.9 14.0 %collective-permute-start.23 = (bf16[256,768]{1,0:T(8,128)(2,1)S(1)}, bf16[256,768]{1,0:T(8,128)(2,1)S(1)}, u32[]{:S(2)}, u32[]{:S(2)}) collective-permute-start(bf16[256,768]{1,0:T(8,128)(2,1)S(1)} %pad_maximum_fusion.6.refs_0_), channel_id=1, source_target_pairs={{32,0},{64,32},{96,64},{0,96},{33,1},{65,33},{97,65},{1,97},{34,2}... | collective-permute-start | bytes 1179656 | tf_op jit(solution)/shard_map/ppermute | solution.py:19
  68.2 12.3 %collective-permute-start.25 = (bf16[256,768]{1,0:T(8,128)(2,1)S(1)}, bf16[256,768]{1,0:T(8,128)(2,1)S(1)}, u32[]{:S(2)}, u32[]{:S(2)}) collective-permute-start(bf16[256,768]{1,0:T(8,128)(2,1)S(1)} %pad_maximum_fusion.6.refs_0_), channel_id=1, source_target_pairs={{64,0},{96,32},{0,64},{32,96},{65,1},{97,33},{1,65},{33,97},{66,2}... | collective-permute-start | bytes 1179656 | tf_op jit(solution)/shard_map/ppermute | solution.py:19
  71.8 19.0 %collective-permute-start.27 = (bf16[256,768]{1,0:T(8,128)(2,1)S(1)}, bf16[256,768]{1,0:T(8,128)(2,1)}, u32[]{:S(2)}, u32[]{:S(2)}) collective-permute-start(bf16[256,768]{1,0:T(8,128)(2,1)S(1)} %pad_maximum_fusion.6.refs_0_), channel_id=1, source_target_pairs={{96,0},{0,32},{32,64},{64,96},{97,1},{1,33},{33,65},{65,97},{98,2}... | collective-permute-start | bytes 1179656 | tf_op jit(solution)/shard_map/ppermute | solution.py:19
  73.6 17.5 %collective-permute-start.24 = (bf16[256,768]{1,0:T(8,128)(2,1)S(1)}, bf16[256,768]{1,0:T(8,128)(2,1)}, u32[]{:S(2)}, u32[]{:S(2)}) collective-permute-start(bf16[256,768]{1,0:T(8,128)(2,1)S(1)} %collective-permute-done.22.refs_1_), channel_id=1, source_target_pairs={{32,0},{64,32},{96,64},{0,96},{33,1},{65,33},{97,65},{1,97},{34,2}... | collective-permute-start | bytes 1179656 | tf_op jit(solution)/shard_map/ppermute | solution.py:19
  81.2 16.3 %collective-permute-start.26 = (bf16[256,768]{1,0:T(8,128)(2,1)S(1)}, bf16[256,768]{1,0:T(8,128)(2,1)}, u32[]{:S(2)}, u32[]{:S(2)}) collective-permute-start(bf16[256,768]{1,0:T(8,128)(2,1)S(1)} %collective-permute-done.22.refs_1_), channel_id=1, source_target_pairs={{64,0},{96,32},{0,64},{32,96},{65,1},{97,33},{1,65},{33,97},{66,2}... | collective-permute-start | bytes 1179656 | tf_op jit(solution)/shard_map/ppermute | solution.py:19
  90.7 16.0 %collective-permute-start.28 = (bf16[256,768]{1,0:T(8,128)(2,1)S(1)}, bf16[256,768]{1,0:T(8,128)(2,1)}, u32[]{:S(2)}, u32[]{:S(2)}) collective-permute-start(bf16[256,768]{1,0:T(8,128)(2,1)S(1)} %collective-permute-done.22.refs_1_), channel_id=1, source_target_pairs={{96,0},{0,32},{32,64},{64,96},{97,1},{1,33},{33,65},{65,97},{98,2}... | collective-permute-start | bytes 1179656 | tf_op jit(solution)/shard_map/ppermute | solution.py:19
  120.9 99.2 %all-to-all-start.1 = ((bf16[32,56,768]{2,1,0:T(8,128)(2,1)}), bf16[32,56,768]{2,1,0:T(8,128)(2,1)}, u32[]{:S(2)}, u32[]{:S(2)}) async-start(bf16[32,56,768]{2,1,0:T(8,128)(2,1)} %bitcast.18), calls=%async_computation.1 | async-start | bytes 5505024 | tf_op jit(solution)/shard_map/all_to_all | solution.py:162
  127.3 47.1 %collective-permute-start.14 = (bf16[256,1152]{1,0:T(8,128)(2,1)S(1)}, bf16[256,1152]{1,0:T(8,128)(2,1)S(1)}, u32[]{:S(2)}, u32[]{:S(2)}) collective-permute-start(bf16[256,1152]{1,0:T(8,128)(2,1)S(1)} %pad_maximum_fusion.3), channel_id=1, source_target_pairs={{16,0},{0,16},{17,1},{1,17},{18,2},{2,18},{19,3},{3,19},{20,4},{4,... | collective-permute-start | bytes 1769480 | tf_op jit(solution)/shard_map/ppermute | solution.py:19
  130.4 47.3 %collective-permute-start.15 = (bf16[256,1152]{1,0:T(8,128)(2,1)S(1)}, bf16[256,1152]{1,0:T(8,128)(2,1)S(1)}, u32[]{:S(2)}, u32[]{:S(2)}) collective-permute-start(bf16[256,1152]{1,0:T(8,128)(2,1)S(1)} %pad_maximum_fusion.2.refs_0_), channel_id=1, source_target_pairs={{32,0},{64,32},{96,64},{0,96},{33,1},{65,33},{97,65},{1,97},{34,2}... | collective-permute-start | bytes 1769480 | tf_op jit(solution)/shard_map/ppermute | solution.py:19
  130.8 47.4 %collective-permute-start.17 = (bf16[256,1152]{1,0:T(8,128)(2,1)S(1)}, bf16[256,1152]{1,0:T(8,128)(2,1)S(1)}, u32[]{:S(2)}, u32[]{:S(2)}) collective-permute-start(bf16[256,1152]{1,0:T(8,128)(2,1)S(1)} %pad_maximum_fusion.2.refs_0_), channel_id=1, source_target_pairs={{64,0},{96,32},{0,64},{32,96},{65,1},{97,33},{1,65},{33,97},{66,2}... | collective-permute-start | bytes 1769480 | tf_op jit(solution)/shard_map/ppermute | solution.py:19
  133.7 44.5 %collective-permute-start.19 = (bf16[256,1152]{1,0:T(8,128)(2,1)S(1)}, bf16[256,1152]{1,0:T(8,128)(2,1)S(1)}, u32[]{:S(2)}, u32[]{:S(2)}) collective-permute-start(bf16[256,1152]{1,0:T(8,128)(2,1)S(1)} %pad_maximum_fusion.2.refs_0_), channel_id=1, source_target_pairs={{96,0},{0,32},{32,64},{64,96},{97,1},{1,33},{33,65},{65,97},{98,2}... | collective-permute-start | bytes 1769480 | tf_op jit(solution)/shard_map/ppermute | solution.py:19
  174.4 14.0 %collective-permute-start.16 = (bf16[256,1152]{1,0:T(8,128)(2,1)S(1)}, bf16[256,1152]{1,0:T(8,128)(2,1)S(1)}, u32[]{:S(2)}, u32[]{:S(2)}) collective-permute-start(bf16[256,1152]{1,0:T(8,128)(2,1)S(1)} %collective-permute-done.14.refs_1_), channel_id=1, source_target_pairs={{32,0},{64,32},{96,64},{0,96},{33,1},{65,33},{97,65},{1,97},{34,2}... | collective-permute-start | bytes 1769480 | tf_op jit(solution)/shard_map/ppermute | solution.py:19
  174.7 15.2 %collective-permute-start.18 = (bf16[256,1152]{1,0:T(8,128)(2,1)S(1)}, bf16[256,1152]{1,0:T(8,128)(2,1)S(1)}, u32[]{:S(2)}, u32[]{:S(2)}) collective-permute-start(bf16[256,1152]{1,0:T(8,128)(2,1)S(1)} %collective-permute-done.14.refs_1_), channel_id=1, source_target_pairs={{64,0},{96,32},{0,64},{32,96},{65,1},{97,33},{1,65},{33,97},{66,2}... | collective-permute-start | bytes 1769480 | tf_op jit(solution)/shard_map/ppermute | solution.py:19
  177.7 26.4 %collective-permute-start.20 = (bf16[256,1152]{1,0:T(8,128)(2,1)S(1)}, bf16[256,1152]{1,0:T(8,128)(2,1)S(1)}, u32[]{:S(2)}, u32[]{:S(2)}) collective-permute-start(bf16[256,1152]{1,0:T(8,128)(2,1)S(1)} %collective-permute-done.14.refs_1_), channel_id=1, source_target_pairs={{96,0},{0,32},{32,64},{64,96},{97,1},{1,33},{33,65},{65,97},{98,2}... | collective-permute-start | bytes 1769480 | tf_op jit(solution)/shard_map/ppermute | solution.py:19
  220.1 90.4 %all-to-all-start = ((bf16[32,56,1152]{2,1,0:T(8,128)(2,1)}), bf16[32,56,1152]{2,1,0:T(8,128)(2,1)}, u32[]{:S(2)}, u32[]{:S(2)}) async-start(bf16[32,56,1152]{2,1,0:T(8,128)(2,1)} %bitcast.24), calls=%async_computation | async-start | bytes 8257536 | tf_op jit(solution)/shard_map/all_to_all | solution.py:162
  (6 other events, 30.5 us)

commit v3 on v0

v3 whole, which is shorter than its diff:
```python
import functools

import jax
import jax.numpy as jnp
from jax import lax
from jax.experimental import pallas as pl
from jax.experimental.pallas import tpu as pltpu
from jax.sharding import Mesh, PartitionSpec as P

AXES = ("z", "yh", "x", "yl", "c")
SIZES = (4, 2, 4, 2, 2)
PLANE = ("yh", "x", "yl")
CHIPS = 16
PAIRS = 256
DEPTH = 128
CUT = 1024
STEPS = (0, 1, 3, 2)
Y = ("yh", "yl")
HBM = pl.BlockSpec(memory_space=pltpu.HBM)
VMEM = pl.BlockSpec(memory_space=pltpu.VMEM)
HINT = pl.CostEstimate(flops=10**6, bytes_accessed=1 << 16, transcendentals=0)


def shift(value, axis, step, size):
    return lax.ppermute(value, axis, [((i + step) % size, i) for i in range(size)])


def around(value, axis):
    return tuple(shift(value, axis, step, 4) for step in STEPS[1:])


def product_kernel(held, at_column, *refs):
    panels, refs = refs[:4], refs[4:]
    arrays, energy, pair = refs[:held], refs[held], refs[held + 1]
    out, panel, block, result, loads, fetches, stores = refs[-7:]
    z, yh, yl = lax.axis_index("z"), lax.axis_index("yh"), lax.axis_index("yl")
    rows, width = panels[0].shape[1], pair.shape[1]
    cuts = [(at, min(CUT, width - at)) for at in range(0, width, CUT)]

    def load(i, x):
        there = lax.rem(yh * 2 + yl + STEPS[i], 4)
        row = pl.multiple_of(there // 2 * rows, rows)
        slot = pl.multiple_of((x * 2 + lax.rem(there, 2)) * PAIRS, PAIRS)
        return pltpu.make_async_copy(
            panels[i].at[x], panel.at[pl.ds(row, rows), pl.ds(slot, PAIRS)], loads.at[i, x]
        )

    def fetch(cut):
        at, size = cuts[cut]
        copies = []
        for i in range(8):
            if i < 4:
                low, source = yh, arrays[0].at[i]
            else:
                low, source = 1 - yh, arrays[i - 3]
            slot = pl.multiple_of(lax.rem(z + STEPS[i % 4], 4) * 2 * PAIRS + low * PAIRS, PAIRS)
            target = block.at[pl.ds(slot, PAIRS), pl.ds(at, size)]
            sem = fetches.at[cut, len(copies)]
            copies.append(pltpu.make_async_copy(source.at[:, pl.ds(at, size)], target, sem))
        return copies

    def store(b):
        here = pl.ds(b * rows, rows)
        return pltpu.make_async_copy(result.at[here], out.at[here, pl.ds(at_column, width)], stores.at[b])

    copies = [load(i, x) for i in range(4) for x in range(4)]
    pieces = [fetch(cut) for cut in range(len(cuts))]
    for copy in copies + [copy for piece in pieces for copy in piece]:
        copy.start()
    for copy in copies:
        copy.wait()
    for cut, (at, size) in enumerate(cuts):
        for copy in pieces[cut]:
            copy.wait()
        for b in range(2):
            here = (pl.ds(b * rows, rows), pl.ds(at, size))
            residual = jnp.dot(panel[here[0], :], block[:, here[1]], preferred_element_type=jnp.float32)
            denominator = energy[here[0]] - pair[:, here[1]]
            inverse = pl.reciprocal(denominator, approx=True)
            inverse = inverse * (2.0 - denominator * inverse)
            result[here] = (residual * inverse).astype(out.dtype)
            if cut == len(cuts) - 1:
                store(b).start()
    for b in range(2):
        store(b).wait()


def product(panels, arrays, energy, pair, started=None):
    rows, width = energy.shape[0], pair.shape[1]
    cuts = -(-width // CUT)
    operands = [*panels, *arrays, energy, pair] + ([] if started is None else [started])
    at_column = 0 if started is None else width
    return pl.pallas_call(
        functools.partial(product_kernel, len(arrays), at_column),
        out_shape=jax.ShapeDtypeStruct((rows, 2 * width), jnp.bfloat16),
        in_specs=[HBM] * (4 + len(arrays)) + [VMEM] * 2 + ([] if started is None else [HBM]),
        out_specs=HBM,
        scratch_shapes=[
            pltpu.VMEM((rows, 8 * PAIRS), jnp.bfloat16),
            pltpu.VMEM((8 * PAIRS, width), jnp.bfloat16),
            pltpu.VMEM((rows, width), jnp.bfloat16),
            pltpu.SemaphoreType.DMA((4, 4)),
            pltpu.SemaphoreType.DMA((cuts, 8)),
            pltpu.SemaphoreType.DMA((2,)),
        ],
        input_output_aliases={} if started is None else {len(operands) - 1: 0},
        compiler_params=pltpu.CompilerParams(vmem_limit_bytes=60 << 20),
        cost_estimate=HINT,
        name="product",
    )(*operands)


def place_kernel(columns, piece, out, stage, loads, stores):
    c = lax.axis_index("c")

    def load(s):
        return pltpu.make_async_copy(piece.at[s], stage.at[s], loads.at[s])

    def store(s, h):
        at = (s % 8) * 4 * columns + s // 8 * columns + (1 - c if h else c) * 2 * columns
        target = out.at[:, pl.ds(pl.multiple_of(at, DEPTH), columns)]
        return pltpu.make_async_copy(stage.at[s, :, pl.ds(h * columns, columns)], target, stores.at[s, h])

    for s in range(CHIPS):
        load(s).start()
    for s in range(CHIPS):
        load(s).wait()
        for h in range(2):
            store(s, h).start()
    for s in range(CHIPS):
        for h in range(2):
            store(s, h).wait()


def place(piece):
    rows, width = piece.shape[1:]
    return pl.pallas_call(
        functools.partial(place_kernel, width // 2),
        out_shape=jax.ShapeDtypeStruct((rows, CHIPS * width), jnp.bfloat16),
        in_specs=[HBM],
        out_specs=HBM,
        scratch_shapes=[
            pltpu.VMEM(piece.shape, jnp.bfloat16),
            pltpu.SemaphoreType.DMA((CHIPS,)),
            pltpu.SemaphoreType.DMA((CHIPS, 2)),
        ],
        compiler_params=pltpu.CompilerParams(vmem_limit_bytes=60 << 20),
        cost_estimate=HINT,
        name="place",
    )(piece)


def local(amplitudes, integrals, occ_energy, slab_energy, virt_energy):
    yh, c = lax.axis_index("yh"), lax.axis_index("c")
    portion = amplitudes.shape[0] // CHIPS
    columns = integrals.shape[1] // 2
    after = lax.optimization_barrier

    def pick(value, index, axis):
        return lax.dynamic_index_in_dim(value, index, axis, False)

    def part(h):
        return lax.dynamic_slice(integrals, (0, h * columns), (PAIRS, columns))

    def swap(value):
        return shift(value, "c", 1, 2)

    mine, away = part(yh), part(1 - yh)
    up, down = around(mine, "z")[:2]
    other = shift(away, "yh", 1, 2)
    rows = amplitudes.reshape(8, 2, portion, -1)
    kept = pick(rows, c, 1).reshape(8 * portion, -1)
    got = swap(pick(rows, 1 - c, 1).reshape(8 * portion, -1))
    both = jnp.where(c == 0, jnp.concatenate([kept, got], 1), jnp.concatenate([got, kept], 1))
    occ = pick(occ_energy.reshape(8, 2, portion), c, 1).reshape(1, -1)
    along = lax.all_gather(both, "x", axis=0)

    other, along, occ, slab_energy = after((other, along, occ, slab_energy))
    others = around(other, "z")
    two = shift(up[:DEPTH], "z", 1, 4), shift(down[DEPTH:], "z", 3, 4)
    panels = (along,) + around(along, Y)
    occ_other = shift(occ, "yh", 1, 2)
    slab_other = swap(slab_energy)
    here = jnp.stack([mine, up, down, jnp.concatenate(two)])
    energy = jnp.where(yh == 0, jnp.concatenate([occ, occ_other]), jnp.concatenate([occ_other, occ]))
    energy = energy.reshape(-1, 1)

    def pair(slab):
        pairs = (slab[:, None] + virt_energy[None, :]).reshape(2, columns)
        return pick(pairs, yh, 0).reshape(1, -1)

    pairs, pairs2 = pair(slab_energy), pair(slab_other)
    others, here, panels, energy, pairs, pairs2 = after((others, here, panels, energy, pairs, pairs2))
    there = tuple(swap(value) for value in (here, other) + others)
    update = product(panels, (here, other) + others, energy, pairs)
    update = product(panels, there, energy, pairs2, update)
    return place(lax.all_to_all(update.reshape(CHIPS, portion, -1), PLANE, 0, 0, tiled=True))


def solution(mesh):
    fine = Mesh(mesh.devices.reshape(SIZES), AXES)
    split = P(("z", "yh"), ("x", "yl", "c"))
    return jax.shard_map(
        local,
        mesh=fine,
        in_specs=(split, split, P(("z", "yh")), P(("x", "yl", "c")), P()),
        out_specs=P(AXES, None),
        check_vma=False,
    )
```

time: 343 us -> 222 us (0.65)
  waiting for transfers between devices: 223 us -> 46.6 us
  Pallas kernels: 0 us -> 35.3 us
  starting transfers between devices: 0.04 us -> 28.8 us
  matrix products: 18.4 us -> 0 us
  blocking collectives: 83.9 us -> 97 us
  between operations: 13.4 us -> 0.33 us
  other arithmetic: 0.76 us -> 5.4 us
  local copies, waits for them, and re-layouts: 3.45 us -> 7.98 us
    all_gather x2 -> x0, waiting for transfers between devices: 222 us -> none  [the longest x1 175 us: local(): columns = lax.all_gather(integrals, 'row', axis=0, tiled=True)]
    ppermute x0 -> x19, waiting for transfers between devices: none -> 46.6 us  [shift(): lax.ppermute(value, axis, [((i + step) % size, i) for i in range(size)])]
    pallas_call x0 -> x3, Pallas kernels: none -> 35.3 us  [the longest x2 29.5 us: product(): pl.pallas_call(functools.partial(product_kernel, len(arrays), at_column),...]
    ppermute x0 -> x19, starting transfers between devices: none -> 28.8 us  [shift(): lax.ppermute(value, axis, [((i + step) % size, i) for i in range(size)])]
    dot_general x1 -> x0, matrix products: 18.4 us -> none  [local(): residual = jnp.dot(panels, columns, preferred_element_type=jnp.float32)]
    all_gather x0 -> x1, blocking collectives: none -> 13 us  [local(): along = lax.all_gather(both, 'x', axis=0)]
    another operation x0 -> x2, other arithmetic: none -> 4.61 us  [local(): here = jnp.stack([mine, up, down, jnp.concatenate(two)])]
  transfers between devices with their start and end apart: 2 -> 19, of which waited for: 2 -> 7; matrix products, arithmetic and copies ran while one was open for 0% -> 5% of each run, Pallas kernels for 0% -> 7%
where the time goes in v3:
time: 222 us; the launch traced here: 221 us
  blocking collectives  97 us (44%)
  waiting for transfers between devices  46.6 us (21%)
  Pallas kernels  35.3 us (16%)
  starting transfers between devices  28.8 us (13%)
  local copies, waits for them, and re-layouts  7.98 us (4%)
  other arithmetic  5.4 us (2%)
    all_to_all x1, blocking collectives, local(): lax.all_to_all(update.reshape(CHIPS, portion, -1), PLANE, 0, 0, tiled=True)  84 us
    ppermute x19, waiting for transfers between devices, shift(): lax.ppermute(value, axis, [((i + step) % size, i) for i in range(size)])  46.6 us
    pallas_call x2, Pallas kernels, product(): pl.pallas_call(functools.partial(product_kernel, len(arrays), at_column),...  29.5 us
    ppermute x19, starting transfers between devices, shift(): lax.ppermute(value, axis, [((i + step) % size, i) for i in range(size)])  28.8 us
    all_gather x1, blocking collectives, local(): along = lax.all_gather(both, 'x', axis=0)  13 us
    pallas_call x1, Pallas kernels, place(): pl.pallas_call(functools.partial(place_kernel, width // 2), out_shape=jax...  5.8 us
    another operation x2, other arithmetic, local(): here = jnp.stack([mine, up, down, jnp.concatenate(two)])  4.61 us
  transfers between devices with their start and end apart: 19, of which 7 were waited for; matrix products, arithmetic and copies ran while one was open for 5% of the time, Pallas kernels for 7%

profile of v3, /device:TPU:1, one launch (start us, length us, event | category | flops | bytes accessed | tf_op | source)
XLA Modules:
  0.0 221.5 jit_solution(1502136590541625575)
XLA Ops:
  0.0 1.7 constant_dynamic-slice_fusion
  1.7 3.8 %collective-permute-start = (bf16[256,1920]{1,0:T(8,128)(2,1)S(1)}, bf16[256,1920]{1,0:T(8,128)(2,1)}, u32[]{:S(2)}, u32[]{:S(2)}) collective-permute-start(bf16[256,1920]{1,0:T(8,128)(2,1)S(1)} %get-tuple-element.36), channel_id=1, source_target_pairs={{16,0},{0,16},{17,1},{1,17},{18,2},{2,18},{19,3},{3,19},{20,4},{4,... | collective-permute-start | bytes 2949128 | tf_op jit(solution)/shard_map/ppermute | solution.py:25
  5.6 1.0 collective-permute-start.1
  6.6 3.8 %collective-permute-start.5 = (bf16[256,1920]{1,0:T(8,128)(2,1)S(1)}, bf16[256,1920]{1,0:T(8,128)(2,1)}, u32[]{:S(2)}, u32[]{:S(2)}) collective-permute-start(bf16[256,1920]{1,0:T(8,128)(2,1)S(1)} %get-tuple-element.35), channel_id=1, source_target_pairs={{32,0},{64,32},{96,64},{0,96},{33,1},{65,33},{97,65},{1,97},{34,2}... | collective-permute-start | bytes 2949128 | tf_op jit(solution)/shard_map/ppermute | solution.py:25
  10.7 13.0 %all_gather.4.refs_0_ = bf16[4,448,256]{2,1,0:T(8,128)(2,1)S(1)} all-gather(bf16[1,448,256]{2,1,0:T(8,128)(2,1)S(1)} %maximum_select_fusion), channel_id=1, replica_groups=mesh['z'=4,'yh'=2,'x'=4,'yl'=2,'c'=2] {'x'}, dimensions={0}, use_global_device_ids=true | all-gather | bytes 1146880 | tf_op jit(solution)/shard_map/all_gather | solution.py:176
  23.6 3.2 %collective-permute-done.refs_5_ = bf16[256,1920]{1,0:T(8,128)(2,1)} collective-permute-done((bf16[256,1920]{1,0:T(8,128)(2,1)S(1)}, bf16[256,1920]{1,0:T(8,128)(2,1)}, u32[]{:S(2)}, u32[]{:S(2)}) %collective-permute-start) | collective-permute-done | bytes 983072 | tf_op jit(solution)/shard_map/ppermute | solution.py:25
  26.8 1.3 collective-permute-start.10
  28.1 3.3 %collective-permute-done.5 = bf16[256,1920]{1,0:T(8,128)(2,1)} collective-permute-done((bf16[256,1920]{1,0:T(8,128)(2,1)S(1)}, bf16[256,1920]{1,0:T(8,128)(2,1)}, u32[]{:S(2)}, u32[]{:S(2)}) %collective-permute-start.5) | collective-permute-done | bytes 983072 | tf_op jit(solution)/shard_map/ppermute | solution.py:25
  31.5 1.1 slice.8
  32.5 3.6 %collective-permute-start.7 = (bf16[128,1920]{1,0:T(8,128)(2,1)S(1)}, bf16[128,1920]{1,0:T(8,128)(2,1)}, u32[]{:S(2)}, u32[]{:S(2)}) collective-permute-start(bf16[128,1920]{1,0:T(8,128)(2,1)S(1)} %slice.8), channel_id=1, source_target_pairs={{32,0},{64,32},{96,64},{0,96},{33,1},{65,33},{97,65},{1,97},{34,2}... | collective-permute-start | bytes 1474568 | tf_op jit(solution)/shard_map/ppermute | solution.py:25
  36.1 1.8 slice.9
  38.1 1.9 collective-permute-start.13
  40.3 0.6 collective-permute-done.13
  40.8 3.0 %collective-permute-start.2 = (bf16[256,1920]{1,0:T(8,128)(2,1)}, bf16[256,1920]{1,0:T(8,128)(2,1)}, u32[]{:S(2)}, u32[]{:S(2)}) collective-permute-start(bf16[256,1920]{1,0:T(8,128)(2,1)} %collective-permute-done.refs_5_), channel_id=1, source_target_pairs={{32,0},{64,32},{96,64},{0,96},{33,1},{65,33},{97,65},{1,97},{34,2}... | collective-permute-start | bytes 2949128 | tf_op jit(solution)/shard_map/ppermute | solution.py:25
  44.0 5.3 %collective-permute-done.12 = f32[1,448]{1,0:T(1,128)S(1)} collective-permute-done((f32[1,448]{1,0:T(1,128)S(1)}, f32[1,448]{1,0:T(1,128)S(1)}, u32[]{:S(2)}, u32[]{:S(2)}) %collective-permute-start.12) | collective-permute-done | bytes 1824 | tf_op jit(solution)/shard_map/ppermute | solution.py:25
  49.3 1.6 collective-permute-start.3
  51.0 3.3 %collective-permute-start.4 = (bf16[256,1920]{1,0:T(8,128)(2,1)}, bf16[256,1920]{1,0:T(8,128)(2,1)}, u32[]{:S(2)}, u32[]{:S(2)}) collective-permute-start(bf16[256,1920]{1,0:T(8,128)(2,1)} %collective-permute-done.refs_5_), channel_id=1, source_target_pairs={{64,0},{96,32},{0,64},{32,96},{65,1},{97,33},{1,65},{33,97},{66,2}... | collective-permute-start | bytes 2949128 | tf_op jit(solution)/shard_map/ppermute | solution.py:25
  54.3 0.7 collective-permute-start.11
  55.1 0.7 dynamic-slice_add_fusion
  55.9 1.2 maximum_bitcast_fusion
  57.1 3.4 %pad_maximum_fusion.refs_4_ = bf16[4,256,1920]{2,1,0:T(8,128)(2,1)} fusion(bf16[1,256,1920]{2,1,0:T(8,128)(2,1)S(1)} %maximum_bitcast_fusion, bf16[1,256,1920]{2,1,0:T(8,128)(2,1)} %bitcast.6, bf16[1,256,1920]{2,1,0:T(8,128)(2,1)} %bitcast.5, bf16[1,256,1920]{2,1,0:T(8,128)(2,1)S(1)} %bitcast.15), kind=kLoop, calls=%fused_computation | loop fusion | flops 5898240 | bytes 7864320 | tf_op jit(solution)/shard_map/stack | solution.py:184
  60.5 13.9 %collective-permute-done.11.refs_3_ = bf16[4,448,256]{2,1,0:T(8,128)(2,1)} collective-permute-done((bf16[4,448,256]{2,1,0:T(8,128)(2,1)S(1)}, bf16[4,448,256]{2,1,0:T(8,128)(2,1)}, u32[]{:S(2)}, u32[]{:S(2)}) %collective-permute-start.11) | collective-permute-done | bytes 917536 | tf_op jit(solution)/shard_map/ppermute | solution.py:25
  74.4 17.5 %collective-permute-done.9.refs_1_ = bf16[4,448,256]{2,1,0:T(8,128)(2,1)} collective-permute-done((bf16[4,448,256]{2,1,0:T(8,128)(2,1)S(1)}, bf16[4,448,256]{2,1,0:T(8,128)(2,1)}, u32[]{:S(2)}, u32[]{:S(2)}) %collective-permute-start.9) | collective-permute-done | bytes 917536 | tf_op jit(solution)/shard_map/ppermute | solution.py:25
  91.9 2.8 %collective-permute-done.4.refs_8_ = bf16[256,1920]{1,0:T(8,128)(2,1)} collective-permute-done((bf16[256,1920]{1,0:T(8,128)(2,1)}, bf16[256,1920]{1,0:T(8,128)(2,1)}, u32[]{:S(2)}, u32[]{:S(2)}) %collective-permute-start.4) | collective-permute-done | bytes 983072 | tf_op jit(solution)/shard_map/ppermute | solution.py:25
  94.7 3.7 %collective-permute-start.14 = (bf16[4,256,1920]{2,1,0:T(8,128)(2,1)}, bf16[4,256,1920]{2,1,0:T(8,128)(2,1)}, u32[]{:S(2)}, u32[]{:S(2)}) collective-permute-start(bf16[4,256,1920]{2,1,0:T(8,128)(2,1)} %pad_maximum_fusion.refs_4_), channel_id=1, source_target_pairs={{1,0},{0,1},{3,2},{2,3},{5,4},{4,5},{7,6},{6,7},{9,8},{8,9},{11,10... | collective-permute-start | bytes 11796488 | tf_op jit(solution)/shard_map/ppermute | solution.py:25
  98.9 0.5 collective-permute-start.18
  99.4 1.0 copy.16.refs_9_
  100.4 14.8 %product.2.refs_11_ = bf16[896,3840]{1,0:T(8,128)(2,1)} custom-call(bf16[4,448,256]{2,1,0:T(8,128)(2,1)} %copy-done, bf16[4,448,256]{2,1,0:T(8,128)(2,1)} %collective-permute-done.9.refs_1_, bf16[4,448,256]{2,1,0:T(8,128)(2,1)} %copy-done.1, bf16[4,448,256]{2,1,0:T(8,128)(2,1)} %collective-permute-done.11.refs_3_, ...), custom_call_target="tpu_custom_call" | custom-call | flops 1000000 | bytes 65536 | tf_op jit(solution)/shard_map/product/pallas_call | solution.py:93
  115.2 1.0 copy-done.2
  116.7 14.8 %product.3 = bf16[896,3840]{1,0:T(8,128)(2,1)} custom-call(bf16[4,448,256]{2,1,0:T(8,128)(2,1)} %copy-done, bf16[4,448,256]{2,1,0:T(8,128)(2,1)} %collective-permute-done.9.refs_1_, bf16[4,448,256]{2,1,0:T(8,128)(2,1)} %copy-done.1, bf16[4,448,256]{2,1,0:T(8,128)(2,1)} %collective-permute-done.11.refs_3_, ...), custom_call_target="tpu_custom_call", output_to_operand_aliasing={{}: (11, {})} | custom-call | flops 1000000 | bytes 65536 | tf_op jit(solution)/shard_map/product/pallas_call | solution.py:93
  131.5 84.0 %all_to_all.5.piece = bf16[16,56,3840]{2,1,0:T(8,128)(2,1)} all-to-all(bf16[16,56,3840]{2,1,0:T(8,128)(2,1)} %bitcast.14), channel_id=1, replica_groups=mesh['z'=4,'yh'=2,'x'=4,'yl'=2,'c'=2] {'yh','x','yl'}, dimensions={0} | all-to-all | bytes 13762560 | tf_op jit(solution)/shard_map/all_to_all | solution.py:197
  215.5 5.8 %place.1 = bf16[56,61440]{1,0:T(8,128)(2,1)} custom-call(bf16[16,56,3840]{2,1,0:T(8,128)(2,1)} %all_to_all.5.piece), custom_call_target="tpu_custom_call" | custom-call | flops 1000000 | bytes 65536 | tf_op jit(solution)/shard_map/place/pallas_call | solution.py:137
  (51 shorter events, 2.1 us)
Async XLA Ops:
  0.0 5.5 %copy-start.5 = (bf16[896,128]{1,0:T(8,128)(2,1)S(1)}, bf16[896,128]{1,0:T(8,128)(2,1)}, u32[]{:S(2)}) copy-start(bf16[896,128]{1,0:T(8,128)(2,1)} %param.5) | copy-start | bytes 688132
  0.0 10.4 %copy-start.6 = (f32[896]{0:T(1024)S(1)}, f32[896]{0:T(1024)}, u32[]{:S(2)}) copy-start(f32[896]{0:T(1024)} %param.7) | copy-start | bytes 10756
  0.0 38.0 %copy-start.7 = (f32[960]{0:T(1024)S(1)}, f32[960]{0:T(1024)}, u32[]{:S(2)}) copy-start(f32[960]{0:T(1024)} %param.9) | copy-start | bytes 11524
  0.0 38.1 %copy-start.8 = (f32[4]{0:T(128)S(1)}, f32[4]{0:T(128)}, u32[]{:S(2)}) copy-start(f32[4]{0:T(128)} %param.8) | copy-start | bytes 52
  1.7 25.1 %collective-permute-start = (bf16[256,1920]{1,0:T(8,128)(2,1)S(1)}, bf16[256,1920]{1,0:T(8,128)(2,1)}, u32[]{:S(2)}, u32[]{:S(2)}) collective-permute-start(bf16[256,1920]{1,0:T(8,128)(2,1)S(1)} %get-tuple-element.36), channel_id=1, source_target_pairs={{16,0},{0,16},{17,1},{1,17},{18,2},{2,18},{19,3},{3,19},{20,4},{4,... | collective-permute-start | bytes 2949128 | tf_op jit(solution)/shard_map/ppermute | solution.py:25
  5.6 5.0 %collective-permute-start.1 = (bf16[448,128]{1,0:T(8,128)(2,1)S(1)}, bf16[448,128]{1,0:T(8,128)(2,1)S(1)}, u32[]{:S(2)}, u32[]{:S(2)}) collective-permute-start(bf16[448,128]{1,0:T(8,128)(2,1)S(1)} %bitcast.18), channel_id=1, source_target_pairs={{1,0},{0,1},{3,2},{2,3},{5,4},{4,5},{7,6},{6,7},{9,8},{8,9},{11,10... | collective-permute-start | bytes 344072 | tf_op jit(solution)/shard_map/ppermute | solution.py:25
  6.6 24.9 %collective-permute-start.5 = (bf16[256,1920]{1,0:T(8,128)(2,1)S(1)}, bf16[256,1920]{1,0:T(8,128)(2,1)}, u32[]{:S(2)}, u32[]{:S(2)}) collective-permute-start(bf16[256,1920]{1,0:T(8,128)(2,1)S(1)} %get-tuple-element.35), channel_id=1, source_target_pairs={{32,0},{64,32},{96,64},{0,96},{33,1},{65,33},{97,65},{1,97},{34,2}... | collective-permute-start | bytes 2949128 | tf_op jit(solution)/shard_map/ppermute | solution.py:25
  10.4 25.8 %collective-permute-start.6 = (bf16[256,1920]{1,0:T(8,128)(2,1)S(1)}, bf16[256,1920]{1,0:T(8,128)(2,1)}, u32[]{:S(2)}, u32[]{:S(2)}) collective-permute-start(bf16[256,1920]{1,0:T(8,128)(2,1)S(1)} %get-tuple-element.35), channel_id=1, source_target_pairs={{96,0},{0,32},{32,64},{64,96},{97,1},{1,33},{33,65},{65,97},{98,2}... | collective-permute-start | bytes 2949128 | tf_op jit(solution)/shard_map/ppermute | solution.py:25
  23.6 36.9 %copy-start = (bf16[4,448,256]{2,1,0:T(8,128)(2,1)}, bf16[4,448,256]{2,1,0:T(8,128)(2,1)S(1)}, u32[]{:S(2)}) copy-start(bf16[4,448,256]{2,1,0:T(8,128)(2,1)S(1)} %all_gather.4.refs_0_) | copy-start | bytes 2752516
  26.8 28.2 %collective-permute-start.10 = (bf16[4,448,256]{2,1,0:T(8,128)(2,1)S(1)}, bf16[4,448,256]{2,1,0:T(8,128)(2,1)S(1)}, u32[]{:S(2)}, u32[]{:S(2)}) collective-permute-start(bf16[4,448,256]{2,1,0:T(8,128)(2,1)S(1)} %all_gather.4.refs_0_), channel_id=1, source_target_pairs={{18,0},{0,2},{2,16},{16,18},{19,1},{1,3},{3,17},{17,19},{22,4},{4,... | collective-permute-start | bytes 2752520 | tf_op jit(solution)/shard_map/ppermute | solution.py:25
  32.5 18.4 %collective-permute-start.7 = (bf16[128,1920]{1,0:T(8,128)(2,1)S(1)}, bf16[128,1920]{1,0:T(8,128)(2,1)}, u32[]{:S(2)}, u32[]{:S(2)}) collective-permute-start(bf16[128,1920]{1,0:T(8,128)(2,1)S(1)} %slice.8), channel_id=1, source_target_pairs={{32,0},{64,32},{96,64},{0,96},{33,1},{65,33},{97,65},{1,97},{34,2}... | collective-permute-start | bytes 1474568 | tf_op jit(solution)/shard_map/ppermute | solution.py:25
  38.0 16.3 %collective-permute-start.8 = (bf16[128,1920]{1,0:T(8,128)(2,1)}, bf16[128,1920]{1,0:T(8,128)(2,1)}, u32[]{:S(2)}, u32[]{:S(2)}) collective-permute-start(bf16[128,1920]{1,0:T(8,128)(2,1)} %slice.9), channel_id=1, source_target_pairs={{96,0},{0,32},{32,64},{64,96},{97,1},{1,33},{33,65},{65,97},{98,2}... | collective-permute-start | bytes 1474568 | tf_op jit(solution)/shard_map/ppermute | solution.py:25
  38.0 11.4 %collective-permute-start.12 = (f32[1,448]{1,0:T(1,128)S(1)}, f32[1,448]{1,0:T(1,128)S(1)}, u32[]{:S(2)}, u32[]{:S(2)}) collective-permute-start(f32[1,448]{1,0:T(1,128)S(1)} %reshape.114), channel_id=1, source_target_pairs={{16,0},{0,16},{17,1},{1,17},{18,2},{2,18},{19,3},{3,19},{20,4},{4,... | collective-permute-start | bytes 5384 | tf_op jit(solution)/shard_map/ppermute | solution.py:25
  38.1 2.7 %collective-permute-start.13 = (f32[4]{0:T(128)S(1)}, f32[4]{0:T(128)S(1)}, u32[]{:S(2)}, u32[]{:S(2)}) collective-permute-start(f32[4]{0:T(128)S(1)} %copy-done.8), channel_id=1, source_target_pairs={{1,0},{0,1},{3,2},{2,3},{5,4},{4,5},{7,6},{6,7},{9,8},{8,9},{11,10... | collective-permute-start | bytes 56 | tf_op jit(solution)/shard_map/ppermute | solution.py:25
  40.8 51.1 %collective-permute-start.2 = (bf16[256,1920]{1,0:T(8,128)(2,1)}, bf16[256,1920]{1,0:T(8,128)(2,1)}, u32[]{:S(2)}, u32[]{:S(2)}) collective-permute-start(bf16[256,1920]{1,0:T(8,128)(2,1)} %collective-permute-done.refs_5_), channel_id=1, source_target_pairs={{32,0},{64,32},{96,64},{0,96},{33,1},{65,33},{97,65},{1,97},{34,2}... | collective-permute-start | bytes 2949128 | tf_op jit(solution)/shard_map/ppermute | solution.py:25
  49.3 42.5 %collective-permute-start.3 = (bf16[256,1920]{1,0:T(8,128)(2,1)}, bf16[256,1920]{1,0:T(8,128)(2,1)}, u32[]{:S(2)}, u32[]{:S(2)}) collective-permute-start(bf16[256,1920]{1,0:T(8,128)(2,1)} %collective-permute-done.refs_5_), channel_id=1, source_target_pairs={{96,0},{0,32},{32,64},{64,96},{97,1},{1,33},{33,65},{65,97},{98,2}... | collective-permute-start | bytes 2949128 | tf_op jit(solution)/shard_map/ppermute | solution.py:25
  51.0 43.7 %collective-permute-start.4 = (bf16[256,1920]{1,0:T(8,128)(2,1)}, bf16[256,1920]{1,0:T(8,128)(2,1)}, u32[]{:S(2)}, u32[]{:S(2)}) collective-permute-start(bf16[256,1920]{1,0:T(8,128)(2,1)} %collective-permute-done.refs_5_), channel_id=1, source_target_pairs={{64,0},{96,32},{0,64},{32,96},{65,1},{97,33},{1,65},{33,97},{66,2}... | collective-permute-start | bytes 2949128 | tf_op jit(solution)/shard_map/ppermute | solution.py:25
  54.3 20.1 %collective-permute-start.11 = (bf16[4,448,256]{2,1,0:T(8,128)(2,1)S(1)}, bf16[4,448,256]{2,1,0:T(8,128)(2,1)}, u32[]{:S(2)}, u32[]{:S(2)}) collective-permute-start(bf16[4,448,256]{2,1,0:T(8,128)(2,1)S(1)} %all_gather.4.refs_0_), channel_id=1, source_target_pairs={{16,0},{18,2},{0,16},{2,18},{17,1},{19,3},{1,17},{3,19},{20,4},{22... | collective-permute-start | bytes 2752520 | tf_op jit(solution)/shard_map/ppermute | solution.py:25
  55.0 5.4 %copy-start.1 = (bf16[4,448,256]{2,1,0:T(8,128)(2,1)}, bf16[4,448,256]{2,1,0:T(8,128)(2,1)S(1)}, u32[]{:S(2)}) copy-start(bf16[4,448,256]{2,1,0:T(8,128)(2,1)S(1)} %collective-permute-done.10.refs_2_) | copy-start | bytes 2752516
  55.0 36.8 %collective-permute-start.9 = (bf16[4,448,256]{2,1,0:T(8,128)(2,1)S(1)}, bf16[4,448,256]{2,1,0:T(8,128)(2,1)}, u32[]{:S(2)}, u32[]{:S(2)}) collective-permute-start(bf16[4,448,256]{2,1,0:T(8,128)(2,1)S(1)} %all_gather.4.refs_0_), channel_id=1, source_target_pairs={{2,0},{16,2},{18,16},{0,18},{3,1},{17,3},{19,17},{1,19},{6,4},{20,... | collective-permute-start | bytes 2752520 | tf_op jit(solution)/shard_map/ppermute | solution.py:25
  94.7 20.5 %collective-permute-start.14 = (bf16[4,256,1920]{2,1,0:T(8,128)(2,1)}, bf16[4,256,1920]{2,1,0:T(8,128)(2,1)}, u32[]{:S(2)}, u32[]{:S(2)}) collective-permute-start(bf16[4,256,1920]{2,1,0:T(8,128)(2,1)} %pad_maximum_fusion.refs_4_), channel_id=1, source_target_pairs={{1,0},{0,1},{3,2},{2,3},{5,4},{4,5},{7,6},{6,7},{9,8},{8,9},{11,10... | collective-permute-start | bytes 11796488 | tf_op jit(solution)/shard_map/ppermute | solution.py:25
  98.4 16.8 %collective-permute-start.15 = (bf16[256,1920]{1,0:T(8,128)(2,1)}, bf16[256,1920]{1,0:T(8,128)(2,1)S(1)}, u32[]{:S(2)}, u32[]{:S(2)}) collective-permute-start(bf16[256,1920]{1,0:T(8,128)(2,1)} %collective-permute-done.refs_5_), channel_id=1, source_target_pairs={{1,0},{0,1},{3,2},{2,3},{5,4},{4,5},{7,6},{6,7},{9,8},{8,9},{11,10... | collective-permute-start | bytes 2949128 | tf_op jit(solution)/shard_map/ppermute | solution.py:25
  98.4 16.8 %collective-permute-start.16 = (bf16[256,1920]{1,0:T(8,128)(2,1)}, bf16[256,1920]{1,0:T(8,128)(2,1)S(1)}, u32[]{:S(2)}, u32[]{:S(2)}) collective-permute-start(bf16[256,1920]{1,0:T(8,128)(2,1)} %collective-permute-done.2.refs_6_), channel_id=1, source_target_pairs={{1,0},{0,1},{3,2},{2,3},{5,4},{4,5},{7,6},{6,7},{9,8},{8,9},{11,10... | collective-permute-start | bytes 2949128 | tf_op jit(solution)/shard_map/ppermute | solution.py:25
  98.9 16.3 %collective-permute-start.17 = (bf16[256,1920]{1,0:T(8,128)(2,1)}, bf16[256,1920]{1,0:T(8,128)(2,1)S(1)}, u32[]{:S(2)}, u32[]{:S(2)}) collective-permute-start(bf16[256,1920]{1,0:T(8,128)(2,1)} %collective-permute-done.3.refs_7_), channel_id=1, source_target_pairs={{1,0},{0,1},{3,2},{2,3},{5,4},{4,5},{7,6},{6,7},{9,8},{8,9},{11,10... | collective-permute-start | bytes 2949128 | tf_op jit(solution)/shard_map/ppermute | solution.py:25
  98.9 16.3 %collective-permute-start.18 = (bf16[256,1920]{1,0:T(8,128)(2,1)}, bf16[256,1920]{1,0:T(8,128)(2,1)}, u32[]{:S(2)}, u32[]{:S(2)}) collective-permute-start(bf16[256,1920]{1,0:T(8,128)(2,1)} %collective-permute-done.4.refs_8_), channel_id=1, source_target_pairs={{1,0},{0,1},{3,2},{2,3},{5,4},{4,5},{7,6},{6,7},{9,8},{8,9},{11,10... | collective-permute-start | bytes 2949128 | tf_op jit(solution)/shard_map/ppermute | solution.py:25
  115.2 1.0 copy-start.2
  115.2 1.2 copy-start.3
  115.2 1.5 copy-start.4

commit v4 on v3

v4 whole, which is shorter than its diff:
```python
import functools

import jax
import jax.numpy as jnp
from jax import lax
from jax.experimental import pallas as pl
from jax.experimental.pallas import tpu as pltpu
from jax.sharding import Mesh, PartitionSpec as P

AXES = ("z", "yh", "x", "yl", "c")
SIZES = (4, 2, 4, 2, 2)
PLANE = ("yh", "x", "yl")
CHIPS = 16
PAIRS = 256
DEPTH = 128
CUTS = ((0, 256), (256, 640), (896, 1024))
STEPS = (0, 1, 3, 2)
Y = ("yh", "yl")
HBM = pl.BlockSpec(memory_space=pltpu.HBM)
VMEM = pl.BlockSpec(memory_space=pltpu.VMEM)
HINT = pl.CostEstimate(flops=10**6, bytes_accessed=1 << 16, transcendentals=0)


def shift(value, axis, step, size):
    return lax.ppermute(value, axis, [((i + step) % size, i) for i in range(size)])


def near(value, axis):
    return shift(value, axis, 1, 4), shift(value, axis, 3, 4)


def far(up, down, axis):
    cut = up.shape[0] // 2
    return shift(up[:cut], axis, 1, 4), shift(down[cut:], axis, 3, 4)


def product_kernel(at_column, *refs):
    panels, arrays, energy, pair = refs[:5], refs[5:11], refs[11], refs[12]
    out, panel, block, result, loads, fetches, stores = refs[-7:]
    z, yh, yl = lax.axis_index("z"), lax.axis_index("yh"), lax.axis_index("yl")
    rows, width = panels[0].shape[1], pair.shape[1]
    cuts = [(at, size) for at, size in CUTS if at < width]

    def load(i, x):
        there = lax.rem(yh * 2 + yl + STEPS[i], 4)
        row = pl.multiple_of(there // 2 * rows, rows)
        slot = pl.multiple_of((x * 2 + lax.rem(there, 2)) * PAIRS, PAIRS)
        source = panels[i].at[x] if i < 3 else panels[3 + x // 2].at[x % 2]
        return pltpu.make_async_copy(source, panel.at[pl.ds(row, rows), pl.ds(slot, PAIRS)], loads.at[i, x])

    def fetch(cut):
        at, size = cuts[cut]
        copies = []
        parts = [(yh, STEPS[i], 0, arrays[0].at[i]) for i in range(4)]
        parts += [(1 - yh, STEPS[i], 0, arrays[i + 1]) for i in range(3)]
        parts += [(1 - yh, 2, i * DEPTH, arrays[i + 4]) for i in range(2)]
        for low, step, skip, source in parts:
            count = source.shape[0]
            slot = pl.multiple_of(lax.rem(z + step, 4) * 2 * PAIRS + low * PAIRS + skip, DEPTH)
            target = block.at[pl.ds(slot, count), pl.ds(at, size)]
            sem = fetches.at[cut, len(copies)]
            copies.append(pltpu.make_async_copy(source.at[:, pl.ds(at, size)], target, sem))
        return copies

    def store(cut, b):
        at, size = cuts[cut]
        here = pl.ds(b * rows, rows)
        source = result.at[here, pl.ds(at, size)]
        return pltpu.make_async_copy(source, out.at[here, pl.ds(at_column + at, size)], stores.at[cut, b])

    copies = [load(i, x) for i in range(4) for x in range(4)]
    pieces = [fetch(cut) for cut in range(len(cuts))]
    for copy in copies + [copy for piece in pieces for copy in piece]:
        copy.start()
    for copy in copies:
        copy.wait()
    for cut, (at, size) in enumerate(cuts):
        for copy in pieces[cut]:
            copy.wait()
        for b in range(2):
            here = (pl.ds(b * rows, rows), pl.ds(at, size))
            residual = jnp.dot(panel[here[0], :], block[:, here[1]], preferred_element_type=jnp.float32)
            denominator = energy[here[0]] - pair[:, here[1]]
            inverse = pl.reciprocal(denominator, approx=True)
            inverse = inverse * (2.0 - denominator * inverse)
            result[here] = (residual * inverse).astype(out.dtype)
            store(cut, b).start()
    for cut in range(len(cuts)):
        for b in range(2):
            store(cut, b).wait()


def product(panels, arrays, energy, pair, started=None):
    rows, width = energy.shape[0], pair.shape[1]
    cuts = len(CUTS)
    operands = [*panels, *arrays, energy, pair] + ([] if started is None else [started])
    at_column = 0 if started is None else width
    return pl.pallas_call(
        functools.partial(product_kernel, at_column),
        out_shape=jax.ShapeDtypeStruct((rows, 2 * width), jnp.bfloat16),
        in_specs=[HBM] * (len(panels) + len(arrays)) + [VMEM] * 2 + ([] if started is None else [HBM]),
        out_specs=HBM,
        scratch_shapes=[
            pltpu.VMEM((rows, 8 * PAIRS), jnp.bfloat16),
            pltpu.VMEM((8 * PAIRS, width), jnp.bfloat16),
            pltpu.VMEM((rows, width), jnp.bfloat16),
            pltpu.SemaphoreType.DMA((4, 4)),
            pltpu.SemaphoreType.DMA((cuts, 9)),
            pltpu.SemaphoreType.DMA((cuts, 2)),
        ],
        input_output_aliases={} if started is None else {len(operands) - 1: 0},
        compiler_params=pltpu.CompilerParams(vmem_limit_bytes=60 << 20),
        cost_estimate=HINT,
        name="product",
    )(*operands)


def place_kernel(columns, piece, out, stores):
    c = lax.axis_index("c")
    copies = []
    for s in range(CHIPS):
        for h in range(2):
            at = (s % 8) * 4 * columns + s // 8 * columns + (1 - c if h else c) * 2 * columns
            target = out.at[:, pl.ds(pl.multiple_of(at, DEPTH), columns)]
            source = piece.at[s, :, pl.ds(h * columns, columns)]
            copies.append(pltpu.make_async_copy(source, target, stores.at[s, h]))
    for copy in copies:
        copy.start()
    for copy in copies:
        copy.wait()


def place(piece):
    rows, width = piece.shape[1:]
    return pl.pallas_call(
        functools.partial(place_kernel, width // 2),
        out_shape=jax.ShapeDtypeStruct((rows, CHIPS * width), jnp.bfloat16),
        in_specs=[VMEM],
        out_specs=HBM,
        scratch_shapes=[pltpu.SemaphoreType.DMA((CHIPS, 2))],
        compiler_params=pltpu.CompilerParams(vmem_limit_bytes=16 << 20),
        cost_estimate=HINT,
        name="place",
    )(piece)


def local(amplitudes, integrals, occ_energy, slab_energy, virt_energy):
    yh, c = lax.axis_index("yh"), lax.axis_index("c")
    portion = amplitudes.shape[0] // CHIPS
    columns = integrals.shape[1] // 2
    after = lax.optimization_barrier

    def pick(value, index, axis):
        return lax.dynamic_index_in_dim(value, index, axis, False)

    def part(h):
        return lax.dynamic_slice(integrals, (0, h * columns), (PAIRS, columns))

    def swap(value):
        return shift(value, "c", 1, 2)

    mine, away = part(yh), part(1 - yh)
    up, down = near(mine, "z")
    other = shift(away, "yh", 1, 2)
    rows = amplitudes.reshape(8, 2, portion, -1)
    kept = pick(rows, c, 1).reshape(8 * portion, -1)
    got = swap(pick(rows, 1 - c, 1).reshape(8 * portion, -1))
    both = jnp.where(c == 0, jnp.concatenate([kept, got], 1), jnp.concatenate([got, kept], 1))
    occ = pick(occ_energy.reshape(8, 2, portion), c, 1).reshape(1, -1)
    along = lax.all_gather(both, "x", axis=0)

    other, along, up, down, occ, slab_energy = after((other, along, up, down, occ, slab_energy))
    others = near(other, "z")
    panels = near(along, Y)
    two = far(up, down, "z")
    here = jnp.stack([mine, up, down, jnp.concatenate(two)])
    others, panels, here, slab_energy, occ = after((others, panels, here, slab_energy, occ))
    occ_other = shift(occ, "yh", 1, 2)
    other2, slab_other = swap(other), swap(slab_energy)
    others = others + far(*others, "z")
    panels = (along,) + panels + far(*panels, Y)
    energy = jnp.where(yh == 0, jnp.concatenate([occ, occ_other]), jnp.concatenate([occ_other, occ]))
    energy = energy.reshape(-1, 1)

    def pair(slab):
        pairs = (slab[:, None] + virt_energy[None, :]).reshape(2, columns)
        return pick(pairs, yh, 0).reshape(1, -1)

    pairs, pairs2 = pair(slab_energy), pair(slab_other)
    others, here, panels, energy, pairs, pairs2, other2 = after(
        (others, here, panels, energy, pairs, pairs2, other2)
    )
    there = (swap(here), other2) + tuple(swap(value) for value in others)
    update = product(panels, (here, other) + others, energy, pairs)
    update = product(panels, there, energy, pairs2, update)
    return place(lax.all_to_all(update.reshape(CHIPS, portion, -1), PLANE, 0, 0, tiled=True))


def solution(mesh):
    fine = Mesh(mesh.devices.reshape(SIZES), AXES)
    split = P(("z", "yh"), ("x", "yl", "c"))
    return jax.shard_map(
        local,
        mesh=fine,
        in_specs=(split, split, P(("z", "yh")), P(("x", "yl", "c")), P()),
        out_specs=P(AXES, None),
        check_vma=False,
    )
```

time: 222 us -> 216 us (0.973)
  waiting for transfers between devices: 46.6 us -> 34 us
  starting transfers between devices: 28.8 us -> 36.8 us
  local copies, waits for them, and re-layouts: 7.98 us -> 11 us
    ppermute x19 -> x22, waiting for transfers between devices: 46.6 us -> 34 us  [shift(): lax.ppermute(value, axis, [((i + step) % size, i) for i in range(size)])]
    ppermute x19 -> x22, starting transfers between devices: 28.8 us -> 36.8 us  [shift(): lax.ppermute(value, axis, [((i + step) % size, i) for i in range(size)])]
    slice x2 -> x6, local copies, waits for them, and re-layouts: 2.91 us -> 6.41 us  [far(): return (shift(up[:cut], axis, 1, 4), shift(down[cut:], axis, 3, 4))]
    pallas_call x1, Pallas kernels: 5.8 us -> 3.08 us  [place(): pl.pallas_call(functools.partial(place_kernel, width // 2), out_shape=jax...]
  transfers between devices with their start and end apart: 19 -> 22, of which waited for: 7 -> 12; matrix products, arithmetic and copies ran while one was open for 5% -> 6% of each run, Pallas kernels for 7% -> 7%
where the time goes in v4:
time: 216 us
  blocking collectives  96.2 us (45%)
  starting transfers between devices  36.8 us (17%)
  waiting for transfers between devices  34 us (16%)
  Pallas kernels  33.1 us (15%)
  local copies, waits for them, and re-layouts  11 us (5%)
  other arithmetic  4.12 us (2%)
    all_to_all x1, blocking collectives, local(): lax.all_to_all(update.reshape(CHIPS, portion, -1), PLANE, 0, 0, tiled=True)  83.3 us
    ppermute x22, starting transfers between devices, shift(): lax.ppermute(value, axis, [((i + step) % size, i) for i in range(size)])  36.8 us
    ppermute x22, waiting for transfers between devices, shift(): lax.ppermute(value, axis, [((i + step) % size, i) for i in range(size)])  34 us
    pallas_call x2, Pallas kernels, product(): pl.pallas_call(functools.partial(product_kernel, at_column), out_shape=ja...  30 us
    all_gather x1, blocking collectives, local(): along = lax.all_gather(both, 'x', axis=0)  13 us
    slice x6, local copies, waits for them, and re-layouts, far(): return (shift(up[:cut], axis, 1, 4), shift(down[cut:], axis, 3, 4))  6.41 us
  transfers between devices with their start and end apart: 22, of which 12 were waited for; matrix products, arithmetic and copies ran while one was open for 6% of the time, Pallas kernels for 7%

profile of v4, /device:TPU:1, one launch (start us, length us, event | category | flops | bytes accessed | tf_op | source)
XLA Modules:
  0.0 215.6 jit_solution(456538671658201154)
XLA Ops:
  0.0 2.6 %constant_dynamic-slice_fusion = (bf16[256,1920]{1,0:T(8,128)(2,1)S(1)}, bf16[256,1920]{1,0:T(8,128)(2,1)}) fusion(bf16[256,3840]{1,0:T(8,128)(2,1)} %param.6, s32[]{:T(128)S(6)} %select_n.58, s32[]{:T(128)S(6)} %select_n.53), kind=kLoop, calls=%fused_computation.7 | loop fusion | bytes 3932168 | tf_op jit(solution)/shard_map/dynamic_slice | solution.py:157
  2.6 4.6 %collective-permute-start.2 = (bf16[256,1920]{1,0:T(8,128)(2,1)S(1)}, bf16[256,1920]{1,0:T(8,128)(2,1)S(1)}, u32[]{:S(2)}, u32[]{:S(2)}) collective-permute-start(bf16[256,1920]{1,0:T(8,128)(2,1)S(1)} %get-tuple-element.59), channel_id=1, source_target_pairs={{32,0},{64,32},{96,64},{0,96},{33,1},{65,33},{97,65},{1,97},{34,2}... | collective-permute-start | bytes 2949128 | tf_op jit(solution)/shard_map/ppermute | solution.py:25
  7.2 2.9 %collective-permute-start = (bf16[256,1920]{1,0:T(8,128)(2,1)}, bf16[256,1920]{1,0:T(8,128)(2,1)}, u32[]{:S(2)}, u32[]{:S(2)}) collective-permute-start(bf16[256,1920]{1,0:T(8,128)(2,1)} %get-tuple-element.60), channel_id=1, source_target_pairs={{16,0},{0,16},{17,1},{1,17},{18,2},{2,18},{19,3},{3,19},{20,4},{4,... | collective-permute-start | bytes 2949128 | tf_op jit(solution)/shard_map/ppermute | solution.py:25
  10.2 1.3 collective-permute-start.1
  12.5 13.0 %all_gather.4.refs_0_ = bf16[4,448,256]{2,1,0:T(8,128)(2,1)S(1)} all-gather(bf16[1,448,256]{2,1,0:T(8,128)(2,1)S(1)} %maximum_select_fusion), channel_id=1, replica_groups=mesh['z'=4,'yh'=2,'x'=4,'yl'=2,'c'=2] {'x'}, dimensions={0}, use_global_device_ids=true | all-gather | bytes 1146880 | tf_op jit(solution)/shard_map/all_gather | solution.py:170
  25.5 2.2 collective-permute-done.2
  27.6 3.2 %collective-permute-done.3 = bf16[256,1920]{1,0:T(8,128)(2,1)} collective-permute-done((bf16[256,1920]{1,0:T(8,128)(2,1)S(1)}, bf16[256,1920]{1,0:T(8,128)(2,1)}, u32[]{:S(2)}, u32[]{:S(2)}) %collective-permute-start.3) | collective-permute-done | bytes 983072 | tf_op jit(solution)/shard_map/ppermute | solution.py:25
  31.4 2.4 %collective-permute-start.8 = (bf16[128,1920]{1,0:T(8,128)(2,1)S(1)}, bf16[128,1920]{1,0:T(8,128)(2,1)S(1)}, u32[]{:S(2)}, u32[]{:S(2)}) collective-permute-start(bf16[128,1920]{1,0:T(8,128)(2,1)S(1)} %slice.18), channel_id=1, source_target_pairs={{32,0},{64,32},{96,64},{0,96},{33,1},{65,33},{97,65},{1,97},{34,2}... | collective-permute-start | bytes 1474568 | tf_op jit(solution)/shard_map/ppermute | solution.py:25
  33.8 1.1 slice.19
  35.0 2.7 %collective-permute-start.4 = (bf16[256,1920]{1,0:T(8,128)(2,1)}, bf16[256,1920]{1,0:T(8,128)(2,1)}, u32[]{:S(2)}, u32[]{:S(2)}) collective-permute-start(bf16[256,1920]{1,0:T(8,128)(2,1)} %collective-permute-done.refs_6_), channel_id=1, source_target_pairs={{32,0},{64,32},{96,64},{0,96},{33,1},{65,33},{97,65},{1,97},{34,2}... | collective-permute-start | bytes 2949128 | tf_op jit(solution)/shard_map/ppermute | solution.py:25
  37.7 2.7 %collective-permute-start.6 = (bf16[4,448,256]{2,1,0:T(8,128)(2,1)S(1)}, bf16[4,448,256]{2,1,0:T(8,128)(2,1)S(1)}, u32[]{:S(2)}, u32[]{:S(2)}) collective-permute-start(bf16[4,448,256]{2,1,0:T(8,128)(2,1)S(1)} %all_gather.4.refs_0_), channel_id=1, source_target_pairs={{2,0},{16,2},{18,16},{0,18},{3,1},{17,3},{19,17},{1,19},{6,4},{20,... | collective-permute-start | bytes 2752520 | tf_op jit(solution)/shard_map/ppermute | solution.py:25
  40.4 1.9 collective-permute-done.8
  42.3 1.3 collective-permute-start.7
  43.6 2.9 %collective-permute-done.9 = bf16[128,1920]{1,0:T(8,128)(2,1)S(1)} collective-permute-done((bf16[128,1920]{1,0:T(8,128)(2,1)S(1)}, bf16[128,1920]{1,0:T(8,128)(2,1)S(1)}, u32[]{:S(2)}, u32[]{:S(2)}) %collective-permute-start.9) | collective-permute-done | bytes 491552 | tf_op jit(solution)/shard_map/ppermute | solution.py:25
  46.5 6.3 %collective-permute-start.16 = (bf16[256,1920]{1,0:T(8,128)(2,1)}, bf16[256,1920]{1,0:T(8,128)(2,1)}, u32[]{:S(2)}, u32[]{:S(2)}) collective-permute-start(bf16[256,1920]{1,0:T(8,128)(2,1)} %collective-permute-done.refs_6_), channel_id=1, source_target_pairs={{1,0},{0,1},{3,2},{2,3},{5,4},{4,5},{7,6},{6,7},{9,8},{8,9},{11,10... | collective-permute-start | bytes 2949128 | tf_op jit(solution)/shard_map/ppermute | solution.py:25
  52.9 3.3 %pad_maximum_fusion.refs_5_ = bf16[4,256,1920]{2,1,0:T(8,128)(2,1)} fusion(bf16[1,256,1920]{2,1,0:T(8,128)(2,1)S(1)} %maximum_bitcast_fusion, bf16[1,256,1920]{2,1,0:T(8,128)(2,1)} %bitcast.6, bf16[1,256,1920]{2,1,0:T(8,128)(2,1)} %bitcast.16, bf16[1,256,1920]{2,1,0:T(8,128)(2,1)S(1)} %bitcast.15), kind=kLoop, calls=%fused_computation | loop fusion | flops 5898240 | bytes 7864320 | tf_op jit(solution)/shard_map/stack | solution.py:176
  57.0 2.9 %collective-permute-done.7.refs_2_ = bf16[4,448,256]{2,1,0:T(8,128)(2,1)S(1)} collective-permute-done((bf16[4,448,256]{2,1,0:T(8,128)(2,1)S(1)}, bf16[4,448,256]{2,1,0:T(8,128)(2,1)S(1)}, u32[]{:S(2)}, u32[]{:S(2)}) %collective-permute-start.7) | collective-permute-done | bytes 917536 | tf_op jit(solution)/shard_map/ppermute | solution.py:25
  59.9 3.5 %collective-permute-done.4.refs_7_ = bf16[256,1920]{1,0:T(8,128)(2,1)} collective-permute-done((bf16[256,1920]{1,0:T(8,128)(2,1)}, bf16[256,1920]{1,0:T(8,128)(2,1)}, u32[]{:S(2)}, u32[]{:S(2)}) %collective-permute-start.4) | collective-permute-done | bytes 983072 | tf_op jit(solution)/shard_map/ppermute | solution.py:25
  63.5 4.1 %collective-permute-done.5.refs_8_ = bf16[256,1920]{1,0:T(8,128)(2,1)} collective-permute-done((bf16[256,1920]{1,0:T(8,128)(2,1)}, bf16[256,1920]{1,0:T(8,128)(2,1)}, u32[]{:S(2)}, u32[]{:S(2)}) %collective-permute-start.5) | collective-permute-done | bytes 983072 | tf_op jit(solution)/shard_map/ppermute | solution.py:25
  67.6 2.9 %collective-permute-start.14 = (f32[1,448]{1,0:T(1,128)S(1)}, f32[1,448]{1,0:T(1,128)S(1)}, u32[]{:S(2)}, u32[]{:S(2)}) collective-permute-start(f32[1,448]{1,0:T(1,128)S(1)} %reshape.114), channel_id=1, source_target_pairs={{16,0},{0,16},{17,1},{1,17},{18,2},{2,18},{19,3},{3,19},{20,4},{4,... | collective-permute-start | bytes 5384 | tf_op jit(solution)/shard_map/ppermute | solution.py:25
  70.6 3.7 %collective-permute-start.15 = (f32[4]{0:T(128)S(1)}, f32[4]{0:T(128)S(1)}, u32[]{:S(2)}, u32[]{:S(2)}) collective-permute-start(f32[4]{0:T(128)S(1)} %copy-done.10), channel_id=1, source_target_pairs={{1,0},{0,1},{3,2},{2,3},{5,4},{4,5},{7,6},{6,7},{9,8},{8,9},{11,10... | collective-permute-start | bytes 56 | tf_op jit(solution)/shard_map/ppermute | solution.py:25
  74.6 1.8 slice.20
  76.4 1.8 slice.21
  78.2 1.5 collective-permute-start.11
  83.9 9.2 %collective-permute-done.12.refs_3_ = bf16[2,448,256]{2,1,0:T(8,128)(2,1)S(1)} collective-permute-done((bf16[2,448,256]{2,1,0:T(8,128)(2,1)}, bf16[2,448,256]{2,1,0:T(8,128)(2,1)S(1)}, u32[]{:S(2)}, u32[]{:S(2)}) %collective-permute-start.12) | collective-permute-done | bytes 458784 | tf_op jit(solution)/shard_map/ppermute | solution.py:25
  93.1 2.0 collective-permute-done.13.refs_4_
  95.1 1.8 collective-permute-start.17
  97.9 1.0 copy.16.refs_11_
  98.9 15.0 %product.2.refs_13_ = bf16[896,3840]{1,0:T(8,128)(2,1)} custom-call(bf16[4,448,256]{2,1,0:T(8,128)(2,1)} %copy-done, bf16[4,448,256]{2,1,0:T(8,128)(2,1)} %copy-done.1, bf16[4,448,256]{2,1,0:T(8,128)(2,1)} %copy-done.2, bf16[2,448,256]{2,1,0:T(8,128)(2,1)} %copy-done.4, bf16[2,448,256]{2,1,0:T(8,128)(2,1)} %copy-done.5, ...), custom_call_target="tpu_custom_call" | custom-call | flops 1000000 | bytes 65536 | tf_op jit(solution)/shard_map/product/pallas_call | solution.py:98
  114.0 15.0 %product.3 = bf16[896,3840]{1,0:T(8,128)(2,1)} custom-call(bf16[4,448,256]{2,1,0:T(8,128)(2,1)} %copy-done, bf16[4,448,256]{2,1,0:T(8,128)(2,1)} %copy-done.1, bf16[4,448,256]{2,1,0:T(8,128)(2,1)} %copy-done.2, bf16[2,448,256]{2,1,0:T(8,128)(2,1)} %copy-done.4, bf16[2,448,256]{2,1,0:T(8,128)(2,1)} %copy-done.5, ...), custom_call_target="tpu_custom_call", output_to_operand_aliasing={{}: (13, {})} | custom-call | flops 1000000 | bytes 65536 | tf_op jit(solution)/shard_map/product/pallas_call | solution.py:98
  129.0 83.3 %all_to_all.5.piece = bf16[16,56,3840]{2,1,0:T(8,128)(2,1)S(1)} all-to-all(bf16[16,56,3840]{2,1,0:T(8,128)(2,1)} %bitcast.14), channel_id=1, replica_groups=mesh['z'=4,'yh'=2,'x'=4,'yl'=2,'c'=2] {'yh','x','yl'}, dimensions={0} | all-to-all | bytes 13762560 | tf_op jit(solution)/shard_map/all_to_all | solution.py:196
  212.3 3.1 %place.1 = bf16[56,61440]{1,0:T(8,128)(2,1)} custom-call(bf16[16,56,3840]{2,1,0:T(8,128)(2,1)S(1)} %all_to_all.5.piece), custom_call_target="tpu_custom_call" | custom-call | flops 1000000 | bytes 65536 | tf_op jit(solution)/shard_map/place/pallas_call | solution.py:135
  (65 shorter events, 8.1 us)
Async XLA Ops:
  0.0 10.1 %copy-start.7 = (bf16[896,128]{1,0:T(8,128)(2,1)S(1)}, bf16[896,128]{1,0:T(8,128)(2,1)}, u32[]{:S(2)}) copy-start(bf16[896,128]{1,0:T(8,128)(2,1)} %param.5) | copy-start | bytes 688132
  0.0 11.5 %copy-start.8 = (f32[896]{0:T(1024)S(1)}, f32[896]{0:T(1024)}, u32[]{:S(2)}) copy-start(f32[896]{0:T(1024)} %param.7) | copy-start | bytes 10756
  2.6 25.0 %collective-permute-start.2 = (bf16[256,1920]{1,0:T(8,128)(2,1)S(1)}, bf16[256,1920]{1,0:T(8,128)(2,1)S(1)}, u32[]{:S(2)}, u32[]{:S(2)}) collective-permute-start(bf16[256,1920]{1,0:T(8,128)(2,1)S(1)} %get-tuple-element.59), channel_id=1, source_target_pairs={{32,0},{64,32},{96,64},{0,96},{33,1},{65,33},{97,65},{1,97},{34,2}... | collective-permute-start | bytes 2949128 | tf_op jit(solution)/shard_map/ppermute | solution.py:25
  7.2 23.6 %collective-permute-start.3 = (bf16[256,1920]{1,0:T(8,128)(2,1)S(1)}, bf16[256,1920]{1,0:T(8,128)(2,1)}, u32[]{:S(2)}, u32[]{:S(2)}) collective-permute-start(bf16[256,1920]{1,0:T(8,128)(2,1)S(1)} %get-tuple-element.59), channel_id=1, source_target_pairs={{96,0},{0,32},{32,64},{64,96},{97,1},{1,33},{33,65},{65,97},{98,2}... | collective-permute-start | bytes 2949128 | tf_op jit(solution)/shard_map/ppermute | solution.py:25
  7.2 24.1 %collective-permute-start = (bf16[256,1920]{1,0:T(8,128)(2,1)}, bf16[256,1920]{1,0:T(8,128)(2,1)}, u32[]{:S(2)}, u32[]{:S(2)}) collective-permute-start(bf16[256,1920]{1,0:T(8,128)(2,1)} %get-tuple-element.60), channel_id=1, source_target_pairs={{16,0},{0,16},{17,1},{1,17},{18,2},{2,18},{19,3},{3,19},{20,4},{4,... | collective-permute-start | bytes 2949128 | tf_op jit(solution)/shard_map/ppermute | solution.py:25
  10.2 2.3 %collective-permute-start.1 = (bf16[448,128]{1,0:T(8,128)(2,1)S(1)}, bf16[448,128]{1,0:T(8,128)(2,1)S(1)}, u32[]{:S(2)}, u32[]{:S(2)}) collective-permute-start(bf16[448,128]{1,0:T(8,128)(2,1)S(1)} %bitcast.19), channel_id=1, source_target_pairs={{1,0},{0,1},{3,2},{2,3},{5,4},{4,5},{7,6},{6,7},{9,8},{8,9},{11,10... | collective-permute-start | bytes 344072 | tf_op jit(solution)/shard_map/ppermute | solution.py:25
  25.5 30.7 %copy-start = (bf16[4,448,256]{2,1,0:T(8,128)(2,1)}, bf16[4,448,256]{2,1,0:T(8,128)(2,1)S(1)}, u32[]{:S(2)}) copy-start(bf16[4,448,256]{2,1,0:T(8,128)(2,1)S(1)} %all_gather.4.refs_0_) | copy-start | bytes 2752516
  27.6 10.0 %copy-start.3 = (bf16[256,1920]{1,0:T(8,128)(2,1)}, bf16[256,1920]{1,0:T(8,128)(2,1)S(1)}, u32[]{:S(2)}) copy-start(bf16[256,1920]{1,0:T(8,128)(2,1)S(1)} %collective-permute-done.2) | copy-start | bytes 2949124
  31.4 10.9 %collective-permute-start.8 = (bf16[128,1920]{1,0:T(8,128)(2,1)S(1)}, bf16[128,1920]{1,0:T(8,128)(2,1)S(1)}, u32[]{:S(2)}, u32[]{:S(2)}) collective-permute-start(bf16[128,1920]{1,0:T(8,128)(2,1)S(1)} %slice.18), channel_id=1, source_target_pairs={{32,0},{64,32},{96,64},{0,96},{33,1},{65,33},{97,65},{1,97},{34,2}... | collective-permute-start | bytes 1474568 | tf_op jit(solution)/shard_map/ppermute | solution.py:25
  34.9 11.6 %collective-permute-start.9 = (bf16[128,1920]{1,0:T(8,128)(2,1)S(1)}, bf16[128,1920]{1,0:T(8,128)(2,1)S(1)}, u32[]{:S(2)}, u32[]{:S(2)}) collective-permute-start(bf16[128,1920]{1,0:T(8,128)(2,1)S(1)} %slice.19), channel_id=1, source_target_pairs={{96,0},{0,32},{32,64},{64,96},{97,1},{1,33},{33,65},{65,97},{98,2}... | collective-permute-start | bytes 1474568 | tf_op jit(solution)/shard_map/ppermute | solution.py:25
  35.0 28.5 %collective-permute-start.4 = (bf16[256,1920]{1,0:T(8,128)(2,1)}, bf16[256,1920]{1,0:T(8,128)(2,1)}, u32[]{:S(2)}, u32[]{:S(2)}) collective-permute-start(bf16[256,1920]{1,0:T(8,128)(2,1)} %collective-permute-done.refs_6_), channel_id=1, source_target_pairs={{32,0},{64,32},{96,64},{0,96},{33,1},{65,33},{97,65},{1,97},{34,2}... | collective-permute-start | bytes 2949128 | tf_op jit(solution)/shard_map/ppermute | solution.py:25
  37.7 30.0 %collective-permute-start.5 = (bf16[256,1920]{1,0:T(8,128)(2,1)}, bf16[256,1920]{1,0:T(8,128)(2,1)}, u32[]{:S(2)}, u32[]{:S(2)}) collective-permute-start(bf16[256,1920]{1,0:T(8,128)(2,1)} %collective-permute-done.refs_6_), channel_id=1, source_target_pairs={{96,0},{0,32},{32,64},{64,96},{97,1},{1,33},{33,65},{65,97},{98,2}... | collective-permute-start | bytes 2949128 | tf_op jit(solution)/shard_map/ppermute | solution.py:25
  37.7 19.4 %collective-permute-start.6 = (bf16[4,448,256]{2,1,0:T(8,128)(2,1)S(1)}, bf16[4,448,256]{2,1,0:T(8,128)(2,1)S(1)}, u32[]{:S(2)}, u32[]{:S(2)}) collective-permute-start(bf16[4,448,256]{2,1,0:T(8,128)(2,1)S(1)} %all_gather.4.refs_0_), channel_id=1, source_target_pairs={{2,0},{16,2},{18,16},{0,18},{3,1},{17,3},{19,17},{1,19},{6,4},{20,... | collective-permute-start | bytes 2752520 | tf_op jit(solution)/shard_map/ppermute | solution.py:25
  42.3 17.6 %collective-permute-start.7 = (bf16[4,448,256]{2,1,0:T(8,128)(2,1)S(1)}, bf16[4,448,256]{2,1,0:T(8,128)(2,1)S(1)}, u32[]{:S(2)}, u32[]{:S(2)}) collective-permute-start(bf16[4,448,256]{2,1,0:T(8,128)(2,1)S(1)} %all_gather.4.refs_0_), channel_id=1, source_target_pairs={{18,0},{0,2},{2,16},{16,18},{19,1},{1,3},{3,17},{17,19},{22,4},{4,... | collective-permute-start | bytes 2752520 | tf_op jit(solution)/shard_map/ppermute | solution.py:25
  46.5 37.4 %collective-permute-start.16 = (bf16[256,1920]{1,0:T(8,128)(2,1)}, bf16[256,1920]{1,0:T(8,128)(2,1)}, u32[]{:S(2)}, u32[]{:S(2)}) collective-permute-start(bf16[256,1920]{1,0:T(8,128)(2,1)} %collective-permute-done.refs_6_), channel_id=1, source_target_pairs={{1,0},{0,1},{3,2},{2,3},{5,4},{4,5},{7,6},{6,7},{9,8},{8,9},{11,10... | collective-permute-start | bytes 2949128 | tf_op jit(solution)/shard_map/ppermute | solution.py:25
  52.9 17.7 %copy-start.9 = (f32[960]{0:T(1024)S(1)}, f32[960]{0:T(1024)}, u32[]{:S(2)}) copy-start(f32[960]{0:T(1024)} %param.9) | copy-start | bytes 11524
  52.9 17.8 %copy-start.10 = (f32[4]{0:T(128)S(1)}, f32[4]{0:T(128)}, u32[]{:S(2)}) copy-start(f32[4]{0:T(128)} %param.8) | copy-start | bytes 52
  57.0 41.9 %copy-start.1 = (bf16[4,448,256]{2,1,0:T(8,128)(2,1)}, bf16[4,448,256]{2,1,0:T(8,128)(2,1)S(1)}, u32[]{:S(2)}) copy-start(bf16[4,448,256]{2,1,0:T(8,128)(2,1)S(1)} %collective-permute-done.6.refs_1_) | copy-start | bytes 2752516
  59.9 39.0 %copy-start.2 = (bf16[4,448,256]{2,1,0:T(8,128)(2,1)}, bf16[4,448,256]{2,1,0:T(8,128)(2,1)S(1)}, u32[]{:S(2)}) copy-start(bf16[4,448,256]{2,1,0:T(8,128)(2,1)S(1)} %collective-permute-done.7.refs_2_) | copy-start | bytes 2752516
  67.6 14.7 %collective-permute-start.14 = (f32[1,448]{1,0:T(1,128)S(1)}, f32[1,448]{1,0:T(1,128)S(1)}, u32[]{:S(2)}, u32[]{:S(2)}) collective-permute-start(f32[1,448]{1,0:T(1,128)S(1)} %reshape.114), channel_id=1, source_target_pairs={{16,0},{0,16},{17,1},{1,17},{18,2},{2,18},{19,3},{3,19},{20,4},{4,... | collective-permute-start | bytes 5384 | tf_op jit(solution)/shard_map/ppermute | solution.py:25
  70.6 10.7 %collective-permute-start.15 = (f32[4]{0:T(128)S(1)}, f32[4]{0:T(128)S(1)}, u32[]{:S(2)}, u32[]{:S(2)}) collective-permute-start(f32[4]{0:T(128)S(1)} %copy-done.10), channel_id=1, source_target_pairs={{1,0},{0,1},{3,2},{2,3},{5,4},{4,5},{7,6},{6,7},{9,8},{8,9},{11,10... | collective-permute-start | bytes 56 | tf_op jit(solution)/shard_map/ppermute | solution.py:25
  76.4 18.7 %collective-permute-start.10 = (bf16[128,1920]{1,0:T(8,128)(2,1)}, bf16[128,1920]{1,0:T(8,128)(2,1)S(1)}, u32[]{:S(2)}, u32[]{:S(2)}) collective-permute-start(bf16[128,1920]{1,0:T(8,128)(2,1)} %slice.20), channel_id=1, source_target_pairs={{32,0},{64,32},{96,64},{0,96},{33,1},{65,33},{97,65},{1,97},{34,2}... | collective-permute-start | bytes 1474568 | tf_op jit(solution)/shard_map/ppermute | solution.py:25
  78.2 16.8 %collective-permute-start.11 = (bf16[128,1920]{1,0:T(8,128)(2,1)}, bf16[128,1920]{1,0:T(8,128)(2,1)}, u32[]{:S(2)}, u32[]{:S(2)}) collective-permute-start(bf16[128,1920]{1,0:T(8,128)(2,1)} %slice.21), channel_id=1, source_target_pairs={{96,0},{0,32},{32,64},{64,96},{97,1},{1,33},{33,65},{65,97},{98,2}... | collective-permute-start | bytes 1474568 | tf_op jit(solution)/shard_map/ppermute | solution.py:25
  81.3 11.7 %collective-permute-start.12 = (bf16[2,448,256]{2,1,0:T(8,128)(2,1)}, bf16[2,448,256]{2,1,0:T(8,128)(2,1)S(1)}, u32[]{:S(2)}, u32[]{:S(2)}) collective-permute-start(bf16[2,448,256]{2,1,0:T(8,128)(2,1)} %slice.22), channel_id=1, source_target_pairs={{2,0},{16,2},{18,16},{0,18},{3,1},{17,3},{19,17},{1,19},{6,4},{20,... | collective-permute-start | bytes 1376264 | tf_op jit(solution)/shard_map/ppermute | solution.py:25
  82.4 12.7 %collective-permute-start.13 = (bf16[2,448,256]{2,1,0:T(8,128)(2,1)}, bf16[2,448,256]{2,1,0:T(8,128)(2,1)S(1)}, u32[]{:S(2)}, u32[]{:S(2)}) collective-permute-start(bf16[2,448,256]{2,1,0:T(8,128)(2,1)} %slice.23), channel_id=1, source_target_pairs={{18,0},{0,2},{2,16},{16,18},{19,1},{1,3},{3,17},{17,19},{22,4},{4,... | collective-permute-start | bytes 1376264 | tf_op jit(solution)/shard_map/ppermute | solution.py:25
  93.0 5.9 %copy-start.4 = (bf16[2,448,256]{2,1,0:T(8,128)(2,1)}, bf16[2,448,256]{2,1,0:T(8,128)(2,1)S(1)}, u32[]{:S(2)}) copy-start(bf16[2,448,256]{2,1,0:T(8,128)(2,1)S(1)} %collective-permute-done.12.refs_3_) | copy-start | bytes 1376260
  95.0 3.9 %copy-start.5 = (bf16[2,448,256]{2,1,0:T(8,128)(2,1)}, bf16[2,448,256]{2,1,0:T(8,128)(2,1)S(1)}, u32[]{:S(2)}) copy-start(bf16[2,448,256]{2,1,0:T(8,128)(2,1)S(1)} %collective-permute-done.13.refs_4_) | copy-start | bytes 1376260
  95.1 18.9 %collective-permute-start.17 = (bf16[4,256,1920]{2,1,0:T(8,128)(2,1)}, bf16[4,256,1920]{2,1,0:T(8,128)(2,1)}, u32[]{:S(2)}, u32[]{:S(2)}) collective-permute-start(bf16[4,256,1920]{2,1,0:T(8,128)(2,1)} %pad_maximum_fusion.refs_5_), channel_id=1, source_target_pairs={{1,0},{0,1},{3,2},{2,3},{5,4},{4,5},{7,6},{6,7},{9,8},{8,9},{11,10... | collective-permute-start | bytes 11796488 | tf_op jit(solution)/shard_map/ppermute | solution.py:25
  96.9 17.1 %collective-permute-start.18 = (bf16[256,1920]{1,0:T(8,128)(2,1)}, bf16[256,1920]{1,0:T(8,128)(2,1)}, u32[]{:S(2)}, u32[]{:S(2)}) collective-permute-start(bf16[256,1920]{1,0:T(8,128)(2,1)} %collective-permute-done.4.refs_7_), channel_id=1, source_target_pairs={{1,0},{0,1},{3,2},{2,3},{5,4},{4,5},{7,6},{6,7},{9,8},{8,9},{11,10... | collective-permute-start | bytes 2949128 | tf_op jit(solution)/shard_map/ppermute | solution.py:25
  97.0 17.0 %collective-permute-start.19 = (bf16[256,1920]{1,0:T(8,128)(2,1)}, bf16[256,1920]{1,0:T(8,128)(2,1)}, u32[]{:S(2)}, u32[]{:S(2)}) collective-permute-start(bf16[256,1920]{1,0:T(8,128)(2,1)} %collective-permute-done.5.refs_8_), channel_id=1, source_target_pairs={{1,0},{0,1},{3,2},{2,3},{5,4},{4,5},{7,6},{6,7},{9,8},{8,9},{11,10... | collective-permute-start | bytes 2949128 | tf_op jit(solution)/shard_map/ppermute | solution.py:25
  97.4 16.5 %collective-permute-start.20 = (bf16[128,1920]{1,0:T(8,128)(2,1)S(1)}, bf16[128,1920]{1,0:T(8,128)(2,1)}, u32[]{:S(2)}, u32[]{:S(2)}) collective-permute-start(bf16[128,1920]{1,0:T(8,128)(2,1)S(1)} %collective-permute-done.10.refs_9_), channel_id=1, source_target_pairs={{1,0},{0,1},{3,2},{2,3},{5,4},{4,5},{7,6},{6,7},{9,8},{8,9},{11,10... | collective-permute-start | bytes 1474568 | tf_op jit(solution)/shard_map/ppermute | solution.py:25
  97.5 16.5 %collective-permute-start.21 = (bf16[128,1920]{1,0:T(8,128)(2,1)}, bf16[128,1920]{1,0:T(8,128)(2,1)}, u32[]{:S(2)}, u32[]{:S(2)}) collective-permute-start(bf16[128,1920]{1,0:T(8,128)(2,1)} %collective-permute-done.11.refs_10_), channel_id=1, source_target_pairs={{1,0},{0,1},{3,2},{2,3},{5,4},{4,5},{7,6},{6,7},{9,8},{8,9},{11,10... | collective-permute-start | bytes 1474568 | tf_op jit(solution)/shard_map/ppermute | solution.py:25
  (1 other events, 3.9 us)

commit v5 on v4

--- a/solution.py
+++ b/solution.py
@@ -174,7 +174,7 @@
     panels = near(along, Y)
     two = far(up, down, "z")
     here = jnp.stack([mine, up, down, jnp.concatenate(two)])
-    others, panels, here, slab_energy, occ = after((others, panels, here, slab_energy, occ))
+    panels, slab_energy, occ = after((panels, slab_energy, occ))
     occ_other = shift(occ, "yh", 1, 2)
     other2, slab_other = swap(other), swap(slab_energy)
     others = others + far(*others, "z")

time: 216 us -> 210 us (0.972)
  waiting for transfers between devices: 34 us -> 24.1 us
  blocking collectives: 96.2 us -> 98.6 us
    ppermute x22, waiting for transfers between devices: 34 us -> 24.1 us  [shift(): lax.ppermute(value, axis, [((i + step) % size, i) for i in range(size)])]
    unnamed x22 -> x32, local copies, waits for them, and re-layouts: 0.05 us -> 2.88 us
    slice x6, local copies, waits for them, and re-layouts: 6.41 us -> 4.06 us  [far(): return (shift(up[:cut], axis, 1, 4), shift(down[cut:], axis, 3, 4))]
    all_to_all x1, blocking collectives: 83.3 us -> 85.6 us  [local(): lax.all_to_all(update.reshape(CHIPS, portion, -1), PLANE, 0, 0, tiled=True)]
  transfers between devices with their start and end apart: 22 -> 22, of which waited for: 12 -> 10; matrix products, arithmetic and copies ran while one was open for 6% -> 5% of each run, Pallas kernels for 7% -> 7%
where the time goes in v5:
time: 210 us; the launch traced here: 209 us
  blocking collectives  98.6 us (47%)
  starting transfers between devices  36.1 us (17%)
  Pallas kernels  33.1 us (16%)
  waiting for transfers between devices  24.1 us (11%)
  local copies, waits for them, and re-layouts  11.5 us (5%)
  other arithmetic  5.46 us (3%)
    all_to_all x1, blocking collectives, local(): lax.all_to_all(update.reshape(CHIPS, portion, -1), PLANE, 0, 0, tiled=True)  85.6 us
    ppermute x22, starting transfers between devices, shift(): lax.ppermute(value, axis, [((i + step) % size, i) for i in range(size)])  36.1 us
    pallas_call x2, Pallas kernels, product(): pl.pallas_call(functools.partial(product_kernel, at_column), out_shape=ja...  30 us
    ppermute x22, waiting for transfers between devices, shift(): lax.ppermute(value, axis, [((i + step) % size, i) for i in range(size)])  24.1 us
    all_gather x1, blocking collectives, local(): along = lax.all_gather(both, 'x', axis=0)  13 us
    another operation x2, other arithmetic, local(): here = jnp.stack([mine, up, down, jnp.concatenate(two)])  4.76 us
  transfers between devices with their start and end apart: 22, of which 10 were waited for; matrix products, arithmetic and copies ran while one was open for 5% of the time, Pallas kernels for 7%

profile of v5, /device:TPU:1, one launch (start us, length us, event | category | flops | bytes accessed | tf_op | source)
XLA Modules:
  0.0 209.2 jit_solution(2516100656760781395)
XLA Ops:
  0.0 2.6 %constant_dynamic-slice_fusion = (bf16[256,1920]{1,0:T(8,128)(2,1)S(1)}, bf16[256,1920]{1,0:T(8,128)(2,1)}) fusion(bf16[256,3840]{1,0:T(8,128)(2,1)} %param.6, s32[]{:T(128)S(6)} %select_n.58, s32[]{:T(128)S(6)} %select_n.53), kind=kLoop, calls=%fused_computation.7 | loop fusion | bytes 3932168 | tf_op jit(solution)/shard_map/dynamic_slice | solution.py:157
  2.6 4.6 %collective-permute-start.2 = (bf16[256,1920]{1,0:T(8,128)(2,1)S(1)}, bf16[256,1920]{1,0:T(8,128)(2,1)S(1)}, u32[]{:S(2)}, u32[]{:S(2)}) collective-permute-start(bf16[256,1920]{1,0:T(8,128)(2,1)S(1)} %get-tuple-element.53), channel_id=1, source_target_pairs={{32,0},{64,32},{96,64},{0,96},{33,1},{65,33},{97,65},{1,97},{34,2}... | collective-permute-start | bytes 2949128 | tf_op jit(solution)/shard_map/ppermute | solution.py:25
  7.2 2.9 %collective-permute-start = (bf16[256,1920]{1,0:T(8,128)(2,1)}, bf16[256,1920]{1,0:T(8,128)(2,1)}, u32[]{:S(2)}, u32[]{:S(2)}) collective-permute-start(bf16[256,1920]{1,0:T(8,128)(2,1)} %get-tuple-element.54), channel_id=1, source_target_pairs={{16,0},{0,16},{17,1},{1,17},{18,2},{2,18},{19,3},{3,19},{20,4},{4,... | collective-permute-start | bytes 2949128 | tf_op jit(solution)/shard_map/ppermute | solution.py:25
  10.2 1.3 collective-permute-start.1
  12.5 13.0 %all_gather.4.refs_0_ = bf16[4,448,256]{2,1,0:T(8,128)(2,1)S(1)} all-gather(bf16[1,448,256]{2,1,0:T(8,128)(2,1)S(1)} %maximum_select_fusion), channel_id=1, replica_groups=mesh['z'=4,'yh'=2,'x'=4,'yl'=2,'c'=2] {'x'}, dimensions={0}, use_global_device_ids=true | all-gather | bytes 1146880 | tf_op jit(solution)/shard_map/all_gather | solution.py:170
  25.5 2.2 %collective-permute-done.2 = bf16[256,1920]{1,0:T(8,128)(2,1)S(1)} collective-permute-done((bf16[256,1920]{1,0:T(8,128)(2,1)S(1)}, bf16[256,1920]{1,0:T(8,128)(2,1)S(1)}, u32[]{:S(2)}, u32[]{:S(2)}) %collective-permute-start.2) | collective-permute-done | bytes 983072 | tf_op jit(solution)/shard_map/ppermute | solution.py:25
  27.7 3.2 %collective-permute-done.3 = bf16[256,1920]{1,0:T(8,128)(2,1)} collective-permute-done((bf16[256,1920]{1,0:T(8,128)(2,1)S(1)}, bf16[256,1920]{1,0:T(8,128)(2,1)}, u32[]{:S(2)}, u32[]{:S(2)}) %collective-permute-start.3) | collective-permute-done | bytes 983072 | tf_op jit(solution)/shard_map/ppermute | solution.py:25
  31.4 2.4 %collective-permute-start.8 = (bf16[128,1920]{1,0:T(8,128)(2,1)S(1)}, bf16[128,1920]{1,0:T(8,128)(2,1)S(1)}, u32[]{:S(2)}, u32[]{:S(2)}) collective-permute-start(bf16[128,1920]{1,0:T(8,128)(2,1)S(1)} %slice.20), channel_id=1, source_target_pairs={{32,0},{64,32},{96,64},{0,96},{33,1},{65,33},{97,65},{1,97},{34,2}... | collective-permute-start | bytes 1474568 | tf_op jit(solution)/shard_map/ppermute | solution.py:25
  33.9 2.7 %collective-permute-start.10 = (bf16[4,448,256]{2,1,0:T(8,128)(2,1)S(1)}, bf16[4,448,256]{2,1,0:T(8,128)(2,1)S(1)}, u32[]{:S(2)}, u32[]{:S(2)}) collective-permute-start(bf16[4,448,256]{2,1,0:T(8,128)(2,1)S(1)} %all_gather.4.refs_0_), channel_id=1, source_target_pairs={{2,0},{16,2},{18,16},{0,18},{3,1},{17,3},{19,17},{1,19},{6,4},{20,... | collective-permute-start | bytes 2752520 | tf_op jit(solution)/shard_map/ppermute | solution.py:25
  36.6 1.1 slice.21
  37.7 2.7 %collective-permute-start.4 = (bf16[256,1920]{1,0:T(8,128)(2,1)}, bf16[256,1920]{1,0:T(8,128)(2,1)}, u32[]{:S(2)}, u32[]{:S(2)}) collective-permute-start(bf16[256,1920]{1,0:T(8,128)(2,1)} %collective-permute-done.refs_6_), channel_id=1, source_target_pairs={{32,0},{64,32},{96,64},{0,96},{33,1},{65,33},{97,65},{1,97},{34,2}... | collective-permute-start | bytes 2949128 | tf_op jit(solution)/shard_map/ppermute | solution.py:25
  40.4 1.9 collective-permute-done.8
  43.2 5.8 %collective-permute-done.9 = bf16[128,1920]{1,0:T(8,128)(2,1)} collective-permute-done((bf16[128,1920]{1,0:T(8,128)(2,1)S(1)}, bf16[128,1920]{1,0:T(8,128)(2,1)}, u32[]{:S(2)}, u32[]{:S(2)}) %collective-permute-start.9) | collective-permute-done | bytes 491552 | tf_op jit(solution)/shard_map/ppermute | solution.py:25
  49.0 6.9 %collective-permute-start.16 = (bf16[256,1920]{1,0:T(8,128)(2,1)}, bf16[256,1920]{1,0:T(8,128)(2,1)}, u32[]{:S(2)}, u32[]{:S(2)}) collective-permute-start(bf16[256,1920]{1,0:T(8,128)(2,1)} %collective-permute-done.refs_6_), channel_id=1, source_target_pairs={{1,0},{0,1},{3,2},{2,3},{5,4},{4,5},{7,6},{6,7},{9,8},{8,9},{11,10... | collective-permute-start | bytes 2949128 | tf_op jit(solution)/shard_map/ppermute | solution.py:25
  55.9 1.2 maximum_bitcast_fusion
  57.2 1.5 collective-permute-start.14
  58.7 3.5 %pad_maximum_fusion.refs_5_ = bf16[4,256,1920]{2,1,0:T(8,128)(2,1)} fusion(bf16[1,256,1920]{2,1,0:T(8,128)(2,1)S(1)} %maximum_bitcast_fusion, bf16[1,256,1920]{2,1,0:T(8,128)(2,1)} %bitcast.6, bf16[1,256,1920]{2,1,0:T(8,128)(2,1)} %bitcast.16, bf16[1,256,1920]{2,1,0:T(8,128)(2,1)} %bitcast.15), kind=kLoop, calls=%fused_computation | loop fusion | flops 5898240 | bytes 7864320 | tf_op jit(solution)/shard_map/stack | solution.py:176
  62.2 2.3 %collective-permute-start.15 = (f32[4]{0:T(128)S(1)}, f32[4]{0:T(128)S(1)}, u32[]{:S(2)}, u32[]{:S(2)}) collective-permute-start(f32[4]{0:T(128)S(1)} %copy-done.15), channel_id=1, source_target_pairs={{1,0},{0,1},{3,2},{2,3},{5,4},{4,5},{7,6},{6,7},{9,8},{8,9},{11,10... | collective-permute-start | bytes 56 | tf_op jit(solution)/shard_map/ppermute | solution.py:25
  65.6 1.2 collective-permute-start.12
  67.5 1.1 slice.24
  68.5 1.6 collective-permute-done.5.refs_8_
  70.1 1.1 slice.25
  71.2 1.5 collective-permute-start.7
  73.4 4.6 %collective-permute-done.12.refs_3_ = bf16[2,448,256]{2,1,0:T(8,128)(2,1)S(1)} collective-permute-done((bf16[2,448,256]{2,1,0:T(8,128)(2,1)}, bf16[2,448,256]{2,1,0:T(8,128)(2,1)S(1)}, u32[]{:S(2)}, u32[]{:S(2)}) %collective-permute-start.12) | collective-permute-done | bytes 458784 | tf_op jit(solution)/shard_map/ppermute | solution.py:25
  78.0 2.1 %collective-permute-done.13.refs_4_ = bf16[2,448,256]{2,1,0:T(8,128)(2,1)S(1)} collective-permute-done((bf16[2,448,256]{2,1,0:T(8,128)(2,1)S(1)}, bf16[2,448,256]{2,1,0:T(8,128)(2,1)S(1)}, u32[]{:S(2)}, u32[]{:S(2)}) %collective-permute-start.13) | collective-permute-done | bytes 458784 | tf_op jit(solution)/shard_map/ppermute | solution.py:25
  80.2 1.4 collective-permute-done.7.refs_10_
  82.3 4.6 %collective-permute-start.17 = (bf16[4,256,1920]{2,1,0:T(8,128)(2,1)}, bf16[4,256,1920]{2,1,0:T(8,128)(2,1)}, u32[]{:S(2)}, u32[]{:S(2)}) collective-permute-start(bf16[4,256,1920]{2,1,0:T(8,128)(2,1)} %pad_maximum_fusion.refs_5_), channel_id=1, source_target_pairs={{1,0},{0,1},{3,2},{2,3},{5,4},{4,5},{7,6},{6,7},{9,8},{8,9},{11,10... | collective-permute-start | bytes 11796488 | tf_op jit(solution)/shard_map/ppermute | solution.py:25
  87.9 1.0 copy.16.refs_11_
  88.9 15.0 %product.2.refs_13_ = bf16[896,3840]{1,0:T(8,128)(2,1)} custom-call(bf16[4,448,256]{2,1,0:T(8,128)(2,1)} %copy-done, bf16[4,448,256]{2,1,0:T(8,128)(2,1)} %copy-done.1, bf16[4,448,256]{2,1,0:T(8,128)(2,1)} %copy-done.2, bf16[2,448,256]{2,1,0:T(8,128)(2,1)} %copy-done.5, bf16[2,448,256]{2,1,0:T(8,128)(2,1)} %copy-done.6, ...), custom_call_target="tpu_custom_call" | custom-call | flops 1000000 | bytes 65536 | tf_op jit(solution)/shard_map/product/pallas_call | solution.py:98
  105.3 15.0 %product.3 = bf16[896,3840]{1,0:T(8,128)(2,1)} custom-call(bf16[4,448,256]{2,1,0:T(8,128)(2,1)} %copy-done, bf16[4,448,256]{2,1,0:T(8,128)(2,1)} %copy-done.1, bf16[4,448,256]{2,1,0:T(8,128)(2,1)} %copy-done.2, bf16[2,448,256]{2,1,0:T(8,128)(2,1)} %copy-done.5, bf16[2,448,256]{2,1,0:T(8,128)(2,1)} %copy-done.6, ...), custom_call_target="tpu_custom_call", output_to_operand_aliasing={{}: (13, {})} | custom-call | flops 1000000 | bytes 65536 | tf_op jit(solution)/shard_map/product/pallas_call | solution.py:98
  120.3 85.6 %all_to_all.5.piece = bf16[16,56,3840]{2,1,0:T(8,128)(2,1)S(1)} all-to-all(bf16[16,56,3840]{2,1,0:T(8,128)(2,1)} %bitcast.14), channel_id=1, replica_groups=mesh['z'=4,'yh'=2,'x'=4,'yl'=2,'c'=2] {'yh','x','yl'}, dimensions={0} | all-to-all | bytes 13762560 | tf_op jit(solution)/shard_map/all_to_all | solution.py:196
  205.9 3.1 %place.1 = bf16[56,61440]{1,0:T(8,128)(2,1)} custom-call(bf16[16,56,3840]{2,1,0:T(8,128)(2,1)S(1)} %all_to_all.5.piece), custom_call_target="tpu_custom_call" | custom-call | flops 1000000 | bytes 65536 | tf_op jit(solution)/shard_map/place/pallas_call | solution.py:135
  (75 shorter events, 8.1 us)
Async XLA Ops:
  0.0 10.2 %copy-start.12 = (bf16[896,128]{1,0:T(8,128)(2,1)S(1)}, bf16[896,128]{1,0:T(8,128)(2,1)}, u32[]{:S(2)}) copy-start(bf16[896,128]{1,0:T(8,128)(2,1)} %param.5) | copy-start | bytes 688132
  0.0 11.5 %copy-start.13 = (f32[896]{0:T(1024)S(1)}, f32[896]{0:T(1024)}, u32[]{:S(2)}) copy-start(f32[896]{0:T(1024)} %param.7) | copy-start | bytes 10756
  0.0 43.1 %copy-start.14 = (f32[960]{0:T(1024)S(1)}, f32[960]{0:T(1024)}, u32[]{:S(2)}) copy-start(f32[960]{0:T(1024)} %param.9) | copy-start | bytes 11524
  2.6 28.8 %copy-start.3 = (bf16[256,1920]{1,0:T(8,128)(2,1)}, bf16[256,1920]{1,0:T(8,128)(2,1)S(1)}, u32[]{:S(2)}) copy-start(bf16[256,1920]{1,0:T(8,128)(2,1)S(1)} %get-tuple-element.53) | copy-start | bytes 2949124
  2.6 25.0 %collective-permute-start.2 = (bf16[256,1920]{1,0:T(8,128)(2,1)S(1)}, bf16[256,1920]{1,0:T(8,128)(2,1)S(1)}, u32[]{:S(2)}, u32[]{:S(2)}) collective-permute-start(bf16[256,1920]{1,0:T(8,128)(2,1)S(1)} %get-tuple-element.53), channel_id=1, source_target_pairs={{32,0},{64,32},{96,64},{0,96},{33,1},{65,33},{97,65},{1,97},{34,2}... | collective-permute-start | bytes 2949128 | tf_op jit(solution)/shard_map/ppermute | solution.py:25
  7.2 23.6 %collective-permute-start.3 = (bf16[256,1920]{1,0:T(8,128)(2,1)S(1)}, bf16[256,1920]{1,0:T(8,128)(2,1)}, u32[]{:S(2)}, u32[]{:S(2)}) collective-permute-start(bf16[256,1920]{1,0:T(8,128)(2,1)S(1)} %get-tuple-element.53), channel_id=1, source_target_pairs={{96,0},{0,32},{32,64},{64,96},{97,1},{1,33},{33,65},{65,97},{98,2}... | collective-permute-start | bytes 2949128 | tf_op jit(solution)/shard_map/ppermute | solution.py:25
  7.2 24.1 %collective-permute-start = (bf16[256,1920]{1,0:T(8,128)(2,1)}, bf16[256,1920]{1,0:T(8,128)(2,1)}, u32[]{:S(2)}, u32[]{:S(2)}) collective-permute-start(bf16[256,1920]{1,0:T(8,128)(2,1)} %get-tuple-element.54), channel_id=1, source_target_pairs={{16,0},{0,16},{17,1},{1,17},{18,2},{2,18},{19,3},{3,19},{20,4},{4,... | collective-permute-start | bytes 2949128 | tf_op jit(solution)/shard_map/ppermute | solution.py:25
  10.2 2.3 %collective-permute-start.1 = (bf16[448,128]{1,0:T(8,128)(2,1)S(1)}, bf16[448,128]{1,0:T(8,128)(2,1)S(1)}, u32[]{:S(2)}, u32[]{:S(2)}) collective-permute-start(bf16[448,128]{1,0:T(8,128)(2,1)S(1)} %bitcast.19), channel_id=1, source_target_pairs={{1,0},{0,1},{3,2},{2,3},{5,4},{4,5},{7,6},{6,7},{9,8},{8,9},{11,10... | collective-permute-start | bytes 344072 | tf_op jit(solution)/shard_map/ppermute | solution.py:25
  25.5 36.7 %copy-start = (bf16[4,448,256]{2,1,0:T(8,128)(2,1)}, bf16[4,448,256]{2,1,0:T(8,128)(2,1)S(1)}, u32[]{:S(2)}) copy-start(bf16[4,448,256]{2,1,0:T(8,128)(2,1)S(1)} %all_gather.4.refs_0_) | copy-start | bytes 2752516
  31.4 10.9 %collective-permute-start.8 = (bf16[128,1920]{1,0:T(8,128)(2,1)S(1)}, bf16[128,1920]{1,0:T(8,128)(2,1)S(1)}, u32[]{:S(2)}, u32[]{:S(2)}) collective-permute-start(bf16[128,1920]{1,0:T(8,128)(2,1)S(1)} %slice.20), channel_id=1, source_target_pairs={{32,0},{64,32},{96,64},{0,96},{33,1},{65,33},{97,65},{1,97},{34,2}... | collective-permute-start | bytes 1474568 | tf_op jit(solution)/shard_map/ppermute | solution.py:25
  33.9 23.3 %collective-permute-start.10 = (bf16[4,448,256]{2,1,0:T(8,128)(2,1)S(1)}, bf16[4,448,256]{2,1,0:T(8,128)(2,1)S(1)}, u32[]{:S(2)}, u32[]{:S(2)}) collective-permute-start(bf16[4,448,256]{2,1,0:T(8,128)(2,1)S(1)} %all_gather.4.refs_0_), channel_id=1, source_target_pairs={{2,0},{16,2},{18,16},{0,18},{3,1},{17,3},{19,17},{1,19},{6,4},{20,... | collective-permute-start | bytes 2752520 | tf_op jit(solution)/shard_map/ppermute | solution.py:25
  36.6 20.6 %collective-permute-start.11 = (bf16[4,448,256]{2,1,0:T(8,128)(2,1)S(1)}, bf16[4,448,256]{2,1,0:T(8,128)(2,1)S(1)}, u32[]{:S(2)}, u32[]{:S(2)}) collective-permute-start(bf16[4,448,256]{2,1,0:T(8,128)(2,1)S(1)} %all_gather.4.refs_0_), channel_id=1, source_target_pairs={{18,0},{0,2},{2,16},{16,18},{19,1},{1,3},{3,17},{17,19},{22,4},{4,... | collective-permute-start | bytes 2752520 | tf_op jit(solution)/shard_map/ppermute | solution.py:25
  37.7 11.4 %collective-permute-start.9 = (bf16[128,1920]{1,0:T(8,128)(2,1)S(1)}, bf16[128,1920]{1,0:T(8,128)(2,1)}, u32[]{:S(2)}, u32[]{:S(2)}) collective-permute-start(bf16[128,1920]{1,0:T(8,128)(2,1)S(1)} %slice.21), channel_id=1, source_target_pairs={{96,0},{0,32},{32,64},{64,96},{97,1},{1,33},{33,65},{65,97},{98,2}... | collective-permute-start | bytes 1474568 | tf_op jit(solution)/shard_map/ppermute | solution.py:25
  37.7 29.3 %collective-permute-start.4 = (bf16[256,1920]{1,0:T(8,128)(2,1)}, bf16[256,1920]{1,0:T(8,128)(2,1)}, u32[]{:S(2)}, u32[]{:S(2)}) collective-permute-start(bf16[256,1920]{1,0:T(8,128)(2,1)} %collective-permute-done.refs_6_), channel_id=1, source_target_pairs={{32,0},{64,32},{96,64},{0,96},{33,1},{65,33},{97,65},{1,97},{34,2}... | collective-permute-start | bytes 2949128 | tf_op jit(solution)/shard_map/ppermute | solution.py:25
  43.1 27.0 %collective-permute-start.5 = (bf16[256,1920]{1,0:T(8,128)(2,1)}, bf16[256,1920]{1,0:T(8,128)(2,1)}, u32[]{:S(2)}, u32[]{:S(2)}) collective-permute-start(bf16[256,1920]{1,0:T(8,128)(2,1)} %collective-permute-done.refs_6_), channel_id=1, source_target_pairs={{96,0},{0,32},{32,64},{64,96},{97,1},{1,33},{33,65},{65,97},{98,2}... | collective-permute-start | bytes 2949128 | tf_op jit(solution)/shard_map/ppermute | solution.py:25
  49.0 24.4 %collective-permute-start.16 = (bf16[256,1920]{1,0:T(8,128)(2,1)}, bf16[256,1920]{1,0:T(8,128)(2,1)}, u32[]{:S(2)}, u32[]{:S(2)}) collective-permute-start(bf16[256,1920]{1,0:T(8,128)(2,1)} %collective-permute-done.refs_6_), channel_id=1, source_target_pairs={{1,0},{0,1},{3,2},{2,3},{5,4},{4,5},{7,6},{6,7},{9,8},{8,9},{11,10... | collective-permute-start | bytes 2949128 | tf_op jit(solution)/shard_map/ppermute | solution.py:25
  57.2 7.6 %copy-start.1 = (bf16[4,448,256]{2,1,0:T(8,128)(2,1)}, bf16[4,448,256]{2,1,0:T(8,128)(2,1)S(1)}, u32[]{:S(2)}) copy-start(bf16[4,448,256]{2,1,0:T(8,128)(2,1)S(1)} %collective-permute-done.10.refs_1_) | copy-start | bytes 2752516
  57.2 8.3 %copy-start.2 = (bf16[4,448,256]{2,1,0:T(8,128)(2,1)}, bf16[4,448,256]{2,1,0:T(8,128)(2,1)S(1)}, u32[]{:S(2)}) copy-start(bf16[4,448,256]{2,1,0:T(8,128)(2,1)S(1)} %collective-permute-done.11.refs_2_) | copy-start | bytes 2752516
  57.2 14.0 %collective-permute-start.14 = (f32[1,448]{1,0:T(1,128)S(1)}, f32[1,448]{1,0:T(1,128)S(1)}, u32[]{:S(2)}, u32[]{:S(2)}) collective-permute-start(f32[1,448]{1,0:T(1,128)S(1)} %reshape.114), channel_id=1, source_target_pairs={{16,0},{0,16},{17,1},{1,17},{18,2},{2,18},{19,3},{3,19},{20,4},{4,... | collective-permute-start | bytes 5384 | tf_op jit(solution)/shard_map/ppermute | solution.py:25
  62.2 3.4 %collective-permute-start.15 = (f32[4]{0:T(128)S(1)}, f32[4]{0:T(128)S(1)}, u32[]{:S(2)}, u32[]{:S(2)}) collective-permute-start(f32[4]{0:T(128)S(1)} %copy-done.15), channel_id=1, source_target_pairs={{1,0},{0,1},{3,2},{2,3},{5,4},{4,5},{7,6},{6,7},{9,8},{8,9},{11,10... | collective-permute-start | bytes 56 | tf_op jit(solution)/shard_map/ppermute | solution.py:25
  65.6 12.4 %collective-permute-start.12 = (bf16[2,448,256]{2,1,0:T(8,128)(2,1)}, bf16[2,448,256]{2,1,0:T(8,128)(2,1)S(1)}, u32[]{:S(2)}, u32[]{:S(2)}) collective-permute-start(bf16[2,448,256]{2,1,0:T(8,128)(2,1)} %slice.22), channel_id=1, source_target_pairs={{2,0},{16,2},{18,16},{0,18},{3,1},{17,3},{19,17},{1,19},{6,4},{20,... | collective-permute-start | bytes 1376264 | tf_op jit(solution)/shard_map/ppermute | solution.py:25
  67.1 13.1 %collective-permute-start.13 = (bf16[2,448,256]{2,1,0:T(8,128)(2,1)S(1)}, bf16[2,448,256]{2,1,0:T(8,128)(2,1)S(1)}, u32[]{:S(2)}, u32[]{:S(2)}) collective-permute-start(bf16[2,448,256]{2,1,0:T(8,128)(2,1)S(1)} %slice.23), channel_id=1, source_target_pairs={{18,0},{0,2},{2,16},{16,18},{19,1},{1,3},{3,17},{17,19},{22,4},{4,... | collective-permute-start | bytes 1376264 | tf_op jit(solution)/shard_map/ppermute | solution.py:25
  70.1 10.1 %collective-permute-start.6 = (bf16[128,1920]{1,0:T(8,128)(2,1)S(1)}, bf16[128,1920]{1,0:T(8,128)(2,1)S(1)}, u32[]{:S(2)}, u32[]{:S(2)}) collective-permute-start(bf16[128,1920]{1,0:T(8,128)(2,1)S(1)} %slice.24), channel_id=1, source_target_pairs={{32,0},{64,32},{96,64},{0,96},{33,1},{65,33},{97,65},{1,97},{34,2}... | collective-permute-start | bytes 1474568 | tf_op jit(solution)/shard_map/ppermute | solution.py:25
  71.2 10.4 %collective-permute-start.7 = (bf16[128,1920]{1,0:T(8,128)(2,1)S(1)}, bf16[128,1920]{1,0:T(8,128)(2,1)S(1)}, u32[]{:S(2)}, u32[]{:S(2)}) collective-permute-start(bf16[128,1920]{1,0:T(8,128)(2,1)S(1)} %slice.25), channel_id=1, source_target_pairs={{96,0},{0,32},{32,64},{64,96},{97,1},{1,33},{33,65},{65,97},{98,2}... | collective-permute-start | bytes 1474568 | tf_op jit(solution)/shard_map/ppermute | solution.py:25
  78.0 10.9 %copy-start.5 = (bf16[2,448,256]{2,1,0:T(8,128)(2,1)}, bf16[2,448,256]{2,1,0:T(8,128)(2,1)S(1)}, u32[]{:S(2)}) copy-start(bf16[2,448,256]{2,1,0:T(8,128)(2,1)S(1)} %collective-permute-done.12.refs_3_) | copy-start | bytes 1376260
  80.2 8.8 %copy-start.6 = (bf16[2,448,256]{2,1,0:T(8,128)(2,1)}, bf16[2,448,256]{2,1,0:T(8,128)(2,1)S(1)}, u32[]{:S(2)}) copy-start(bf16[2,448,256]{2,1,0:T(8,128)(2,1)S(1)} %collective-permute-done.13.refs_4_) | copy-start | bytes 1376260
  80.2 8.8 %copy-start.9 = (bf16[128,1920]{1,0:T(8,128)(2,1)}, bf16[128,1920]{1,0:T(8,128)(2,1)S(1)}, u32[]{:S(2)}) copy-start(bf16[128,1920]{1,0:T(8,128)(2,1)S(1)} %collective-permute-done.6.refs_9_) | copy-start | bytes 1474564
  82.3 21.7 %collective-permute-start.17 = (bf16[4,256,1920]{2,1,0:T(8,128)(2,1)}, bf16[4,256,1920]{2,1,0:T(8,128)(2,1)}, u32[]{:S(2)}, u32[]{:S(2)}) collective-permute-start(bf16[4,256,1920]{2,1,0:T(8,128)(2,1)} %pad_maximum_fusion.refs_5_), channel_id=1, source_target_pairs={{1,0},{0,1},{3,2},{2,3},{5,4},{4,5},{7,6},{6,7},{9,8},{8,9},{11,10... | collective-permute-start | bytes 11796488 | tf_op jit(solution)/shard_map/ppermute | solution.py:25
  86.9 17.1 %collective-permute-start.18 = (bf16[256,1920]{1,0:T(8,128)(2,1)}, bf16[256,1920]{1,0:T(8,128)(2,1)S(1)}, u32[]{:S(2)}, u32[]{:S(2)}) collective-permute-start(bf16[256,1920]{1,0:T(8,128)(2,1)} %collective-permute-done.4.refs_7_), channel_id=1, source_target_pairs={{1,0},{0,1},{3,2},{2,3},{5,4},{4,5},{7,6},{6,7},{9,8},{8,9},{11,10... | collective-permute-start | bytes 2949128 | tf_op jit(solution)/shard_map/ppermute | solution.py:25
  86.9 17.1 %collective-permute-start.19 = (bf16[256,1920]{1,0:T(8,128)(2,1)}, bf16[256,1920]{1,0:T(8,128)(2,1)S(1)}, u32[]{:S(2)}, u32[]{:S(2)}) collective-permute-start(bf16[256,1920]{1,0:T(8,128)(2,1)} %collective-permute-done.5.refs_8_), channel_id=1, source_target_pairs={{1,0},{0,1},{3,2},{2,3},{5,4},{4,5},{7,6},{6,7},{9,8},{8,9},{11,10... | collective-permute-start | bytes 2949128 | tf_op jit(solution)/shard_map/ppermute | solution.py:25
  87.4 16.6 %collective-permute-start.20 = (bf16[128,1920]{1,0:T(8,128)(2,1)S(1)}, bf16[128,1920]{1,0:T(8,128)(2,1)}, u32[]{:S(2)}, u32[]{:S(2)}) collective-permute-start(bf16[128,1920]{1,0:T(8,128)(2,1)S(1)} %collective-permute-done.6.refs_9_), channel_id=1, source_target_pairs={{1,0},{0,1},{3,2},{2,3},{5,4},{4,5},{7,6},{6,7},{9,8},{8,9},{11,10... | collective-permute-start | bytes 1474568 | tf_op jit(solution)/shard_map/ppermute | solution.py:25
  87.4 16.6 %collective-permute-start.21 = (bf16[128,1920]{1,0:T(8,128)(2,1)}, bf16[128,1920]{1,0:T(8,128)(2,1)}, u32[]{:S(2)}, u32[]{:S(2)}) collective-permute-start(bf16[128,1920]{1,0:T(8,128)(2,1)} %copy-done.10), channel_id=1, source_target_pairs={{1,0},{0,1},{3,2},{2,3},{5,4},{4,5},{7,6},{6,7},{9,8},{8,9},{11,10... | collective-permute-start | bytes 1474568 | tf_op jit(solution)/shard_map/ppermute | solution.py:25
  (6 other events, 13.5 us)

commit v6 on v5

--- a/solution.py
+++ b/solution.py
@@ -109,7 +109,7 @@
             pltpu.SemaphoreType.DMA((cuts, 2)),
         ],
         input_output_aliases={} if started is None else {len(operands) - 1: 0},
-        compiler_params=pltpu.CompilerParams(vmem_limit_bytes=60 << 20),
+        compiler_params=pltpu.CompilerParams(vmem_limit_bytes=48 << 20),
         cost_estimate=HINT,
         name="product",
     )(*operands)

time: 210 us -> 207 us (0.986)
  Pallas kernels: 33.1 us -> 28.2 us
  local copies, waits for them, and re-layouts: 11.5 us -> 15.3 us
    pallas_call x2, Pallas kernels: 30 us -> 25.1 us  [product(): pl.pallas_call(functools.partial(product_kernel, at_column), out_shape=ja...]
    slice x6, local copies, waits for them, and re-layouts: 4.06 us -> 7.76 us  [far(): return (shift(up[:cut], axis, 1, 4), shift(down[cut:], axis, 3, 4))]
  transfers between devices with their start and end apart: 22 -> 22, of which waited for: 10 -> 10; matrix products, arithmetic and copies ran while one was open for 5% -> 6% of each run, Pallas kernels for 7% -> 6%
where the time goes in v6:
time: 207 us; the launch traced here: 206 us
  blocking collectives  98.9 us (48%)
  starting transfers between devices  35.6 us (17%)
  Pallas kernels  28.2 us (14%)
  waiting for transfers between devices  23 us (11%)
  local copies, waits for them, and re-layouts  15.3 us (7%)
  other arithmetic  4.86 us (2%)
    all_to_all x1, blocking collectives, local(): lax.all_to_all(update.reshape(CHIPS, portion, -1), PLANE, 0, 0, tiled=True)  85.9 us
    ppermute x22, starting transfers between devices, shift(): lax.ppermute(value, axis, [((i + step) % size, i) for i in range(size)])  35.6 us
    pallas_call x2, Pallas kernels, product(): pl.pallas_call(functools.partial(product_kernel, at_column), out_shape=ja...  25.1 us
    ppermute x22, waiting for transfers between devices, shift(): lax.ppermute(value, axis, [((i + step) % size, i) for i in range(size)])  23 us
    all_gather x1, blocking collectives, local(): along = lax.all_gather(both, 'x', axis=0)  13 us
    slice x6, local copies, waits for them, and re-layouts, far(): return (shift(up[:cut], axis, 1, 4), shift(down[cut:], axis, 3, 4))  7.76 us
    another operation x2, other arithmetic, local(): here = jnp.stack([mine, up, down, jnp.concatenate(two)])  4.75 us
  transfers between devices with their start and end apart: 22, of which 10 were waited for; matrix products, arithmetic and copies ran while one was open for 6% of the time, Pallas kernels for 6%

profile of v6, /device:TPU:1, one launch (start us, length us, event | category | flops | bytes accessed | tf_op | source)
XLA Modules:
  0.0 206.2 jit_solution(11916452455443044890)
XLA Ops:
  0.0 2.6 %constant_dynamic-slice_fusion = (bf16[256,1920]{1,0:T(8,128)(2,1)S(1)}, bf16[256,1920]{1,0:T(8,128)(2,1)}) fusion(bf16[256,3840]{1,0:T(8,128)(2,1)} %param.6, s32[]{:T(128)S(6)} %select_n.58, s32[]{:T(128)S(6)} %select_n.53), kind=kLoop, calls=%fused_computation.7 | loop fusion | bytes 3932168 | tf_op jit(solution)/shard_map/dynamic_slice | solution.py:157
  2.6 4.6 %collective-permute-start.2 = (bf16[256,1920]{1,0:T(8,128)(2,1)S(1)}, bf16[256,1920]{1,0:T(8,128)(2,1)}, u32[]{:S(2)}, u32[]{:S(2)}) collective-permute-start(bf16[256,1920]{1,0:T(8,128)(2,1)S(1)} %get-tuple-element.53), channel_id=1, source_target_pairs={{32,0},{64,32},{96,64},{0,96},{33,1},{65,33},{97,65},{1,97},{34,2}... | collective-permute-start | bytes 2949128 | tf_op jit(solution)/shard_map/ppermute | solution.py:25
  7.2 2.9 %collective-permute-start = (bf16[256,1920]{1,0:T(8,128)(2,1)}, bf16[256,1920]{1,0:T(8,128)(2,1)S(1)}, u32[]{:S(2)}, u32[]{:S(2)}) collective-permute-start(bf16[256,1920]{1,0:T(8,128)(2,1)} %get-tuple-element.54), channel_id=1, source_target_pairs={{16,0},{0,16},{17,1},{1,17},{18,2},{2,18},{19,3},{3,19},{20,4},{4,... | collective-permute-start | bytes 2949128 | tf_op jit(solution)/shard_map/ppermute | solution.py:25
  10.2 1.3 collective-permute-start.1
  12.5 13.0 %all_gather.4.refs_0_ = bf16[4,448,256]{2,1,0:T(8,128)(2,1)S(1)} all-gather(bf16[1,448,256]{2,1,0:T(8,128)(2,1)S(1)} %maximum_select_fusion), channel_id=1, replica_groups=mesh['z'=4,'yh'=2,'x'=4,'yl'=2,'c'=2] {'x'}, dimensions={0}, use_global_device_ids=true | all-gather | bytes 1146880 | tf_op jit(solution)/shard_map/all_gather | solution.py:170
  25.5 2.2 %collective-permute-done.2 = bf16[256,1920]{1,0:T(8,128)(2,1)} collective-permute-done((bf16[256,1920]{1,0:T(8,128)(2,1)S(1)}, bf16[256,1920]{1,0:T(8,128)(2,1)}, u32[]{:S(2)}, u32[]{:S(2)}) %collective-permute-start.2) | collective-permute-done | bytes 983072 | tf_op jit(solution)/shard_map/ppermute | solution.py:25
  27.7 3.2 %collective-permute-done.3 = bf16[256,1920]{1,0:T(8,128)(2,1)} collective-permute-done((bf16[256,1920]{1,0:T(8,128)(2,1)S(1)}, bf16[256,1920]{1,0:T(8,128)(2,1)}, u32[]{:S(2)}, u32[]{:S(2)}) %collective-permute-start.3) | collective-permute-done | bytes 983072 | tf_op jit(solution)/shard_map/ppermute | solution.py:25
  31.3 1.4 slice.20
  32.7 2.4 %collective-permute-start.8 = (bf16[128,1920]{1,0:T(8,128)(2,1)S(1)}, bf16[128,1920]{1,0:T(8,128)(2,1)S(1)}, u32[]{:S(2)}, u32[]{:S(2)}) collective-permute-start(bf16[128,1920]{1,0:T(8,128)(2,1)S(1)} %slice.20), channel_id=1, source_target_pairs={{32,0},{64,32},{96,64},{0,96},{33,1},{65,33},{97,65},{1,97},{34,2}... | collective-permute-start | bytes 1474568 | tf_op jit(solution)/shard_map/ppermute | solution.py:25
  35.1 2.7 %collective-permute-start.10 = (bf16[4,448,256]{2,1,0:T(8,128)(2,1)S(1)}, bf16[4,448,256]{2,1,0:T(8,128)(2,1)S(1)}, u32[]{:S(2)}, u32[]{:S(2)}) collective-permute-start(bf16[4,448,256]{2,1,0:T(8,128)(2,1)S(1)} %all_gather.4.refs_0_), channel_id=1, source_target_pairs={{2,0},{16,2},{18,16},{0,18},{3,1},{17,3},{19,17},{1,19},{6,4},{20,... | collective-permute-start | bytes 2752520 | tf_op jit(solution)/shard_map/ppermute | solution.py:25
  37.9 1.1 slice.21
  39.0 2.7 %collective-permute-start.4 = (bf16[256,1920]{1,0:T(8,128)(2,1)}, bf16[256,1920]{1,0:T(8,128)(2,1)}, u32[]{:S(2)}, u32[]{:S(2)}) collective-permute-start(bf16[256,1920]{1,0:T(8,128)(2,1)} %copy-done.3), channel_id=1, source_target_pairs={{32,0},{64,32},{96,64},{0,96},{33,1},{65,33},{97,65},{1,97},{34,2}... | collective-permute-start | bytes 2949128 | tf_op jit(solution)/shard_map/ppermute | solution.py:25
  41.7 1.9 collective-permute-done.8
  44.5 5.8 %collective-permute-done.9 = bf16[128,1920]{1,0:T(8,128)(2,1)} collective-permute-done((bf16[128,1920]{1,0:T(8,128)(2,1)S(1)}, bf16[128,1920]{1,0:T(8,128)(2,1)}, u32[]{:S(2)}, u32[]{:S(2)}) %collective-permute-start.9) | collective-permute-done | bytes 491552 | tf_op jit(solution)/shard_map/ppermute | solution.py:25
  50.3 6.9 %collective-permute-start.16 = (bf16[256,1920]{1,0:T(8,128)(2,1)}, bf16[256,1920]{1,0:T(8,128)(2,1)}, u32[]{:S(2)}, u32[]{:S(2)}) collective-permute-start(bf16[256,1920]{1,0:T(8,128)(2,1)} %copy-done.3), channel_id=1, source_target_pairs={{1,0},{0,1},{3,2},{2,3},{5,4},{4,5},{7,6},{6,7},{9,8},{8,9},{11,10... | collective-permute-start | bytes 2949128 | tf_op jit(solution)/shard_map/ppermute | solution.py:25
  57.2 1.2 maximum_bitcast_fusion
  58.5 1.4 collective-permute-start.14
  59.9 3.5 %pad_maximum_fusion.refs_5_ = bf16[4,256,1920]{2,1,0:T(8,128)(2,1)} fusion(bf16[1,256,1920]{2,1,0:T(8,128)(2,1)S(1)} %maximum_bitcast_fusion, bf16[1,256,1920]{2,1,0:T(8,128)(2,1)} %bitcast.6, bf16[1,256,1920]{2,1,0:T(8,128)(2,1)} %bitcast.5, bf16[1,256,1920]{2,1,0:T(8,128)(2,1)} %bitcast.15), kind=kLoop, calls=%fused_computation | loop fusion | flops 5898240 | bytes 7864320 | tf_op jit(solution)/shard_map/stack | solution.py:176
  63.4 1.9 collective-permute-start.15
  67.2 1.5 collective-permute-start.12
  69.0 1.9 slice.24
  71.4 1.8 slice.25
  73.2 1.5 collective-permute-start.7
  74.8 4.9 %collective-permute-done.12.refs_3_ = bf16[2,448,256]{2,1,0:T(8,128)(2,1)S(1)} collective-permute-done((bf16[2,448,256]{2,1,0:T(8,128)(2,1)}, bf16[2,448,256]{2,1,0:T(8,128)(2,1)S(1)}, u32[]{:S(2)}, u32[]{:S(2)}) %collective-permute-start.12) | collective-permute-done | bytes 458784 | tf_op jit(solution)/shard_map/ppermute | solution.py:25
  80.4 1.9 collective-permute-done.13.refs_4_
  82.4 1.4 collective-permute-done.7.refs_10_
  83.8 4.6 %collective-permute-start.17 = (bf16[4,256,1920]{2,1,0:T(8,128)(2,1)}, bf16[4,256,1920]{2,1,0:T(8,128)(2,1)}, u32[]{:S(2)}, u32[]{:S(2)}) collective-permute-start(bf16[4,256,1920]{2,1,0:T(8,128)(2,1)} %pad_maximum_fusion.refs_5_), channel_id=1, source_target_pairs={{1,0},{0,1},{3,2},{2,3},{5,4},{4,5},{7,6},{6,7},{9,8},{8,9},{11,10... | collective-permute-start | bytes 11796488 | tf_op jit(solution)/shard_map/ppermute | solution.py:25
  90.6 1.2 copy-done.4
  91.8 11.4 %product.2.refs_13_ = bf16[896,3840]{1,0:T(8,128)(2,1)} custom-call(bf16[4,448,256]{2,1,0:T(8,128)(2,1)S(1)} %all_gather.4.refs_0_, bf16[4,448,256]{2,1,0:T(8,128)(2,1)S(1)} %collective-permute-done.10.refs_1_, bf16[4,448,256]{2,1,0:T(8,128)(2,1)S(1)} %collective-permute-done.11.refs_2_, bf16[2,448,256]{2,1,0:T(8,128)(2,1)S(1)} %copy-done.1, ...), custom_call_target="tpu_custom_call" | custom-call | flops 1000000 | bytes 65536 | tf_op jit(solution)/shard_map/product/pallas_call | solution.py:98
  103.3 13.7 %product.3 = bf16[896,3840]{1,0:T(8,128)(2,1)} custom-call(bf16[4,448,256]{2,1,0:T(8,128)(2,1)S(1)} %all_gather.4.refs_0_, bf16[4,448,256]{2,1,0:T(8,128)(2,1)S(1)} %collective-permute-done.10.refs_1_, bf16[4,448,256]{2,1,0:T(8,128)(2,1)S(1)} %collective-permute-done.11.refs_2_, bf16[2,448,256]{2,1,0:T(8,128)(2,1)S(1)} %copy-done.2, ...), custom_call_target="tpu_custom_call", output_to_operand_aliasing={{}: (13, {})} | custom-call | flops 1000000 | bytes 65536 | tf_op jit(solution)/shard_map/product/pallas_call | solution.py:98
  117.0 85.9 %all_to_all.5.piece = bf16[16,56,3840]{2,1,0:T(8,128)(2,1)S(1)} all-to-all(bf16[16,56,3840]{2,1,0:T(8,128)(2,1)} %bitcast.14), channel_id=1, replica_groups=mesh['z'=4,'yh'=2,'x'=4,'yl'=2,'c'=2] {'yh','x','yl'}, dimensions={0} | all-to-all | bytes 13762560 | tf_op jit(solution)/shard_map/all_to_all | solution.py:196
  202.9 3.1 %place.1 = bf16[56,61440]{1,0:T(8,128)(2,1)} custom-call(bf16[16,56,3840]{2,1,0:T(8,128)(2,1)S(1)} %all_to_all.5.piece), custom_call_target="tpu_custom_call" | custom-call | flops 1000000 | bytes 65536 | tf_op jit(solution)/shard_map/place/pallas_call | solution.py:135
  (65 shorter events, 8.3 us)
Async XLA Ops:
  0.0 10.2 %copy-start.7 = (bf16[896,128]{1,0:T(8,128)(2,1)S(1)}, bf16[896,128]{1,0:T(8,128)(2,1)}, u32[]{:S(2)}) copy-start(bf16[896,128]{1,0:T(8,128)(2,1)} %param.5) | copy-start | bytes 688132
  0.0 11.5 %copy-start.8 = (f32[896]{0:T(1024)S(1)}, f32[896]{0:T(1024)}, u32[]{:S(2)}) copy-start(f32[896]{0:T(1024)} %param.7) | copy-start | bytes 10756
  0.0 44.4 %copy-start.9 = (f32[960]{0:T(1024)S(1)}, f32[960]{0:T(1024)}, u32[]{:S(2)}) copy-start(f32[960]{0:T(1024)} %param.9) | copy-start | bytes 11524
  2.6 32.5 %copy-start.5 = (bf16[256,1920]{1,0:T(8,128)(2,1)}, bf16[256,1920]{1,0:T(8,128)(2,1)S(1)}, u32[]{:S(2)}) copy-start(bf16[256,1920]{1,0:T(8,128)(2,1)S(1)} %get-tuple-element.53) | copy-start | bytes 2949124
  2.6 25.0 %collective-permute-start.2 = (bf16[256,1920]{1,0:T(8,128)(2,1)S(1)}, bf16[256,1920]{1,0:T(8,128)(2,1)}, u32[]{:S(2)}, u32[]{:S(2)}) collective-permute-start(bf16[256,1920]{1,0:T(8,128)(2,1)S(1)} %get-tuple-element.53), channel_id=1, source_target_pairs={{32,0},{64,32},{96,64},{0,96},{33,1},{65,33},{97,65},{1,97},{34,2}... | collective-permute-start | bytes 2949128 | tf_op jit(solution)/shard_map/ppermute | solution.py:25
  7.2 23.6 %collective-permute-start.3 = (bf16[256,1920]{1,0:T(8,128)(2,1)S(1)}, bf16[256,1920]{1,0:T(8,128)(2,1)}, u32[]{:S(2)}, u32[]{:S(2)}) collective-permute-start(bf16[256,1920]{1,0:T(8,128)(2,1)S(1)} %get-tuple-element.53), channel_id=1, source_target_pairs={{96,0},{0,32},{32,64},{64,96},{97,1},{1,33},{33,65},{65,97},{98,2}... | collective-permute-start | bytes 2949128 | tf_op jit(solution)/shard_map/ppermute | solution.py:25
  7.2 24.0 %collective-permute-start = (bf16[256,1920]{1,0:T(8,128)(2,1)}, bf16[256,1920]{1,0:T(8,128)(2,1)S(1)}, u32[]{:S(2)}, u32[]{:S(2)}) collective-permute-start(bf16[256,1920]{1,0:T(8,128)(2,1)} %get-tuple-element.54), channel_id=1, source_target_pairs={{16,0},{0,16},{17,1},{1,17},{18,2},{2,18},{19,3},{3,19},{20,4},{4,... | collective-permute-start | bytes 2949128 | tf_op jit(solution)/shard_map/ppermute | solution.py:25
  10.2 2.3 %collective-permute-start.1 = (bf16[448,128]{1,0:T(8,128)(2,1)S(1)}, bf16[448,128]{1,0:T(8,128)(2,1)S(1)}, u32[]{:S(2)}, u32[]{:S(2)}) collective-permute-start(bf16[448,128]{1,0:T(8,128)(2,1)S(1)} %bitcast.18), channel_id=1, source_target_pairs={{1,0},{0,1},{3,2},{2,3},{5,4},{4,5},{7,6},{6,7},{9,8},{8,9},{11,10... | collective-permute-start | bytes 344072 | tf_op jit(solution)/shard_map/ppermute | solution.py:25
  31.3 1.4 copy-start.3
  32.7 10.9 %collective-permute-start.8 = (bf16[128,1920]{1,0:T(8,128)(2,1)S(1)}, bf16[128,1920]{1,0:T(8,128)(2,1)S(1)}, u32[]{:S(2)}, u32[]{:S(2)}) collective-permute-start(bf16[128,1920]{1,0:T(8,128)(2,1)S(1)} %slice.20), channel_id=1, source_target_pairs={{32,0},{64,32},{96,64},{0,96},{33,1},{65,33},{97,65},{1,97},{34,2}... | collective-permute-start | bytes 1474568 | tf_op jit(solution)/shard_map/ppermute | solution.py:25
  35.1 23.3 %collective-permute-start.10 = (bf16[4,448,256]{2,1,0:T(8,128)(2,1)S(1)}, bf16[4,448,256]{2,1,0:T(8,128)(2,1)S(1)}, u32[]{:S(2)}, u32[]{:S(2)}) collective-permute-start(bf16[4,448,256]{2,1,0:T(8,128)(2,1)S(1)} %all_gather.4.refs_0_), channel_id=1, source_target_pairs={{2,0},{16,2},{18,16},{0,18},{3,1},{17,3},{19,17},{1,19},{6,4},{20,... | collective-permute-start | bytes 2752520 | tf_op jit(solution)/shard_map/ppermute | solution.py:25
  37.9 20.6 %collective-permute-start.11 = (bf16[4,448,256]{2,1,0:T(8,128)(2,1)S(1)}, bf16[4,448,256]{2,1,0:T(8,128)(2,1)S(1)}, u32[]{:S(2)}, u32[]{:S(2)}) collective-permute-start(bf16[4,448,256]{2,1,0:T(8,128)(2,1)S(1)} %all_gather.4.refs_0_), channel_id=1, source_target_pairs={{18,0},{0,2},{2,16},{16,18},{19,1},{1,3},{3,17},{17,19},{22,4},{4,... | collective-permute-start | bytes 2752520 | tf_op jit(solution)/shard_map/ppermute | solution.py:25
  38.9 11.4 %collective-permute-start.9 = (bf16[128,1920]{1,0:T(8,128)(2,1)S(1)}, bf16[128,1920]{1,0:T(8,128)(2,1)}, u32[]{:S(2)}, u32[]{:S(2)}) collective-permute-start(bf16[128,1920]{1,0:T(8,128)(2,1)S(1)} %slice.21), channel_id=1, source_target_pairs={{96,0},{0,32},{32,64},{64,96},{97,1},{1,33},{33,65},{65,97},{98,2}... | collective-permute-start | bytes 1474568 | tf_op jit(solution)/shard_map/ppermute | solution.py:25
  39.0 29.9 %collective-permute-start.4 = (bf16[256,1920]{1,0:T(8,128)(2,1)}, bf16[256,1920]{1,0:T(8,128)(2,1)}, u32[]{:S(2)}, u32[]{:S(2)}) collective-permute-start(bf16[256,1920]{1,0:T(8,128)(2,1)} %copy-done.3), channel_id=1, source_target_pairs={{32,0},{64,32},{96,64},{0,96},{33,1},{65,33},{97,65},{1,97},{34,2}... | collective-permute-start | bytes 2949128 | tf_op jit(solution)/shard_map/ppermute | solution.py:25
  43.6 0.8 copy-start.6
  44.4 27.0 %collective-permute-start.5 = (bf16[256,1920]{1,0:T(8,128)(2,1)}, bf16[256,1920]{1,0:T(8,128)(2,1)}, u32[]{:S(2)}, u32[]{:S(2)}) collective-permute-start(bf16[256,1920]{1,0:T(8,128)(2,1)} %copy-done.3), channel_id=1, source_target_pairs={{96,0},{0,32},{32,64},{64,96},{97,1},{1,33},{33,65},{65,97},{98,2}... | collective-permute-start | bytes 2949128 | tf_op jit(solution)/shard_map/ppermute | solution.py:25
  50.3 24.5 %collective-permute-start.16 = (bf16[256,1920]{1,0:T(8,128)(2,1)}, bf16[256,1920]{1,0:T(8,128)(2,1)}, u32[]{:S(2)}, u32[]{:S(2)}) collective-permute-start(bf16[256,1920]{1,0:T(8,128)(2,1)} %copy-done.3), channel_id=1, source_target_pairs={{1,0},{0,1},{3,2},{2,3},{5,4},{4,5},{7,6},{6,7},{9,8},{8,9},{11,10... | collective-permute-start | bytes 2949128 | tf_op jit(solution)/shard_map/ppermute | solution.py:25
  58.5 14.7 %collective-permute-start.14 = (f32[1,448]{1,0:T(1,128)S(1)}, f32[1,448]{1,0:T(1,128)S(1)}, u32[]{:S(2)}, u32[]{:S(2)}) collective-permute-start(f32[1,448]{1,0:T(1,128)S(1)} %reshape.114), channel_id=1, source_target_pairs={{16,0},{0,16},{17,1},{1,17},{18,2},{2,18},{19,3},{3,19},{20,4},{4,... | collective-permute-start | bytes 5384 | tf_op jit(solution)/shard_map/ppermute | solution.py:25
  59.9 3.5 %copy-start.10 = (f32[4]{0:T(128)S(1)}, f32[4]{0:T(128)}, u32[]{:S(2)}) copy-start(f32[4]{0:T(128)} %param.8) | copy-start | bytes 52
  63.4 3.8 %collective-permute-start.15 = (f32[4]{0:T(128)S(1)}, f32[4]{0:T(128)S(1)}, u32[]{:S(2)}, u32[]{:S(2)}) collective-permute-start(f32[4]{0:T(128)S(1)} %copy-done.10), channel_id=1, source_target_pairs={{1,0},{0,1},{3,2},{2,3},{5,4},{4,5},{7,6},{6,7},{9,8},{8,9},{11,10... | collective-permute-start | bytes 56 | tf_op jit(solution)/shard_map/ppermute | solution.py:25
  67.2 12.5 %collective-permute-start.12 = (bf16[2,448,256]{2,1,0:T(8,128)(2,1)}, bf16[2,448,256]{2,1,0:T(8,128)(2,1)S(1)}, u32[]{:S(2)}, u32[]{:S(2)}) collective-permute-start(bf16[2,448,256]{2,1,0:T(8,128)(2,1)} %slice.22), channel_id=1, source_target_pairs={{2,0},{16,2},{18,16},{0,18},{3,1},{17,3},{19,17},{1,19},{6,4},{20,... | collective-permute-start | bytes 1376264 | tf_op jit(solution)/shard_map/ppermute | solution.py:25
  68.9 13.4 %collective-permute-start.13 = (bf16[2,448,256]{2,1,0:T(8,128)(2,1)}, bf16[2,448,256]{2,1,0:T(8,128)(2,1)}, u32[]{:S(2)}, u32[]{:S(2)}) collective-permute-start(bf16[2,448,256]{2,1,0:T(8,128)(2,1)} %slice.23), channel_id=1, source_target_pairs={{18,0},{0,2},{2,16},{16,18},{19,1},{1,3},{3,17},{17,19},{22,4},{4,... | collective-permute-start | bytes 1376264 | tf_op jit(solution)/shard_map/ppermute | solution.py:25
  71.4 11.0 %collective-permute-start.6 = (bf16[128,1920]{1,0:T(8,128)(2,1)}, bf16[128,1920]{1,0:T(8,128)(2,1)}, u32[]{:S(2)}, u32[]{:S(2)}) collective-permute-start(bf16[128,1920]{1,0:T(8,128)(2,1)} %slice.24), channel_id=1, source_target_pairs={{32,0},{64,32},{96,64},{0,96},{33,1},{65,33},{97,65},{1,97},{34,2}... | collective-permute-start | bytes 1474568 | tf_op jit(solution)/shard_map/ppermute | solution.py:25
  73.2 10.6 %collective-permute-start.7 = (bf16[128,1920]{1,0:T(8,128)(2,1)}, bf16[128,1920]{1,0:T(8,128)(2,1)}, u32[]{:S(2)}, u32[]{:S(2)}) collective-permute-start(bf16[128,1920]{1,0:T(8,128)(2,1)} %slice.25), channel_id=1, source_target_pairs={{96,0},{0,32},{32,64},{64,96},{97,1},{1,33},{33,65},{65,97},{98,2}... | collective-permute-start | bytes 1474568 | tf_op jit(solution)/shard_map/ppermute | solution.py:25
  83.8 19.5 %collective-permute-start.17 = (bf16[4,256,1920]{2,1,0:T(8,128)(2,1)}, bf16[4,256,1920]{2,1,0:T(8,128)(2,1)}, u32[]{:S(2)}, u32[]{:S(2)}) collective-permute-start(bf16[4,256,1920]{2,1,0:T(8,128)(2,1)} %pad_maximum_fusion.refs_5_), channel_id=1, source_target_pairs={{1,0},{0,1},{3,2},{2,3},{5,4},{4,5},{7,6},{6,7},{9,8},{8,9},{11,10... | collective-permute-start | bytes 11796488 | tf_op jit(solution)/shard_map/ppermute | solution.py:25
  88.4 14.9 %collective-permute-start.18 = (bf16[256,1920]{1,0:T(8,128)(2,1)}, bf16[256,1920]{1,0:T(8,128)(2,1)}, u32[]{:S(2)}, u32[]{:S(2)}) collective-permute-start(bf16[256,1920]{1,0:T(8,128)(2,1)} %collective-permute-done.4.refs_7_), channel_id=1, source_target_pairs={{1,0},{0,1},{3,2},{2,3},{5,4},{4,5},{7,6},{6,7},{9,8},{8,9},{11,10... | collective-permute-start | bytes 2949128 | tf_op jit(solution)/shard_map/ppermute | solution.py:25
  88.4 14.9 %collective-permute-start.19 = (bf16[256,1920]{1,0:T(8,128)(2,1)}, bf16[256,1920]{1,0:T(8,128)(2,1)}, u32[]{:S(2)}, u32[]{:S(2)}) collective-permute-start(bf16[256,1920]{1,0:T(8,128)(2,1)} %collective-permute-done.5.refs_8_), channel_id=1, source_target_pairs={{1,0},{0,1},{3,2},{2,3},{5,4},{4,5},{7,6},{6,7},{9,8},{8,9},{11,10... | collective-permute-start | bytes 2949128 | tf_op jit(solution)/shard_map/ppermute | solution.py:25
  88.9 14.4 %collective-permute-start.20 = (bf16[128,1920]{1,0:T(8,128)(2,1)}, bf16[128,1920]{1,0:T(8,128)(2,1)}, u32[]{:S(2)}, u32[]{:S(2)}) collective-permute-start(bf16[128,1920]{1,0:T(8,128)(2,1)} %collective-permute-done.6.refs_9_), channel_id=1, source_target_pairs={{1,0},{0,1},{3,2},{2,3},{5,4},{4,5},{7,6},{6,7},{9,8},{8,9},{11,10... | collective-permute-start | bytes 1474568 | tf_op jit(solution)/shard_map/ppermute | solution.py:25
  88.9 14.4 %collective-permute-start.21 = (bf16[128,1920]{1,0:T(8,128)(2,1)}, bf16[128,1920]{1,0:T(8,128)(2,1)}, u32[]{:S(2)}, u32[]{:S(2)}) collective-permute-start(bf16[128,1920]{1,0:T(8,128)(2,1)} %collective-permute-done.7.refs_10_), channel_id=1, source_target_pairs={{1,0},{0,1},{3,2},{2,3},{5,4},{4,5},{7,6},{6,7},{9,8},{8,9},{11,10... | collective-permute-start | bytes 1474568 | tf_op jit(solution)/shard_map/ppermute | solution.py:25
  89.6 1.0 copy-start.1
  90.6 1.2 copy-start.4
  91.8 11.5 %copy-start.2 = (bf16[2,448,256]{2,1,0:T(8,128)(2,1)S(1)}, bf16[2,448,256]{2,1,0:T(8,128)(2,1)}, u32[]{:S(2)}) copy-start(bf16[2,448,256]{2,1,0:T(8,128)(2,1)} %copy-done) | copy-start | bytes 1376260
  (1 other events, 0.8 us)

commit v7 on v6

--- a/solution.py
+++ b/solution.py
@@ -13,7 +13,7 @@
 CHIPS = 16
 PAIRS = 256
 DEPTH = 128
-CUTS = ((0, 256), (256, 640), (896, 1024))
+CUTS = ((0, 896), (896, 1024))
 STEPS = (0, 1, 3, 2)
 Y = ("yh", "yl")
 HBM = pl.BlockSpec(memory_space=pltpu.HBM)

time: 207 us -> 207 us (level)
  no operation moved by 1% of the time
where the time goes in v7:
time: 207 us; the launch traced here: 206 us
  blocking collectives  99 us (48%)
  starting transfers between devices  35.6 us (17%)
  Pallas kernels  28.1 us (14%)
  waiting for transfers between devices  23 us (11%)
  local copies, waits for them, and re-layouts  15.3 us (7%)
  other arithmetic  4.86 us (2%)
    all_to_all x1, blocking collectives, local(): lax.all_to_all(update.reshape(CHIPS, portion, -1), PLANE, 0, 0, tiled=True)  86 us
    ppermute x22, starting transfers between devices, shift(): lax.ppermute(value, axis, [((i + step) % size, i) for i in range(size)])  35.6 us
    pallas_call x2, Pallas kernels, product(): pl.pallas_call(functools.partial(product_kernel, at_column), out_shape=ja...  25 us
    ppermute x22, waiting for transfers between devices, shift(): lax.ppermute(value, axis, [((i + step) % size, i) for i in range(size)])  23 us
    all_gather x1, blocking collectives, local(): along = lax.all_gather(both, 'x', axis=0)  13 us
    slice x6, local copies, waits for them, and re-layouts, far(): return (shift(up[:cut], axis, 1, 4), shift(down[cut:], axis, 3, 4))  7.76 us
    another operation x2, other arithmetic, local(): here = jnp.stack([mine, up, down, jnp.concatenate(two)])  4.75 us
  transfers between devices with their start and end apart: 22, of which 10 were waited for; matrix products, arithmetic and copies ran while one was open for 6% of the time, Pallas kernels for 6%

profile of v7, /device:TPU:1, one launch (start us, length us, event | category | flops | bytes accessed | tf_op | source)
XLA Modules:
  0.0 206.2 jit_solution(7023526273011466715)
XLA Ops:
  0.0 2.6 %constant_dynamic-slice_fusion = (bf16[256,1920]{1,0:T(8,128)(2,1)S(1)}, bf16[256,1920]{1,0:T(8,128)(2,1)}) fusion(bf16[256,3840]{1,0:T(8,128)(2,1)} %param.6, s32[]{:T(128)S(6)} %select_n.58, s32[]{:T(128)S(6)} %select_n.53), kind=kLoop, calls=%fused_computation.7 | loop fusion | bytes 3932168 | tf_op jit(solution)/shard_map/dynamic_slice | solution.py:157
  2.6 4.6 %collective-permute-start.2 = (bf16[256,1920]{1,0:T(8,128)(2,1)S(1)}, bf16[256,1920]{1,0:T(8,128)(2,1)}, u32[]{:S(2)}, u32[]{:S(2)}) collective-permute-start(bf16[256,1920]{1,0:T(8,128)(2,1)S(1)} %get-tuple-element.53), channel_id=1, source_target_pairs={{32,0},{64,32},{96,64},{0,96},{33,1},{65,33},{97,65},{1,97},{34,2}... | collective-permute-start | bytes 2949128 | tf_op jit(solution)/shard_map/ppermute | solution.py:25
  7.2 2.9 %collective-permute-start = (bf16[256,1920]{1,0:T(8,128)(2,1)}, bf16[256,1920]{1,0:T(8,128)(2,1)S(1)}, u32[]{:S(2)}, u32[]{:S(2)}) collective-permute-start(bf16[256,1920]{1,0:T(8,128)(2,1)} %get-tuple-element.54), channel_id=1, source_target_pairs={{16,0},{0,16},{17,1},{1,17},{18,2},{2,18},{19,3},{3,19},{20,4},{4,... | collective-permute-start | bytes 2949128 | tf_op jit(solution)/shard_map/ppermute | solution.py:25
  10.2 1.3 collective-permute-start.1
  12.5 13.0 %all_gather.4.refs_0_ = bf16[4,448,256]{2,1,0:T(8,128)(2,1)S(1)} all-gather(bf16[1,448,256]{2,1,0:T(8,128)(2,1)S(1)} %maximum_select_fusion), channel_id=1, replica_groups=mesh['z'=4,'yh'=2,'x'=4,'yl'=2,'c'=2] {'x'}, dimensions={0}, use_global_device_ids=true | all-gather | bytes 1146880 | tf_op jit(solution)/shard_map/all_gather | solution.py:170
  25.5 2.2 %collective-permute-done.2 = bf16[256,1920]{1,0:T(8,128)(2,1)} collective-permute-done((bf16[256,1920]{1,0:T(8,128)(2,1)S(1)}, bf16[256,1920]{1,0:T(8,128)(2,1)}, u32[]{:S(2)}, u32[]{:S(2)}) %collective-permute-start.2) | collective-permute-done | bytes 983072 | tf_op jit(solution)/shard_map/ppermute | solution.py:25
  27.7 3.2 %collective-permute-done.3 = bf16[256,1920]{1,0:T(8,128)(2,1)} collective-permute-done((bf16[256,1920]{1,0:T(8,128)(2,1)S(1)}, bf16[256,1920]{1,0:T(8,128)(2,1)}, u32[]{:S(2)}, u32[]{:S(2)}) %collective-permute-start.3) | collective-permute-done | bytes 983072 | tf_op jit(solution)/shard_map/ppermute | solution.py:25
  31.3 1.4 slice.20
  32.7 2.4 %collective-permute-start.8 = (bf16[128,1920]{1,0:T(8,128)(2,1)S(1)}, bf16[128,1920]{1,0:T(8,128)(2,1)S(1)}, u32[]{:S(2)}, u32[]{:S(2)}) collective-permute-start(bf16[128,1920]{1,0:T(8,128)(2,1)S(1)} %slice.20), channel_id=1, source_target_pairs={{32,0},{64,32},{96,64},{0,96},{33,1},{65,33},{97,65},{1,97},{34,2}... | collective-permute-start | bytes 1474568 | tf_op jit(solution)/shard_map/ppermute | solution.py:25
  35.1 2.7 %collective-permute-start.10 = (bf16[4,448,256]{2,1,0:T(8,128)(2,1)S(1)}, bf16[4,448,256]{2,1,0:T(8,128)(2,1)S(1)}, u32[]{:S(2)}, u32[]{:S(2)}) collective-permute-start(bf16[4,448,256]{2,1,0:T(8,128)(2,1)S(1)} %all_gather.4.refs_0_), channel_id=1, source_target_pairs={{2,0},{16,2},{18,16},{0,18},{3,1},{17,3},{19,17},{1,19},{6,4},{20,... | collective-permute-start | bytes 2752520 | tf_op jit(solution)/shard_map/ppermute | solution.py:25
  37.9 1.1 slice.21
  39.0 2.7 %collective-permute-start.4 = (bf16[256,1920]{1,0:T(8,128)(2,1)}, bf16[256,1920]{1,0:T(8,128)(2,1)}, u32[]{:S(2)}, u32[]{:S(2)}) collective-permute-start(bf16[256,1920]{1,0:T(8,128)(2,1)} %copy-done.3), channel_id=1, source_target_pairs={{32,0},{64,32},{96,64},{0,96},{33,1},{65,33},{97,65},{1,97},{34,2}... | collective-permute-start | bytes 2949128 | tf_op jit(solution)/shard_map/ppermute | solution.py:25
  41.7 1.9 collective-permute-done.8
  44.5 5.8 %collective-permute-done.9 = bf16[128,1920]{1,0:T(8,128)(2,1)} collective-permute-done((bf16[128,1920]{1,0:T(8,128)(2,1)S(1)}, bf16[128,1920]{1,0:T(8,128)(2,1)}, u32[]{:S(2)}, u32[]{:S(2)}) %collective-permute-start.9) | collective-permute-done | bytes 491552 | tf_op jit(solution)/shard_map/ppermute | solution.py:25
  50.3 6.9 %collective-permute-start.16 = (bf16[256,1920]{1,0:T(8,128)(2,1)}, bf16[256,1920]{1,0:T(8,128)(2,1)}, u32[]{:S(2)}, u32[]{:S(2)}) collective-permute-start(bf16[256,1920]{1,0:T(8,128)(2,1)} %copy-done.3), channel_id=1, source_target_pairs={{1,0},{0,1},{3,2},{2,3},{5,4},{4,5},{7,6},{6,7},{9,8},{8,9},{11,10... | collective-permute-start | bytes 2949128 | tf_op jit(solution)/shard_map/ppermute | solution.py:25
  57.2 1.2 maximum_bitcast_fusion
  58.5 1.4 collective-permute-start.14
  59.9 3.5 %pad_maximum_fusion.refs_5_ = bf16[4,256,1920]{2,1,0:T(8,128)(2,1)} fusion(bf16[1,256,1920]{2,1,0:T(8,128)(2,1)S(1)} %maximum_bitcast_fusion, bf16[1,256,1920]{2,1,0:T(8,128)(2,1)} %bitcast.6, bf16[1,256,1920]{2,1,0:T(8,128)(2,1)} %bitcast.5, bf16[1,256,1920]{2,1,0:T(8,128)(2,1)} %bitcast.15), kind=kLoop, calls=%fused_computation | loop fusion | flops 5898240 | bytes 7864320 | tf_op jit(solution)/shard_map/stack | solution.py:176
  63.4 1.9 collective-permute-start.15
  67.2 1.5 collective-permute-start.12
  69.0 1.9 slice.24
  71.4 1.8 slice.25
  73.2 1.5 collective-permute-start.7
  74.8 4.9 %collective-permute-done.12.refs_3_ = bf16[2,448,256]{2,1,0:T(8,128)(2,1)S(1)} collective-permute-done((bf16[2,448,256]{2,1,0:T(8,128)(2,1)}, bf16[2,448,256]{2,1,0:T(8,128)(2,1)S(1)}, u32[]{:S(2)}, u32[]{:S(2)}) %collective-permute-start.12) | collective-permute-done | bytes 458784 | tf_op jit(solution)/shard_map/ppermute | solution.py:25
  80.4 1.9 collective-permute-done.13.refs_4_
  82.4 1.4 collective-permute-done.7.refs_10_
  83.8 4.6 %collective-permute-start.17 = (bf16[4,256,1920]{2,1,0:T(8,128)(2,1)}, bf16[4,256,1920]{2,1,0:T(8,128)(2,1)}, u32[]{:S(2)}, u32[]{:S(2)}) collective-permute-start(bf16[4,256,1920]{2,1,0:T(8,128)(2,1)} %pad_maximum_fusion.refs_5_), channel_id=1, source_target_pairs={{1,0},{0,1},{3,2},{2,3},{5,4},{4,5},{7,6},{6,7},{9,8},{8,9},{11,10... | collective-permute-start | bytes 11796488 | tf_op jit(solution)/shard_map/ppermute | solution.py:25
  90.6 1.2 copy-done.4
  91.8 11.7 %product.2.refs_13_ = bf16[896,3840]{1,0:T(8,128)(2,1)} custom-call(bf16[4,448,256]{2,1,0:T(8,128)(2,1)S(1)} %all_gather.4.refs_0_, bf16[4,448,256]{2,1,0:T(8,128)(2,1)S(1)} %collective-permute-done.10.refs_1_, bf16[4,448,256]{2,1,0:T(8,128)(2,1)S(1)} %collective-permute-done.11.refs_2_, bf16[2,448,256]{2,1,0:T(8,128)(2,1)S(1)} %copy-done.1, ...), custom_call_target="tpu_custom_call" | custom-call | flops 1000000 | bytes 65536 | tf_op jit(solution)/shard_map/product/pallas_call | solution.py:98
  103.6 13.3 %product.3 = bf16[896,3840]{1,0:T(8,128)(2,1)} custom-call(bf16[4,448,256]{2,1,0:T(8,128)(2,1)S(1)} %all_gather.4.refs_0_, bf16[4,448,256]{2,1,0:T(8,128)(2,1)S(1)} %collective-permute-done.10.refs_1_, bf16[4,448,256]{2,1,0:T(8,128)(2,1)S(1)} %collective-permute-done.11.refs_2_, bf16[2,448,256]{2,1,0:T(8,128)(2,1)S(1)} %copy-done.2, ...), custom_call_target="tpu_custom_call", output_to_operand_aliasing={{}: (13, {})} | custom-call | flops 1000000 | bytes 65536 | tf_op jit(solution)/shard_map/product/pallas_call | solution.py:98
  116.9 86.0 %all_to_all.5.piece = bf16[16,56,3840]{2,1,0:T(8,128)(2,1)S(1)} all-to-all(bf16[16,56,3840]{2,1,0:T(8,128)(2,1)} %bitcast.14), channel_id=1, replica_groups=mesh['z'=4,'yh'=2,'x'=4,'yl'=2,'c'=2] {'yh','x','yl'}, dimensions={0} | all-to-all | bytes 13762560 | tf_op jit(solution)/shard_map/all_to_all | solution.py:196
  202.9 3.1 %place.1 = bf16[56,61440]{1,0:T(8,128)(2,1)} custom-call(bf16[16,56,3840]{2,1,0:T(8,128)(2,1)S(1)} %all_to_all.5.piece), custom_call_target="tpu_custom_call" | custom-call | flops 1000000 | bytes 65536 | tf_op jit(solution)/shard_map/place/pallas_call | solution.py:135
  (65 shorter events, 8.3 us)
Async XLA Ops:
  0.0 10.2 %copy-start.7 = (bf16[896,128]{1,0:T(8,128)(2,1)S(1)}, bf16[896,128]{1,0:T(8,128)(2,1)}, u32[]{:S(2)}) copy-start(bf16[896,128]{1,0:T(8,128)(2,1)} %param.5) | copy-start | bytes 688132
  0.0 11.5 %copy-start.8 = (f32[896]{0:T(1024)S(1)}, f32[896]{0:T(1024)}, u32[]{:S(2)}) copy-start(f32[896]{0:T(1024)} %param.7) | copy-start | bytes 10756
  0.0 44.4 %copy-start.9 = (f32[960]{0:T(1024)S(1)}, f32[960]{0:T(1024)}, u32[]{:S(2)}) copy-start(f32[960]{0:T(1024)} %param.9) | copy-start | bytes 11524
  2.6 32.5 %copy-start.5 = (bf16[256,1920]{1,0:T(8,128)(2,1)}, bf16[256,1920]{1,0:T(8,128)(2,1)S(1)}, u32[]{:S(2)}) copy-start(bf16[256,1920]{1,0:T(8,128)(2,1)S(1)} %get-tuple-element.53) | copy-start | bytes 2949124
  2.6 25.0 %collective-permute-start.2 = (bf16[256,1920]{1,0:T(8,128)(2,1)S(1)}, bf16[256,1920]{1,0:T(8,128)(2,1)}, u32[]{:S(2)}, u32[]{:S(2)}) collective-permute-start(bf16[256,1920]{1,0:T(8,128)(2,1)S(1)} %get-tuple-element.53), channel_id=1, source_target_pairs={{32,0},{64,32},{96,64},{0,96},{33,1},{65,33},{97,65},{1,97},{34,2}... | collective-permute-start | bytes 2949128 | tf_op jit(solution)/shard_map/ppermute | solution.py:25
  7.2 23.6 %collective-permute-start.3 = (bf16[256,1920]{1,0:T(8,128)(2,1)S(1)}, bf16[256,1920]{1,0:T(8,128)(2,1)}, u32[]{:S(2)}, u32[]{:S(2)}) collective-permute-start(bf16[256,1920]{1,0:T(8,128)(2,1)S(1)} %get-tuple-element.53), channel_id=1, source_target_pairs={{96,0},{0,32},{32,64},{64,96},{97,1},{1,33},{33,65},{65,97},{98,2}... | collective-permute-start | bytes 2949128 | tf_op jit(solution)/shard_map/ppermute | solution.py:25
  7.2 24.0 %collective-permute-start = (bf16[256,1920]{1,0:T(8,128)(2,1)}, bf16[256,1920]{1,0:T(8,128)(2,1)S(1)}, u32[]{:S(2)}, u32[]{:S(2)}) collective-permute-start(bf16[256,1920]{1,0:T(8,128)(2,1)} %get-tuple-element.54), channel_id=1, source_target_pairs={{16,0},{0,16},{17,1},{1,17},{18,2},{2,18},{19,3},{3,19},{20,4},{4,... | collective-permute-start | bytes 2949128 | tf_op jit(solution)/shard_map/ppermute | solution.py:25
  10.2 2.3 %collective-permute-start.1 = (bf16[448,128]{1,0:T(8,128)(2,1)S(1)}, bf16[448,128]{1,0:T(8,128)(2,1)S(1)}, u32[]{:S(2)}, u32[]{:S(2)}) collective-permute-start(bf16[448,128]{1,0:T(8,128)(2,1)S(1)} %bitcast.18), channel_id=1, source_target_pairs={{1,0},{0,1},{3,2},{2,3},{5,4},{4,5},{7,6},{6,7},{9,8},{8,9},{11,10... | collective-permute-start | bytes 344072 | tf_op jit(solution)/shard_map/ppermute | solution.py:25
  31.3 1.4 copy-start.3
  32.7 10.9 %collective-permute-start.8 = (bf16[128,1920]{1,0:T(8,128)(2,1)S(1)}, bf16[128,1920]{1,0:T(8,128)(2,1)S(1)}, u32[]{:S(2)}, u32[]{:S(2)}) collective-permute-start(bf16[128,1920]{1,0:T(8,128)(2,1)S(1)} %slice.20), channel_id=1, source_target_pairs={{32,0},{64,32},{96,64},{0,96},{33,1},{65,33},{97,65},{1,97},{34,2}... | collective-permute-start | bytes 1474568 | tf_op jit(solution)/shard_map/ppermute | solution.py:25
  35.1 23.3 %collective-permute-start.10 = (bf16[4,448,256]{2,1,0:T(8,128)(2,1)S(1)}, bf16[4,448,256]{2,1,0:T(8,128)(2,1)S(1)}, u32[]{:S(2)}, u32[]{:S(2)}) collective-permute-start(bf16[4,448,256]{2,1,0:T(8,128)(2,1)S(1)} %all_gather.4.refs_0_), channel_id=1, source_target_pairs={{2,0},{16,2},{18,16},{0,18},{3,1},{17,3},{19,17},{1,19},{6,4},{20,... | collective-permute-start | bytes 2752520 | tf_op jit(solution)/shard_map/ppermute | solution.py:25
  37.9 20.6 %collective-permute-start.11 = (bf16[4,448,256]{2,1,0:T(8,128)(2,1)S(1)}, bf16[4,448,256]{2,1,0:T(8,128)(2,1)S(1)}, u32[]{:S(2)}, u32[]{:S(2)}) collective-permute-start(bf16[4,448,256]{2,1,0:T(8,128)(2,1)S(1)} %all_gather.4.refs_0_), channel_id=1, source_target_pairs={{18,0},{0,2},{2,16},{16,18},{19,1},{1,3},{3,17},{17,19},{22,4},{4,... | collective-permute-start | bytes 2752520 | tf_op jit(solution)/shard_map/ppermute | solution.py:25
  38.9 11.4 %collective-permute-start.9 = (bf16[128,1920]{1,0:T(8,128)(2,1)S(1)}, bf16[128,1920]{1,0:T(8,128)(2,1)}, u32[]{:S(2)}, u32[]{:S(2)}) collective-permute-start(bf16[128,1920]{1,0:T(8,128)(2,1)S(1)} %slice.21), channel_id=1, source_target_pairs={{96,0},{0,32},{32,64},{64,96},{97,1},{1,33},{33,65},{65,97},{98,2}... | collective-permute-start | bytes 1474568 | tf_op jit(solution)/shard_map/ppermute | solution.py:25
  39.0 29.9 %collective-permute-start.4 = (bf16[256,1920]{1,0:T(8,128)(2,1)}, bf16[256,1920]{1,0:T(8,128)(2,1)}, u32[]{:S(2)}, u32[]{:S(2)}) collective-permute-start(bf16[256,1920]{1,0:T(8,128)(2,1)} %copy-done.3), channel_id=1, source_target_pairs={{32,0},{64,32},{96,64},{0,96},{33,1},{65,33},{97,65},{1,97},{34,2}... | collective-permute-start | bytes 2949128 | tf_op jit(solution)/shard_map/ppermute | solution.py:25
  43.6 0.8 copy-start.6
  44.4 27.0 %collective-permute-start.5 = (bf16[256,1920]{1,0:T(8,128)(2,1)}, bf16[256,1920]{1,0:T(8,128)(2,1)}, u32[]{:S(2)}, u32[]{:S(2)}) collective-permute-start(bf16[256,1920]{1,0:T(8,128)(2,1)} %copy-done.3), channel_id=1, source_target_pairs={{96,0},{0,32},{32,64},{64,96},{97,1},{1,33},{33,65},{65,97},{98,2}... | collective-permute-start | bytes 2949128 | tf_op jit(solution)/shard_map/ppermute | solution.py:25
  50.3 24.5 %collective-permute-start.16 = (bf16[256,1920]{1,0:T(8,128)(2,1)}, bf16[256,1920]{1,0:T(8,128)(2,1)}, u32[]{:S(2)}, u32[]{:S(2)}) collective-permute-start(bf16[256,1920]{1,0:T(8,128)(2,1)} %copy-done.3), channel_id=1, source_target_pairs={{1,0},{0,1},{3,2},{2,3},{5,4},{4,5},{7,6},{6,7},{9,8},{8,9},{11,10... | collective-permute-start | bytes 2949128 | tf_op jit(solution)/shard_map/ppermute | solution.py:25
  58.5 14.7 %collective-permute-start.14 = (f32[1,448]{1,0:T(1,128)S(1)}, f32[1,448]{1,0:T(1,128)S(1)}, u32[]{:S(2)}, u32[]{:S(2)}) collective-permute-start(f32[1,448]{1,0:T(1,128)S(1)} %reshape.114), channel_id=1, source_target_pairs={{16,0},{0,16},{17,1},{1,17},{18,2},{2,18},{19,3},{3,19},{20,4},{4,... | collective-permute-start | bytes 5384 | tf_op jit(solution)/shard_map/ppermute | solution.py:25
  59.9 3.5 %copy-start.10 = (f32[4]{0:T(128)S(1)}, f32[4]{0:T(128)}, u32[]{:S(2)}) copy-start(f32[4]{0:T(128)} %param.8) | copy-start | bytes 52
  63.4 3.8 %collective-permute-start.15 = (f32[4]{0:T(128)S(1)}, f32[4]{0:T(128)S(1)}, u32[]{:S(2)}, u32[]{:S(2)}) collective-permute-start(f32[4]{0:T(128)S(1)} %copy-done.10), channel_id=1, source_target_pairs={{1,0},{0,1},{3,2},{2,3},{5,4},{4,5},{7,6},{6,7},{9,8},{8,9},{11,10... | collective-permute-start | bytes 56 | tf_op jit(solution)/shard_map/ppermute | solution.py:25
  67.2 12.5 %collective-permute-start.12 = (bf16[2,448,256]{2,1,0:T(8,128)(2,1)}, bf16[2,448,256]{2,1,0:T(8,128)(2,1)S(1)}, u32[]{:S(2)}, u32[]{:S(2)}) collective-permute-start(bf16[2,448,256]{2,1,0:T(8,128)(2,1)} %slice.22), channel_id=1, source_target_pairs={{2,0},{16,2},{18,16},{0,18},{3,1},{17,3},{19,17},{1,19},{6,4},{20,... | collective-permute-start | bytes 1376264 | tf_op jit(solution)/shard_map/ppermute | solution.py:25
  68.9 13.4 %collective-permute-start.13 = (bf16[2,448,256]{2,1,0:T(8,128)(2,1)}, bf16[2,448,256]{2,1,0:T(8,128)(2,1)}, u32[]{:S(2)}, u32[]{:S(2)}) collective-permute-start(bf16[2,448,256]{2,1,0:T(8,128)(2,1)} %slice.23), channel_id=1, source_target_pairs={{18,0},{0,2},{2,16},{16,18},{19,1},{1,3},{3,17},{17,19},{22,4},{4,... | collective-permute-start | bytes 1376264 | tf_op jit(solution)/shard_map/ppermute | solution.py:25
  71.4 11.0 %collective-permute-start.6 = (bf16[128,1920]{1,0:T(8,128)(2,1)}, bf16[128,1920]{1,0:T(8,128)(2,1)}, u32[]{:S(2)}, u32[]{:S(2)}) collective-permute-start(bf16[128,1920]{1,0:T(8,128)(2,1)} %slice.24), channel_id=1, source_target_pairs={{32,0},{64,32},{96,64},{0,96},{33,1},{65,33},{97,65},{1,97},{34,2}... | collective-permute-start | bytes 1474568 | tf_op jit(solution)/shard_map/ppermute | solution.py:25
  73.2 10.6 %collective-permute-start.7 = (bf16[128,1920]{1,0:T(8,128)(2,1)}, bf16[128,1920]{1,0:T(8,128)(2,1)}, u32[]{:S(2)}, u32[]{:S(2)}) collective-permute-start(bf16[128,1920]{1,0:T(8,128)(2,1)} %slice.25), channel_id=1, source_target_pairs={{96,0},{0,32},{32,64},{64,96},{97,1},{1,33},{33,65},{65,97},{98,2}... | collective-permute-start | bytes 1474568 | tf_op jit(solution)/shard_map/ppermute | solution.py:25
  83.8 19.8 %collective-permute-start.17 = (bf16[4,256,1920]{2,1,0:T(8,128)(2,1)}, bf16[4,256,1920]{2,1,0:T(8,128)(2,1)}, u32[]{:S(2)}, u32[]{:S(2)}) collective-permute-start(bf16[4,256,1920]{2,1,0:T(8,128)(2,1)} %pad_maximum_fusion.refs_5_), channel_id=1, source_target_pairs={{1,0},{0,1},{3,2},{2,3},{5,4},{4,5},{7,6},{6,7},{9,8},{8,9},{11,10... | collective-permute-start | bytes 11796488 | tf_op jit(solution)/shard_map/ppermute | solution.py:25
  88.4 15.2 %collective-permute-start.18 = (bf16[256,1920]{1,0:T(8,128)(2,1)}, bf16[256,1920]{1,0:T(8,128)(2,1)}, u32[]{:S(2)}, u32[]{:S(2)}) collective-permute-start(bf16[256,1920]{1,0:T(8,128)(2,1)} %collective-permute-done.4.refs_7_), channel_id=1, source_target_pairs={{1,0},{0,1},{3,2},{2,3},{5,4},{4,5},{7,6},{6,7},{9,8},{8,9},{11,10... | collective-permute-start | bytes 2949128 | tf_op jit(solution)/shard_map/ppermute | solution.py:25
  88.4 15.2 %collective-permute-start.19 = (bf16[256,1920]{1,0:T(8,128)(2,1)}, bf16[256,1920]{1,0:T(8,128)(2,1)}, u32[]{:S(2)}, u32[]{:S(2)}) collective-permute-start(bf16[256,1920]{1,0:T(8,128)(2,1)} %collective-permute-done.5.refs_8_), channel_id=1, source_target_pairs={{1,0},{0,1},{3,2},{2,3},{5,4},{4,5},{7,6},{6,7},{9,8},{8,9},{11,10... | collective-permute-start | bytes 2949128 | tf_op jit(solution)/shard_map/ppermute | solution.py:25
  88.9 14.7 %collective-permute-start.20 = (bf16[128,1920]{1,0:T(8,128)(2,1)}, bf16[128,1920]{1,0:T(8,128)(2,1)}, u32[]{:S(2)}, u32[]{:S(2)}) collective-permute-start(bf16[128,1920]{1,0:T(8,128)(2,1)} %collective-permute-done.6.refs_9_), channel_id=1, source_target_pairs={{1,0},{0,1},{3,2},{2,3},{5,4},{4,5},{7,6},{6,7},{9,8},{8,9},{11,10... | collective-permute-start | bytes 1474568 | tf_op jit(solution)/shard_map/ppermute | solution.py:25
  88.9 14.7 %collective-permute-start.21 = (bf16[128,1920]{1,0:T(8,128)(2,1)}, bf16[128,1920]{1,0:T(8,128)(2,1)}, u32[]{:S(2)}, u32[]{:S(2)}) collective-permute-start(bf16[128,1920]{1,0:T(8,128)(2,1)} %collective-permute-done.7.refs_10_), channel_id=1, source_target_pairs={{1,0},{0,1},{3,2},{2,3},{5,4},{4,5},{7,6},{6,7},{9,8},{8,9},{11,10... | collective-permute-start | bytes 1474568 | tf_op jit(solution)/shard_map/ppermute | solution.py:25
  89.6 1.0 copy-start.1
  90.6 1.2 copy-start.4
  91.8 11.8 %copy-start.2 = (bf16[2,448,256]{2,1,0:T(8,128)(2,1)S(1)}, bf16[2,448,256]{2,1,0:T(8,128)(2,1)}, u32[]{:S(2)}) copy-start(bf16[2,448,256]{2,1,0:T(8,128)(2,1)} %copy-done) | copy-start | bytes 1376260
  (1 other events, 0.8 us)
